TPU v7x, 32 devices: a whole 2x2x4 slice. The times are simulated.
32 devices in a mesh: wide: 16 (over z, y, x), narrow: 2 (over core).
Axes of the slice: x: 2, y: 2, z: 4, core: 2. Of those that a mesh axis runs over, the one named last changes fastest.
Arguments:
- chi_in: float32 [2560, 128], P('wide', 'narrow'), may hold values from -6 to 6
- val_orb: float32 [2560, 4096], P(('wide', 'narrow')), may hold values from -4 to 4
- cond_orb: float32 [2560, 4096], P(('wide', 'narrow')), may hold values from -4 to 4
- e_val: float32 [4096], replicated, may hold values from -12 to -0.5
- e_cond: float32 [4096], replicated, may hold values from 0.5 to 12
- pair_val: int32 [1, 512], replicated, may hold values from 0 to 4095
- pair_cond: int32 [1, 512], replicated, may hold values from 0 to 4095
Outputs:
- chi_out: float32 [2560, 128], P('wide', 'narrow')
All inputs are finite; a program needn't handle non-finite values.
Results may differ from a plain program's by a relative error of at most 0.0001.
Values sent between devices are 32-bit elements; how exact they have to be, the bound alone decides.
No kernel may reach another device: no remote copies, remote signals or barrier semaphores. Data moves between devices by JAX's collectives and lax.ppermute only.
A program may use at most 64 MiB of HBM per device.

v0:
```python
import jax
import jax.numpy as jnp
from jax import lax
from jax.sharding import PartitionSpec as P

SLAB_DEV = 8


def shards(chi_in, val_orb, cond_orb, e_val, e_cond, pair_val, pair_cond):
    narrow_pos = lax.axis_index("narrow")
    row_sub = SLAB_DEV // lax.axis_size("narrow")
    weight = 1.0 / (e_cond[pair_cond] - e_val[pair_val])
    dens_local = val_orb[:, pair_val] * cond_orb[:, pair_cond]
    columns = lax.all_gather(dens_local, "narrow", axis=0, tiled=True)
    weighted = columns * weight[None, :, :]
    pieces = lax.dynamic_slice_in_dim(columns, narrow_pos * row_sub, row_sub, 0)
    block_cols = weighted[:, 0, :]
    return chi_in + jnp.dot(
        block_cols,
        lax.all_gather(pieces[:, 0, :], "wide", axis=0, tiled=True).T,
        precision=lax.Precision.HIGHEST,
        preferred_element_type=jnp.float32,
    )


def solution(mesh):
    placed = (
        P("wide", "narrow"),
        P(("wide", "narrow"), None),
        P(("wide", "narrow"), None),
        P(),
        P(),
        P(),
        P(),
    )
    return jax.shard_map(
        shards, mesh=mesh, in_specs=placed, out_specs=P("wide", "narrow"), check_vma=False
    )
```

profile of v0, /device:TPU:0, one launch (start us, length us, event | category | flops | bytes accessed | tf_op | source)
XLA Modules:
  0.0 58.8 jit_solution(16796149356083120705)
XLA Ops:
  0.0 0.0 copy-start
  0.0 0.0 copy-start.5
  0.0 0.0 copy-start.1
  0.0 0.7 %compare_select_fusion.1 = s32[1,512]{1,0:T(1,128)S(1)} fusion(s32[1,512]{1,0:T(1,128)} %param.12), kind=kLoop, calls=%fused_computation.10 | loop fusion | flops 1536 | bytes 4096 | tf_op jit(solution)/shard_map/select_n | solution.py:13
  0.7 0.0 copy-done
  0.7 0.0 copy-start.2
  0.8 3.1 %gather_fusion.3 = f32[512]{0:T(512)S(1)} fusion(f32[4096]{0:T(1024)S(1)} %copy-done, s32[1024]{0:T(1024)S(1)} %pad_clamp_fusion.1), kind=kCustom, calls=%fused_computation.3 | custom fusion | bytes 6144 | tf_op jit(solution)/shard_map/gather | solution.py:12
  3.9 0.0 copy-done.5
  3.9 0.0 copy-done.1
  4.0 3.1 %gather_fusion.2 = f32[512]{0:T(512)S(1)} fusion(f32[4096]{0:T(1024)S(1)} %copy-done.1, s32[1024]{0:T(1024)S(1)} %pad_clamp_fusion), kind=kCustom, calls=%fused_computation.2 | custom fusion | bytes 6144 | tf_op jit(solution)/shard_map/gather | solution.py:12
  7.1 0.0 copy-done.2
  7.1 0.8 %copy.15 = f32[80,4096]{0,1:T(8,128)S(1)} copy(f32[80,4096]{1,0:T(8,128)S(1)} %copy-done.2) | data formatting | bytes 2621440 | tf_op args[1]
  7.9 0.0 copy-start.3
  8.0 1.6 %gather_fusion = f32[512,80]{1,0:T(8,128)} fusion(f32[80,4096]{0,1:T(8,128)S(1)} %copy.15, s32[1024]{0:T(1024)S(1)} %pad_clamp_fusion.1), kind=kCustom, calls=%fused_computation | custom fusion | bytes 329728 | tf_op jit(solution)/shard_map/gather | solution.py:13
  9.6 0.0 copy-done.3
  9.6 0.8 %copy.16 = f32[80,4096]{0,1:T(8,128)S(1)} copy(f32[80,4096]{1,0:T(8,128)S(1)} %copy-done.3) | data formatting | bytes 2621440 | tf_op args[2]
  10.4 0.0 copy-start.4
  10.4 1.0 %gather_fusion.1 = f32[512,80]{1,0:T(8,128)S(1)} fusion(f32[80,4096]{0,1:T(8,128)S(1)} %copy.16, s32[1024]{0:T(1024)S(1)} %pad_clamp_fusion), kind=kCustom, calls=%fused_computation.1 | custom fusion | bytes 329728 | tf_op jit(solution)/shard_map/gather | solution.py:13
  11.5 1.0 %multiply_bitcast_fusion = f32[80,512]{0,1:T(8,128)S(1)} fusion(f32[512,80]{1,0:T(8,128)} %gather_fusion, f32[512,80]{1,0:T(8,128)S(1)} %gather_fusion.1), kind=kLoop, calls=%fused_computation.7 | loop fusion | flops 40960 | bytes 491520 | tf_op jit(solution)/shard_map/mul | solution.py:13
  12.4 0.1 copy.17
  12.6 2.1 %all-gather.1 = f32[160,512]{1,0:T(8,128)S(1)} all-gather(f32[80,512]{1,0:T(8,128)S(1)} %copy.17), channel_id=3, replica_groups=mesh['wide'=16,'narrow'=2] {'narrow'}, dimensions={0}, use_global_device_ids=true | all-gather | bytes 491520 | tf_op jit(solution)/shard_map/all_gather | solution.py:14
  14.7 43.0 %all-gather.3 = f32[16,4,512]{2,1,0:T(4,128)S(1)} all-gather(f32[1,4,512]{2,1,0:T(4,128)S(1)} %dynamic-slice_bitcast_fusion), channel_id=4, replica_groups=mesh['wide'=16,'narrow'=2] {'wide'}, dimensions={0}, use_global_device_ids=true | all-gather | bytes 139264 | tf_op jit(solution)/shard_map/all_gather | solution.py:20
  57.7 0.0 copy-done.4
  57.7 1.1 %convolution_add_fusion = f32[160,64]{0,1:T(8,128)} fusion(f32[160,64]{0,1:T(8,128)S(1)} %copy-done.4, f32[64,512]{1,0:T(8,128)S(1)} %reshape.78, f32[160,512]{1,0:T(8,128)S(1)} %all-gather.1, f32[512]{0:T(512)S(1)} %subtract_divide_fusion), kind=kOutput, calls=%fused_computation.4 | convolution fusion | flops 63006720 | bytes 542720 | tf_op jit(solution)/shard_map/dot_general | solution.py:18
  (6 shorter events, 0.1 us)
Async XLA Ops:
  0.0 0.7 %copy-start = (f32[4096]{0:T(1024)S(1)}, f32[4096]{0:T(1024)}, u32[]{:S(2)}) copy-start(f32[4096]{0:T(1024)} %param.10) | copy-start | bytes 49156
  0.0 3.9 %copy-start.5 = (s32[1,512]{1,0:T(1,128)S(1)}, s32[1,512]{1,0:T(1,128)}, u32[]{:S(2)}) copy-start(s32[1,512]{1,0:T(1,128)} %param.13) | copy-start | bytes 6148
  0.0 3.9 %copy-start.1 = (f32[4096]{0:T(1024)S(1)}, f32[4096]{0:T(1024)}, u32[]{:S(2)}) copy-start(f32[4096]{0:T(1024)} %param.11) | copy-start | bytes 49156
  0.7 6.4 %copy-start.2 = (f32[80,4096]{1,0:T(8,128)S(1)}, f32[80,4096]{1,0:T(8,128)}, u32[]{:S(2)}) copy-start(f32[80,4096]{1,0:T(8,128)} %param.8) | copy-start | bytes 3932164
  7.9 1.7 %copy-start.3 = (f32[80,4096]{1,0:T(8,128)S(1)}, f32[80,4096]{1,0:T(8,128)}, u32[]{:S(2)}) copy-start(f32[80,4096]{1,0:T(8,128)} %param.9) | copy-start | bytes 3932164
  10.4 47.3 %copy-start.4 = (f32[160,64]{0,1:T(8,128)S(1)}, f32[160,64]{0,1:T(8,128)}, u32[]{:S(2)}) copy-start(f32[160,64]{0,1:T(8,128)} %param.7) | copy-start | bytes 122884
where the time goes:
time: 59 us; the launch traced here: 58.8 us
  blocking collectives  45.1 us (76%)
  local copies, waits for them, and re-layouts  10.8 us (18%)
  other arithmetic  1.72 us (3%)
  matrix products  1.08 us (2%)
    all_gather x1, blocking collectives, shards(): lax.all_gather(pieces[:, 0, :], 'wide', axis=0, tiled=True)  43 us
    gather x2, local copies, waits for them, and re-layouts, shards(): weight = 1.0 / (e_cond[pair_cond] - e_val[pair_val])  6.29 us
    gather x2, local copies, waits for them, and re-layouts, shards(): dens_local = val_orb[:, pair_val] * cond_orb[:, pair_cond]  2.68 us
    all_gather x1, blocking collectives, shards(): columns = lax.all_gather(dens_local, 'narrow', axis=0, tiled=True)  2.13 us
    unnamed x16, local copies, waits for them, and re-layouts  1.68 us

commit v1 on v0

v1 whole, which is shorter than its diff:
```python
import functools

import jax
import jax.numpy as jnp
from jax import lax
from jax.experimental import pallas as pl
from jax.experimental.pallas import tpu as pltpu
from jax.sharding import PartitionSpec as P

SLAB_DEV = 8
ROWS = 8
LANES = 128
CHUNK = 256
MIB = 1 << 20


def params(mib):
    return pltpu.CompilerParams(vmem_limit_bytes=mib * MIB)


def split(x, terms):
    out = []
    for _ in range(terms - 1):
        out.append(x.astype(jnp.bfloat16))
        x = x - out[-1].astype(jnp.float32)
    return out + [x.astype(jnp.bfloat16)]


def one_hot(idx, chunk):
    place = lax.broadcasted_iota(jnp.int32, (chunk, idx.shape[1]), 0)
    return jnp.where(place == (idx & (chunk - 1)), 1.0, 0.0).astype(jnp.bfloat16)


def by_chunk(rows, chunk):
    return jnp.concatenate([rows[:, at : at + chunk] for at in range(0, rows.shape[1], chunk)], axis=0)


def own_chunk(every, idx, chunk, r):
    chunk_of = idx >> (chunk.bit_length() - 1)
    out = every[:r]
    for c in range(1, every.shape[0] // r):
        out = jnp.where(chunk_of == c, every[c * r : (c + 1) * r], out)
    return out


def pick_few(rows, hot, idx):
    terms = split(by_chunk(rows, CHUNK), 3)
    m = terms[0].shape[0]
    every = jnp.dot(jnp.concatenate(terms, axis=0), hot, preferred_element_type=jnp.float32)
    return own_chunk(every[:m] + (every[m : 2 * m] + every[2 * m :]), idx, CHUNK, rows.shape[0])


def pick_many(rows, idx):
    hot = one_hot(idx, 2 * CHUNK)
    terms = jnp.concatenate(split(by_chunk(rows, 2 * CHUNK), 2), axis=1)
    every = jnp.dot(terms, jnp.concatenate([hot, hot], axis=0), preferred_element_type=jnp.float32)
    return own_chunk(every, idx, 2 * CHUNK, rows.shape[0])


def slab_kernel(val_ref, cond_ref, pv_ref, pc_ref, *refs):
    *out_refs, val, cond, pv, pc, sems = refs
    moves = ((pv_ref, pv), (pc_ref, pc), (val_ref.at[pl.ds(0, ROWS)], val), (cond_ref.at[pl.ds(0, ROWS)], cond))
    copies = [pltpu.make_async_copy(src, dst, sems.at[i]) for i, (src, dst) in enumerate(moves)]
    for copy in copies:
        copy.start()
    copies[0].wait()
    pv = pv[...]
    hot_v = one_hot(pv, CHUNK)
    copies[1].wait()
    pc = pc[...]
    hot_c = one_hot(pc, CHUNK)
    copies[2].wait()
    dens = pick_few(val[...], hot_v, pv)
    copies[3].wait()
    dens = dens * pick_few(cond[...], hot_c, pc)
    n_narrow = len(out_refs)
    sub, share = SLAB_DEV // n_narrow, dens.shape[1] // n_narrow
    for n, out_ref in enumerate(out_refs):
        for to in range(n_narrow):
            rows = dens[to * sub : (to + 1) * sub, n * share : (n + 1) * share]
            out_ref[to] = by_chunk(rows, LANES)


def with_energy(orb_ref, e_ref):
    return jnp.concatenate([orb_ref[...], jnp.broadcast_to(e_ref[...], (ROWS, e_ref.shape[1]))], axis=0)


def val_kernel(val_ref, ev_ref, pv_ref, out_ref):
    out_ref[...] = pick_many(with_energy(val_ref, ev_ref), pv_ref[...])


def dens_kernel(cond_ref, ec_ref, pc_ref, v_ref, out_ref):
    r = out_ref.shape[0]
    c = pick_many(with_energy(cond_ref, ec_ref), pc_ref[...])
    weight = 1.0 / (c[r : r + 1] - v_ref[r : r + 1])
    out_ref[...] = v_ref[:r] * c[:r] * weight


def by_source(parts, me):
    step = 1
    while step < len(parts):
        odd = (me & step) != 0
        parts = [jnp.where(odd, parts[j ^ step], parts[j]) for j in range(len(parts))]
        step *= 2
    return parts


def product_kernel(chi_ref, slab_ref, *refs):
    cols_refs, out_ref = refs[:-1], refs[-1]
    n_narrow = len(cols_refs)
    sub = SLAB_DEV // n_narrow
    contract = (((1,), (1,)), ((), ()))
    dot = functools.partial(lax.dot_general, dimension_numbers=contract, preferred_element_type=jnp.float32)
    lanes = []
    for n in range(n_narrow):
        for at in range(0, slab_ref.shape[1], sub):
            lanes.append([slab_ref[w, at : at + sub] for w in range(n, slab_ref.shape[0], n_narrow)])
    slab = jnp.concatenate([jnp.concatenate(rows, axis=0) for rows in lanes], axis=1)
    s_hi, s_lo = split(slab, 2)
    cols = by_source([ref[...] for ref in cols_refs], lax.axis_index("narrow"))
    d_hi, d_lo = split(jnp.concatenate(cols, axis=0), 2)
    out_ref[...] = chi_ref[...] + (dot(s_hi, d_hi) + (dot(s_hi, d_lo) + dot(s_lo, d_hi)))


def in_hbm(x):
    return pltpu.with_memory_space_constraint(x, pltpu.HBM)


def shards(chi_in, val_orb, cond_orb, e_val, e_cond, pair_val, pair_cond):
    n_wide, n_narrow = lax.axis_size("wide"), lax.axis_size("narrow")
    row_sub = SLAB_DEV // n_narrow
    pairs, rows, bands = pair_val.shape[1], val_orb.shape[0], val_orb.shape[1]
    tile_rows = row_sub * (pairs // n_narrow // LANES)
    vmem = pl.BlockSpec(memory_space=pltpu.VMEM)
    hbm = pl.BlockSpec(memory_space=pltpu.HBM)
    mine = pl.pallas_call(
        slab_kernel,
        in_specs=[hbm] * 4,
        out_specs=[vmem] * n_narrow,
        out_shape=[jax.ShapeDtypeStruct((n_narrow, tile_rows, LANES), jnp.float32)] * n_narrow,
        scratch_shapes=[
            pltpu.VMEM((ROWS, bands), jnp.float32),
            pltpu.VMEM((ROWS, bands), jnp.float32),
            pltpu.VMEM((1, pairs), jnp.int32),
            pltpu.VMEM((1, pairs), jnp.int32),
            pltpu.SemaphoreType.DMA((4,)),
        ],
        compiler_params=params(16),
        name="slab_rows",
    )(*(in_hbm(x) for x in (val_orb, cond_orb, pair_val, pair_cond)))
    def exchange(x, axis, bit):
        return lax.ppermute(x, axis, [(i, i ^ bit) for i in range(lax.axis_size(axis))])

    def exchange(x, bit):
        return lax.ppermute(x, "narrow", [(i, i ^ bit) for i in range(n_narrow)])

    share = mine[0]
    for n in range(1, n_narrow):
        share = jnp.where(lax.axis_index("narrow") == n, exchange(mine[n], n), share)
    parts = jnp.broadcast_to(share[None], (n_wide, *share.shape)).reshape(-1, *share.shape[1:])
    pair_val, pair_cond, parts = lax.optimization_barrier((pair_val, pair_cond, parts))
    slab = lax.all_to_all(parts, ("wide", "narrow"), 0, 0, tiled=True)
    v = pl.pallas_call(
        val_kernel,
        in_specs=[vmem] * 3,
        out_specs=vmem,
        out_shape=jax.ShapeDtypeStruct((rows + ROWS, pairs), jnp.float32),
        compiler_params=params(24),
        name="val_columns",
    )(val_orb, e_val[None, :], pair_val)
    own = pl.pallas_call(
        dens_kernel,
        in_specs=[vmem] * 4,
        out_specs=vmem,
        out_shape=jax.ShapeDtypeStruct((rows, pairs), jnp.float32),
        compiler_params=params(24),
        name="densities",
    )(cond_orb, e_cond[None, :], pair_cond, v)
    columns = [own] + [exchange(own, n) for n in range(1, n_narrow)]
    out = pl.pallas_call(
        product_kernel,
        in_specs=[vmem] * (2 + len(columns)),
        out_specs=vmem,
        out_shape=jax.ShapeDtypeStruct(chi_in.shape[::-1], jnp.float32),
        compiler_params=params(16),
        name="product",
    )(chi_in.T, slab, *columns)
    return out.T


def solution(mesh):
    placed = (
        P("wide", "narrow"),
        P(("wide", "narrow"), None),
        P(("wide", "narrow"), None),
        P(),
        P(),
        P(),
        P(),
    )
    return jax.shard_map(
        shards, mesh=mesh, in_specs=placed, out_specs=P("wide", "narrow"), check_vma=False
    )
```

time: 59 us -> 20.2 us (0.34)
  blocking collectives: 45.1 us -> 0 us
  local copies, waits for them, and re-layouts: 10.8 us -> 0.68 us
  starting transfers between devices: 0 us -> 8.02 us
  waiting for transfers between devices: 0 us -> 6.75 us
  Pallas kernels: 0 us -> 4.42 us
  other arithmetic: 1.72 us -> 0.01 us
  matrix products: 1.08 us -> 0 us
    all_gather x2 -> x0, blocking collectives: 45.1 us -> none  [the longest x1 43 us: shards(): lax.all_gather(pieces[:, 0, :], 'wide', axis=0, tiled=True)]
    gather x4 -> x0, local copies, waits for them, and re-layouts: 8.97 us -> none  [the longest x2 6.29 us: shards(): weight = 1.0 / (e_cond[pair_cond] - e_val[pair_val])]
    all_to_all x0 -> x1, starting transfers between devices: none -> 7.18 us  [shards(): slab = lax.all_to_all(parts, ('wide', 'narrow'), 0, 0, tiled=True)]
    all_to_all x0 -> x1, waiting for transfers between devices: none -> 4.78 us  [shards(): slab = lax.all_to_all(parts, ('wide', 'narrow'), 0, 0, tiled=True)]
    pallas_call x0 -> x4, Pallas kernels: none -> 4.42 us  [the longest x1 1.59 us: shards(): pl.pallas_call(slab_kernel, in_specs=[hbm] * 4, out_specs=[vmem] * n_narr...]
    ppermute x0 -> x2, waiting for transfers between devices: none -> 1.97 us  [exchange(): return lax.ppermute(x, 'narrow', [(i, i ^ bit) for i in range(n_narrow)])]
    unnamed x16 -> x14, local copies, waits for them, and re-layouts: 1.68 us -> 0.04 us
    dot_general x1 -> x0, matrix products: 1.08 us -> none  [shards(): jnp.dot(block_cols, lax.all_gather(pieces[:, 0, :], 'wide', axis=0, tiled...]
  transfers between devices with their start and end apart: 0 -> 3, of which waited for: 0 -> 3; matrix products, arithmetic and copies ran while one was open for 0% -> 0% of each run, Pallas kernels for 0% -> 10%
where the time goes in v1:
time: 20.2 us; the launch traced here: 20 us
  starting transfers between devices  8.02 us (40%)
  waiting for transfers between devices  6.75 us (33%)
  Pallas kernels  4.42 us (22%)
  local copies, waits for them, and re-layouts  0.68 us (3%)
    all_to_all x1, starting transfers between devices, shards(): slab = lax.all_to_all(parts, ('wide', 'narrow'), 0, 0, tiled=True)  7.18 us
    all_to_all x1, waiting for transfers between devices, shards(): slab = lax.all_to_all(parts, ('wide', 'narrow'), 0, 0, tiled=True)  4.78 us
    ppermute x2, waiting for transfers between devices, exchange(): return lax.ppermute(x, 'narrow', [(i, i ^ bit) for i in range(n_narrow)])  1.97 us
    pallas_call x1, Pallas kernels, shards(): pl.pallas_call(slab_kernel, in_specs=[hbm] * 4, out_specs=[vmem] * n_narr...  1.59 us
    pallas_call x1, Pallas kernels, shards(): pl.pallas_call(dens_kernel, in_specs=[vmem] * 4, out_specs=vmem, out_shap...  0.96 us
    pallas_call x1, Pallas kernels, shards(): pl.pallas_call(val_kernel, in_specs=[vmem] * 3, out_specs=vmem, out_shape...  0.94 us
    pallas_call x1, Pallas kernels, shards(): pl.pallas_call(product_kernel, in_specs=[vmem] * (2 + len(columns)), out_...  0.93 us
    ppermute x2, starting transfers between devices, exchange(): return lax.ppermute(x, 'narrow', [(i, i ^ bit) for i in range(n_narrow)])  0.84 us
  transfers between devices with their start and end apart: 3, of which 3 were waited for; matrix products, arithmetic and copies ran while one was open for 0% of the time, Pallas kernels for 10%

profile of v1, /device:TPU:0, one launch (start us, length us, event | category | flops | bytes accessed | tf_op | source)
XLA Modules:
  0.0 20.0 jit_solution(1986905861168208183)
XLA Ops:
  0.0 0.0 copy-start.5
  0.0 0.0 copy-start
  0.0 0.0 copy-start.3
  0.0 1.6 %slab_rows.1 = (f32[2,8,128]{2,1,0:T(8,128)S(1)}, f32[2,8,128]{2,1,0:T(8,128)S(1)}) custom-call(f32[80,4096]{1,0:T(8,128)} %val_ref.3, f32[80,4096]{1,0:T(8,128)} %cond_ref.3, s32[1,512]{1,0:T(1,128)} %pv_ref.2, s32[1,512]{1,0:T(1,128)} %pc_ref.2), custom_call_target="tpu_custom_call" | custom-call | tf_op jit(solution)/shard_map/slab_rows/pallas_call | solution.py:136
  1.6 0.0 copy-start.1
  1.6 0.0 copy-start.4
  1.6 0.0 copy-start.6
  1.6 0.5 %collective-permute-start = (f32[2,8,128]{2,1,0:T(8,128)S(1)}, f32[2,8,128]{2,1,0:T(8,128)S(1)}, u32[]{:S(2)}, u32[]{:S(2)}) collective-permute-start(f32[2,8,128]{2,1,0:T(8,128)S(1)} %get-tuple-element.10), channel_id=1, source_target_pairs={{0,1},{1,0},{2,3},{3,2},{4,5},{5,4},{6,7},{7,6},{8,9},{9,8},{10,11... | collective-permute-start | bytes 24584 | tf_op jit(solution)/shard_map/ppermute | solution.py:155
  2.2 0.8 %collective-permute-done = f32[2,8,128]{2,1,0:T(8,128)S(1)} collective-permute-done((f32[2,8,128]{2,1,0:T(8,128)S(1)}, f32[2,8,128]{2,1,0:T(8,128)S(1)}, u32[]{:S(2)}, u32[]{:S(2)}) %collective-permute-start) | collective-permute-done | bytes 8224 | tf_op jit(solution)/shard_map/ppermute | solution.py:155
  3.0 0.6 %broadcast_in_dim.12 = f32[16,2,8,128]{3,2,1,0:T(8,128)} broadcast(f32[2,8,128]{2,1,0:T(8,128)S(1)} %broadcast_select_fusion), dimensions={1,2,3} | broadcast | bytes 139264 | tf_op jit(solution)/shard_map/broadcast_in_dim | solution.py:160
  3.6 7.2 %all-to-all-start = ((f32[32,8,128]{2,1,0:T(8,128)}), f32[32,8,128]{2,1,0:T(8,128)S(1)}, u32[]{:S(2)}, u32[]{:S(2)}) async-start(f32[32,8,128]{2,1,0:T(8,128)} %bitcast.1), calls=%async_computation | async-start | bytes 262144 | tf_op jit(solution)/shard_map/all_to_all | solution.py:162
  10.8 0.0 copy-done.5
  10.8 0.0 copy-done
  10.9 0.0 copy-done.3
  10.9 0.0 copy-start.2
  10.9 0.9 %val_columns.1.v_ref = f32[88,512]{1,0:T(8,128)S(1)} custom-call(f32[80,4096]{1,0:T(8,128)S(1)} %copy-done, f32[1,4096]{1,0:T(1,128)S(1)} %bitcast.6, s32[1,512]{1,0:T(1,128)S(1)} %copy-done.5), custom_call_target="tpu_custom_call" | custom-call | tf_op jit(solution)/shard_map/val_columns/pallas_call | solution.py:163
  11.8 0.0 copy-done.1
  11.8 0.0 copy-done.4
  11.8 0.0 copy-done.6
  11.9 1.0 %densities.1.refs_0_ = f32[80,512]{1,0:T(8,128)S(1)} custom-call(f32[80,4096]{1,0:T(8,128)S(1)} %copy-done.1, f32[1,4096]{1,0:T(1,128)S(1)} %bitcast.7, s32[1,512]{1,0:T(1,128)S(1)} %copy-done.6, f32[88,512]{1,0:T(8,128)S(1)} %val_columns.1.v_ref), custom_call_target="tpu_custom_call" | custom-call | tf_op jit(solution)/shard_map/densities/pallas_call | solution.py:171
  12.8 0.3 %collective-permute-start.1 = (f32[80,512]{1,0:T(8,128)S(1)}, f32[80,512]{1,0:T(8,128)S(1)}, u32[]{:S(2)}, u32[]{:S(2)}) collective-permute-start(f32[80,512]{1,0:T(8,128)S(1)} %densities.1.refs_0_), channel_id=1, source_target_pairs={{0,1},{1,0},{2,3},{3,2},{4,5},{5,4},{6,7},{7,6},{8,9},{9,8},{10,11... | collective-permute-start | bytes 491528 | tf_op jit(solution)/shard_map/ppermute | solution.py:155
  13.1 1.1 %collective-permute-done.1.refs_1_ = f32[80,512]{1,0:T(8,128)S(1)} collective-permute-done((f32[80,512]{1,0:T(8,128)S(1)}, f32[80,512]{1,0:T(8,128)S(1)}, u32[]{:S(2)}, u32[]{:S(2)}) %collective-permute-start.1) | collective-permute-done | bytes 163872 | tf_op jit(solution)/shard_map/ppermute | solution.py:155
  14.3 4.8 %all-to-all-done.slab_ref = f32[32,8,128]{2,1,0:T(8,128)S(1)} async-done(((f32[32,8,128]{2,1,0:T(8,128)}), f32[32,8,128]{2,1,0:T(8,128)S(1)}, u32[]{:S(2)}, u32[]{:S(2)}) %all-to-all-start) | async-done | bytes 131104 | tf_op jit(solution)/shard_map/all_to_all | solution.py:162
  19.1 0.0 copy-done.2
  19.1 0.9 %product.1 = f32[64,160]{1,0:T(8,128)} custom-call(f32[64,160]{1,0:T(8,128)S(1)} %bitcast.5, f32[32,8,128]{2,1,0:T(8,128)S(1)} %all-to-all-done.slab_ref, f32[80,512]{1,0:T(8,128)S(1)} %densities.1.refs_0_, f32[80,512]{1,0:T(8,128)S(1)} %collective-permute-done.1.refs_1_), custom_call_target="tpu_custom_call" | custom-call | tf_op jit(solution)/shard_map/product/pallas_call | solution.py:180
  (1 shorter events, 0.0 us)
Async XLA Ops:
  0.0 10.8 %copy-start.5 = (s32[1,512]{1,0:T(1,128)S(1)}, s32[1,512]{1,0:T(1,128)}, u32[]{:S(2)}) copy-start(s32[1,512]{1,0:T(1,128)} %pv_ref.2) | copy-start | bytes 6148
  0.0 10.8 %copy-start = (f32[80,4096]{1,0:T(8,128)S(1)}, f32[80,4096]{1,0:T(8,128)}, u32[]{:S(2)}) copy-start(f32[80,4096]{1,0:T(8,128)} %val_ref.3) | copy-start | bytes 3932164
  0.0 10.9 %copy-start.3 = (f32[4096]{0:T(1024)S(1)}, f32[4096]{0:T(1024)}, u32[]{:S(2)}) copy-start(f32[4096]{0:T(1024)} %param.10) | copy-start | bytes 49156
  1.6 10.2 %copy-start.1 = (f32[80,4096]{1,0:T(8,128)S(1)}, f32[80,4096]{1,0:T(8,128)}, u32[]{:S(2)}) copy-start(f32[80,4096]{1,0:T(8,128)} %cond_ref.3) | copy-start | bytes 3932164
  1.6 10.2 %copy-start.4 = (f32[4096]{0:T(1024)S(1)}, f32[4096]{0:T(1024)}, u32[]{:S(2)}) copy-start(f32[4096]{0:T(1024)} %param.11) | copy-start | bytes 49156
  1.6 10.2 %copy-start.6 = (s32[1,512]{1,0:T(1,128)S(1)}, s32[1,512]{1,0:T(1,128)}, u32[]{:S(2)}) copy-start(s32[1,512]{1,0:T(1,128)} %pc_ref.2) | copy-start | bytes 6148
  1.6 1.4 %collective-permute-start = (f32[2,8,128]{2,1,0:T(8,128)S(1)}, f32[2,8,128]{2,1,0:T(8,128)S(1)}, u32[]{:S(2)}, u32[]{:S(2)}) collective-permute-start(f32[2,8,128]{2,1,0:T(8,128)S(1)} %get-tuple-element.10), channel_id=1, source_target_pairs={{0,1},{1,0},{2,3},{3,2},{4,5},{5,4},{6,7},{7,6},{8,9},{9,8},{10,11... | collective-permute-start | bytes 24584 | tf_op jit(solution)/shard_map/ppermute | solution.py:155
  3.6 15.4 %all-to-all-start = ((f32[32,8,128]{2,1,0:T(8,128)}), f32[32,8,128]{2,1,0:T(8,128)S(1)}, u32[]{:S(2)}, u32[]{:S(2)}) async-start(f32[32,8,128]{2,1,0:T(8,128)} %bitcast.1), calls=%async_computation | async-start | bytes 262144 | tf_op jit(solution)/shard_map/all_to_all | solution.py:162
  10.9 8.2 %copy-start.2 = (f32[160,64]{0,1:T(8,128)S(1)}, f32[160,64]{0,1:T(8,128)}, u32[]{:S(2)}) copy-start(f32[160,64]{0,1:T(8,128)} %param.7) | copy-start | bytes 122884
  12.8 1.5 %collective-permute-start.1 = (f32[80,512]{1,0:T(8,128)S(1)}, f32[80,512]{1,0:T(8,128)S(1)}, u32[]{:S(2)}, u32[]{:S(2)}) collective-permute-start(f32[80,512]{1,0:T(8,128)S(1)} %densities.1.refs_0_), channel_id=1, source_target_pairs={{0,1},{1,0},{2,3},{3,2},{4,5},{5,4},{6,7},{7,6},{8,9},{9,8},{10,11... | collective-permute-start | bytes 491528 | tf_op jit(solution)/shard_map/ppermute | solution.py:155

commit v2 on v1

--- a/solution.py
+++ b/solution.py
@@ -77,8 +77,18 @@
     sub, share = SLAB_DEV // n_narrow, dens.shape[1] // n_narrow
     for n, out_ref in enumerate(out_refs):
         for to in range(n_narrow):
-            rows = dens[to * sub : (to + 1) * sub, n * share : (n + 1) * share]
-            out_ref[to] = by_chunk(rows, LANES)
+            out_ref[to] = by_chunk(dens[to * sub : (to + 1) * sub, n * share : (n + 1) * share], LANES)
+
+
+def spread_kernel(*refs):
+    *share_refs, out_ref = refs
+    narrow = lax.axis_index("narrow")
+    n_narrow = len(share_refs)
+    share = [ref[...] for ref in share_refs]
+    for n in range(1, n_narrow):
+        share[0] = jnp.where(narrow == n, share[n], share[0])
+    for place in range(out_ref.shape[0]):
+        out_ref[place] = share[0][place % n_narrow]
 
 
 def with_energy(orb_ref, e_ref):
@@ -105,21 +115,24 @@
     return parts
 
 
-def product_kernel(chi_ref, slab_ref, *refs):
-    cols_refs, out_ref = refs[:-1], refs[-1]
-    n_narrow = len(cols_refs)
+def columns_kernel(*refs):
+    *cols_refs, hi_ref, lo_ref = refs
+    cols = by_source([ref[...] for ref in cols_refs], lax.axis_index("narrow"))
+    hi_ref[...], lo_ref[...] = split(jnp.concatenate(cols, axis=0).T, 2)
+
+
+def product_kernel(n_narrow, chi_ref, slab_ref, hi_ref, lo_ref, out_ref):
     sub = SLAB_DEV // n_narrow
-    contract = (((1,), (1,)), ((), ()))
-    dot = functools.partial(lax.dot_general, dimension_numbers=contract, preferred_element_type=jnp.float32)
     lanes = []
     for n in range(n_narrow):
         for at in range(0, slab_ref.shape[1], sub):
             lanes.append([slab_ref[w, at : at + sub] for w in range(n, slab_ref.shape[0], n_narrow)])
     slab = jnp.concatenate([jnp.concatenate(rows, axis=0) for rows in lanes], axis=1)
     s_hi, s_lo = split(slab, 2)
-    cols = by_source([ref[...] for ref in cols_refs], lax.axis_index("narrow"))
-    d_hi, d_lo = split(jnp.concatenate(cols, axis=0), 2)
-    out_ref[...] = chi_ref[...] + (dot(s_hi, d_hi) + (dot(s_hi, d_lo) + dot(s_lo, d_hi)))
+    m = slab.shape[0]
+    by_hi = jnp.dot(jnp.concatenate([s_hi, s_lo], axis=0), hi_ref[...], preferred_element_type=jnp.float32)
+    by_lo = jnp.dot(s_hi, lo_ref[...], preferred_element_type=jnp.float32)
+    out_ref[...] = chi_ref[...] + (by_hi[:m] + (by_hi[m:] + by_lo))
 
 
 def in_hbm(x):
@@ -133,11 +146,12 @@
     tile_rows = row_sub * (pairs // n_narrow // LANES)
     vmem = pl.BlockSpec(memory_space=pltpu.VMEM)
     hbm = pl.BlockSpec(memory_space=pltpu.HBM)
+    share = jax.ShapeDtypeStruct((n_narrow, tile_rows, LANES), jnp.float32)
     mine = pl.pallas_call(
         slab_kernel,
         in_specs=[hbm] * 4,
         out_specs=[vmem] * n_narrow,
-        out_shape=[jax.ShapeDtypeStruct((n_narrow, tile_rows, LANES), jnp.float32)] * n_narrow,
+        out_shape=[share] * n_narrow,
         scratch_shapes=[
             pltpu.VMEM((ROWS, bands), jnp.float32),
             pltpu.VMEM((ROWS, bands), jnp.float32),
@@ -148,16 +162,21 @@
         compiler_params=params(16),
         name="slab_rows",
     )(*(in_hbm(x) for x in (val_orb, cond_orb, pair_val, pair_cond)))
+
     def exchange(x, axis, bit):
         return lax.ppermute(x, axis, [(i, i ^ bit) for i in range(lax.axis_size(axis))])
 
     def exchange(x, bit):
         return lax.ppermute(x, "narrow", [(i, i ^ bit) for i in range(n_narrow)])
 
-    share = mine[0]
-    for n in range(1, n_narrow):
-        share = jnp.where(lax.axis_index("narrow") == n, exchange(mine[n], n), share)
-    parts = jnp.broadcast_to(share[None], (n_wide, *share.shape)).reshape(-1, *share.shape[1:])
+    parts = pl.pallas_call(
+        spread_kernel,
+        in_specs=[vmem] * n_narrow,
+        out_specs=vmem,
+        out_shape=pltpu.VMEM((n_wide * n_narrow, tile_rows, LANES), jnp.float32),
+        compiler_params=params(4),
+        name="spread",
+    )(mine[0], *(exchange(mine[n], n) for n in range(1, n_narrow)))
     pair_val, pair_cond, parts = lax.optimization_barrier((pair_val, pair_cond, parts))
     slab = lax.all_to_all(parts, ("wide", "narrow"), 0, 0, tiled=True)
     v = pl.pallas_call(
@@ -177,14 +196,22 @@
         name="densities",
     )(cond_orb, e_cond[None, :], pair_cond, v)
     columns = [own] + [exchange(own, n) for n in range(1, n_narrow)]
+    terms = pl.pallas_call(
+        columns_kernel,
+        in_specs=[vmem] * n_narrow,
+        out_specs=[vmem] * 2,
+        out_shape=[jax.ShapeDtypeStruct((pairs, n_narrow * rows), jnp.bfloat16)] * 2,
+        compiler_params=params(16),
+        name="columns",
+    )(*columns)
     out = pl.pallas_call(
-        product_kernel,
-        in_specs=[vmem] * (2 + len(columns)),
+        functools.partial(product_kernel, n_narrow),
+        in_specs=[vmem] * 4,
         out_specs=vmem,
         out_shape=jax.ShapeDtypeStruct(chi_in.shape[::-1], jnp.float32),
         compiler_params=params(16),
         name="product",
-    )(chi_in.T, slab, *columns)
+    )(chi_in.T, slab, *terms)
     return out.T
 
 

time: 20.2 us -> 20.1 us (level)
  Pallas kernels: 4.42 us -> 5.21 us
  local copies, waits for them, and re-layouts: 0.68 us -> 0.04 us
  waiting for transfers between devices: 6.75 us -> 6.53 us
    pallas_call x1 -> x3, Pallas kernels: 0.93 us -> 1.72 us  [the longest x1 0.85 us: shards(): pl.pallas_call(functools.partial(product_kernel, n_narrow), in_specs=[vme...]
    broadcast_in_dim x1 -> x0, local copies, waits for them, and re-layouts: 0.65 us -> none  [shards(): jnp.broadcast_to(share[None], (n_wide, *share.shape))]
    all_to_all x1, waiting for transfers between devices: 4.78 us -> 4.56 us  [shards(): slab = lax.all_to_all(parts, ('wide', 'narrow'), 0, 0, tiled=True)]
  transfers between devices with their start and end apart: 3 -> 3, of which waited for: 3 -> 3; matrix products, arithmetic and copies ran while one was open for 0% -> 0% of each run, Pallas kernels for 10% -> 11%
where the time goes in v2:
time: 20.1 us; the launch traced here: 19.9 us
  starting transfers between devices  8.02 us (40%)
  waiting for transfers between devices  6.53 us (32%)
  Pallas kernels  5.21 us (26%)
    all_to_all x1, starting transfers between devices, shards(): slab = lax.all_to_all(parts, ('wide', 'narrow'), 0, 0, tiled=True)  7.18 us
    all_to_all x1, waiting for transfers between devices, shards(): slab = lax.all_to_all(parts, ('wide', 'narrow'), 0, 0, tiled=True)  4.56 us
    ppermute x2, waiting for transfers between devices, exchange(): return lax.ppermute(x, 'narrow', [(i, i ^ bit) for i in range(n_narrow)])  1.97 us
    pallas_call x1, Pallas kernels, shards(): pl.pallas_call(slab_kernel, in_specs=[hbm] * 4, out_specs=[vmem] * n_narr...  1.59 us
    pallas_call x1, Pallas kernels, shards(): pl.pallas_call(dens_kernel, in_specs=[vmem] * 4, out_specs=vmem, out_shap...  0.96 us
    pallas_call x1, Pallas kernels, shards(): pl.pallas_call(val_kernel, in_specs=[vmem] * 3, out_specs=vmem, out_shape...  0.94 us
    pallas_call x1, Pallas kernels, shards(): pl.pallas_call(functools.partial(product_kernel, n_narrow), in_specs=[vme...  0.85 us
    ppermute x2, starting transfers between devices, exchange(): return lax.ppermute(x, 'narrow', [(i, i ^ bit) for i in range(n_narrow)])  0.84 us
  transfers between devices with their start and end apart: 3, of which 3 were waited for; matrix products, arithmetic and copies ran while one was open for 0% of the time, Pallas kernels for 11%

profile of v2, /device:TPU:0, one launch (start us, length us, event | category | flops | bytes accessed | tf_op | source)
XLA Modules:
  0.0 19.9 jit_solution(7485355624443880181)
XLA Ops:
  0.0 0.0 copy-start.5
  0.0 0.0 copy-start
  0.0 0.0 copy-start.3
  0.0 1.6 %slab_rows.1 = (f32[2,8,128]{2,1,0:T(8,128)S(1)}, f32[2,8,128]{2,1,0:T(8,128)S(1)}) custom-call(f32[80,4096]{1,0:T(8,128)} %val_ref.3, f32[80,4096]{1,0:T(8,128)} %cond_ref.3, s32[1,512]{1,0:T(1,128)} %pv_ref.2, s32[1,512]{1,0:T(1,128)} %pc_ref.2), custom_call_target="tpu_custom_call" | custom-call | tf_op jit(solution)/shard_map/slab_rows/pallas_call | solution.py:150
  1.6 0.0 copy-start.1
  1.6 0.0 copy-start.4
  1.6 0.0 copy-start.6
  1.6 0.5 %collective-permute-start = (f32[2,8,128]{2,1,0:T(8,128)S(1)}, f32[2,8,128]{2,1,0:T(8,128)S(1)}, u32[]{:S(2)}, u32[]{:S(2)}) collective-permute-start(f32[2,8,128]{2,1,0:T(8,128)S(1)} %get-tuple-element.13), channel_id=1, source_target_pairs={{0,1},{1,0},{2,3},{3,2},{4,5},{5,4},{6,7},{7,6},{8,9},{9,8},{10,11... | collective-permute-start | bytes 24584 | tf_op jit(solution)/shard_map/ppermute | solution.py:170
  2.2 0.8 %collective-permute-done.refs_1_ = f32[2,8,128]{2,1,0:T(8,128)S(1)} collective-permute-done((f32[2,8,128]{2,1,0:T(8,128)S(1)}, f32[2,8,128]{2,1,0:T(8,128)S(1)}, u32[]{:S(2)}, u32[]{:S(2)}) %collective-permute-start) | collective-permute-done | bytes 8224 | tf_op jit(solution)/shard_map/ppermute | solution.py:170
  3.0 0.7 %spread.1 = f32[32,8,128]{2,1,0:T(8,128)} custom-call(f32[2,8,128]{2,1,0:T(8,128)S(1)} %get-tuple-element.12.refs_0_, f32[2,8,128]{2,1,0:T(8,128)S(1)} %collective-permute-done.refs_1_), custom_call_target="tpu_custom_call" | custom-call | tf_op jit(solution)/shard_map/spread/pallas_call | solution.py:172
  3.6 7.2 %all-to-all-start = ((f32[32,8,128]{2,1,0:T(8,128)}), f32[32,8,128]{2,1,0:T(8,128)S(1)}, u32[]{:S(2)}, u32[]{:S(2)}) async-start(f32[32,8,128]{2,1,0:T(8,128)} %spread.1), calls=%async_computation | async-start | bytes 262144 | tf_op jit(solution)/shard_map/all_to_all | solution.py:181
  10.8 0.0 copy-done.5
  10.9 0.0 copy-done
  10.9 0.0 copy-done.3
  10.9 0.9 %val_columns.1.v_ref = f32[88,512]{1,0:T(8,128)S(1)} custom-call(f32[80,4096]{1,0:T(8,128)S(1)} %copy-done, f32[1,4096]{1,0:T(1,128)S(1)} %bitcast.5, s32[1,512]{1,0:T(1,128)S(1)} %copy-done.5), custom_call_target="tpu_custom_call" | custom-call | tf_op jit(solution)/shard_map/val_columns/pallas_call | solution.py:182
  11.8 0.0 copy-start.2
  11.8 0.0 copy-done.1
  11.8 0.0 copy-done.4
  11.9 0.0 copy-done.6
  11.9 1.0 %densities.1.refs_0_ = f32[80,512]{1,0:T(8,128)S(1)} custom-call(f32[80,4096]{1,0:T(8,128)S(1)} %copy-done.1, f32[1,4096]{1,0:T(1,128)S(1)} %bitcast.6, s32[1,512]{1,0:T(1,128)S(1)} %copy-done.6, f32[88,512]{1,0:T(8,128)S(1)} %val_columns.1.v_ref), custom_call_target="tpu_custom_call" | custom-call | tf_op jit(solution)/shard_map/densities/pallas_call | solution.py:190
  12.8 0.3 %collective-permute-start.1 = (f32[80,512]{1,0:T(8,128)S(1)}, f32[80,512]{1,0:T(8,128)S(1)}, u32[]{:S(2)}, u32[]{:S(2)}) collective-permute-start(f32[80,512]{1,0:T(8,128)S(1)} %densities.1.refs_0_), channel_id=1, source_target_pairs={{0,1},{1,0},{2,3},{3,2},{4,5},{5,4},{6,7},{7,6},{8,9},{9,8},{10,11... | collective-permute-start | bytes 491528 | tf_op jit(solution)/shard_map/ppermute | solution.py:170
  13.1 1.1 %collective-permute-done.1.refs_1_ = f32[80,512]{1,0:T(8,128)S(1)} collective-permute-done((f32[80,512]{1,0:T(8,128)S(1)}, f32[80,512]{1,0:T(8,128)S(1)}, u32[]{:S(2)}, u32[]{:S(2)}) %collective-permute-start.1) | collective-permute-done | bytes 163872 | tf_op jit(solution)/shard_map/ppermute | solution.py:170
  14.3 0.2 %columns.1 = (bf16[512,160]{1,0:T(8,128)(2,1)S(1)}, bf16[512,160]{1,0:T(8,128)(2,1)S(1)}) custom-call(f32[80,512]{1,0:T(8,128)S(1)} %densities.1.refs_0_, f32[80,512]{1,0:T(8,128)S(1)} %collective-permute-done.1.refs_1_), custom_call_target="tpu_custom_call" | custom-call | tf_op jit(solution)/shard_map/columns/pallas_call | solution.py:199
  14.5 4.6 %all-to-all-done.slab_ref = f32[32,8,128]{2,1,0:T(8,128)S(1)} async-done(((f32[32,8,128]{2,1,0:T(8,128)}), f32[32,8,128]{2,1,0:T(8,128)S(1)}, u32[]{:S(2)}, u32[]{:S(2)}) %all-to-all-start) | async-done | bytes 131104 | tf_op jit(solution)/shard_map/all_to_all | solution.py:181
  19.1 0.0 copy-done.2
  19.1 0.8 %product.1 = f32[64,160]{1,0:T(8,128)} custom-call(f32[64,160]{1,0:T(8,128)S(1)} %bitcast.4, f32[32,8,128]{2,1,0:T(8,128)S(1)} %all-to-all-done.slab_ref, bf16[512,160]{1,0:T(8,128)(2,1)S(1)} %get-tuple-element.17.hi_ref, bf16[512,160]{1,0:T(8,128)(2,1)S(1)} %get-tuple-element.18.lo_ref), custom_call_target="tpu_custom_call" | custom-call | tf_op jit(solution)/shard_map/product/pallas_call | solution.py:207
Async XLA Ops:
  0.0 10.8 %copy-start.5 = (s32[1,512]{1,0:T(1,128)S(1)}, s32[1,512]{1,0:T(1,128)}, u32[]{:S(2)}) copy-start(s32[1,512]{1,0:T(1,128)} %pv_ref.2) | copy-start | bytes 6148
  0.0 10.9 %copy-start = (f32[80,4096]{1,0:T(8,128)S(1)}, f32[80,4096]{1,0:T(8,128)}, u32[]{:S(2)}) copy-start(f32[80,4096]{1,0:T(8,128)} %val_ref.3) | copy-start | bytes 3932164
  0.0 10.9 %copy-start.3 = (f32[4096]{0:T(1024)S(1)}, f32[4096]{0:T(1024)}, u32[]{:S(2)}) copy-start(f32[4096]{0:T(1024)} %param.10) | copy-start | bytes 49156
  1.6 10.2 %copy-start.1 = (f32[80,4096]{1,0:T(8,128)S(1)}, f32[80,4096]{1,0:T(8,128)}, u32[]{:S(2)}) copy-start(f32[80,4096]{1,0:T(8,128)} %cond_ref.3) | copy-start | bytes 3932164
  1.6 10.2 %copy-start.4 = (f32[4096]{0:T(1024)S(1)}, f32[4096]{0:T(1024)}, u32[]{:S(2)}) copy-start(f32[4096]{0:T(1024)} %param.11) | copy-start | bytes 49156
  1.6 10.2 %copy-start.6 = (s32[1,512]{1,0:T(1,128)S(1)}, s32[1,512]{1,0:T(1,128)}, u32[]{:S(2)}) copy-start(s32[1,512]{1,0:T(1,128)} %pc_ref.2) | copy-start | bytes 6148
  1.6 1.4 %collective-permute-start = (f32[2,8,128]{2,1,0:T(8,128)S(1)}, f32[2,8,128]{2,1,0:T(8,128)S(1)}, u32[]{:S(2)}, u32[]{:S(2)}) collective-permute-start(f32[2,8,128]{2,1,0:T(8,128)S(1)} %get-tuple-element.13), channel_id=1, source_target_pairs={{0,1},{1,0},{2,3},{3,2},{4,5},{5,4},{6,7},{7,6},{8,9},{9,8},{10,11... | collective-permute-start | bytes 24584 | tf_op jit(solution)/shard_map/ppermute | solution.py:170
  3.6 15.4 %all-to-all-start = ((f32[32,8,128]{2,1,0:T(8,128)}), f32[32,8,128]{2,1,0:T(8,128)S(1)}, u32[]{:S(2)}, u32[]{:S(2)}) async-start(f32[32,8,128]{2,1,0:T(8,128)} %spread.1), calls=%async_computation | async-start | bytes 262144 | tf_op jit(solution)/shard_map/all_to_all | solution.py:181
  11.8 7.3 %copy-start.2 = (f32[160,64]{0,1:T(8,128)S(1)}, f32[160,64]{0,1:T(8,128)}, u32[]{:S(2)}) copy-start(f32[160,64]{0,1:T(8,128)} %param.7) | copy-start | bytes 122884
  12.8 1.5 %collective-permute-start.1 = (f32[80,512]{1,0:T(8,128)S(1)}, f32[80,512]{1,0:T(8,128)S(1)}, u32[]{:S(2)}, u32[]{:S(2)}) collective-permute-start(f32[80,512]{1,0:T(8,128)S(1)} %densities.1.refs_0_), channel_id=1, source_target_pairs={{0,1},{1,0},{2,3},{3,2},{4,5},{5,4},{6,7},{7,6},{8,9},{9,8},{10,11... | collective-permute-start | bytes 491528 | tf_op jit(solution)/shard_map/ppermute | solution.py:170

commit v3 on v2

--- a/solution.py
+++ b/solution.py
@@ -88,7 +88,7 @@
     for n in range(1, n_narrow):
         share[0] = jnp.where(narrow == n, share[n], share[0])
     for place in range(out_ref.shape[0]):
-        out_ref[place] = share[0][place % n_narrow]
+        out_ref[out_ref.shape[0] - 1 - place] = share[0][place % n_narrow]
 
 
 def with_energy(orb_ref, e_ref):
@@ -123,10 +123,10 @@
 
 def product_kernel(n_narrow, chi_ref, slab_ref, hi_ref, lo_ref, out_ref):
     sub = SLAB_DEV // n_narrow
-    lanes = []
+    lanes, blocks = [], slab_ref.shape[0]
     for n in range(n_narrow):
         for at in range(0, slab_ref.shape[1], sub):
-            lanes.append([slab_ref[w, at : at + sub] for w in range(n, slab_ref.shape[0], n_narrow)])
+            lanes.append([slab_ref[blocks - 1 - w, at : at + sub] for w in range(n, blocks, n_narrow)])
     slab = jnp.concatenate([jnp.concatenate(rows, axis=0) for rows in lanes], axis=1)
     s_hi, s_lo = split(slab, 2)
     m = slab.shape[0]
@@ -173,12 +173,13 @@
         spread_kernel,
         in_specs=[vmem] * n_narrow,
         out_specs=vmem,
-        out_shape=pltpu.VMEM((n_wide * n_narrow, tile_rows, LANES), jnp.float32),
-        compiler_params=params(4),
+        out_shape=jax.ShapeDtypeStruct((n_wide * n_narrow, tile_rows, LANES), jnp.float32),
+        compiler_params=params(16),
         name="spread",
     )(mine[0], *(exchange(mine[n], n) for n in range(1, n_narrow)))
     pair_val, pair_cond, parts = lax.optimization_barrier((pair_val, pair_cond, parts))
-    slab = lax.all_to_all(parts, ("wide", "narrow"), 0, 0, tiled=True)
+    last_first = [list(range(n_wide * n_narrow))[::-1]]
+    slab = lax.all_to_all(parts, ("wide", "narrow"), 0, 0, axis_index_groups=last_first, tiled=True)
     v = pl.pallas_call(
         val_kernel,
         in_specs=[vmem] * 3,

time: 20.1 us -> 19.8 us (0.985)
  waiting for transfers between devices: 6.53 us -> 6.21 us
    all_to_all x1, waiting for transfers between devices: 4.56 us -> 4.24 us  [shards(): lax.all_to_all(parts, ('wide', 'narrow'), 0, 0, axis_index_groups=last_fi...]
where the time goes in v3:
time: 19.8 us; the launch traced here: 19.6 us
  starting transfers between devices  8.02 us (41%)
  waiting for transfers between devices  6.21 us (31%)
  Pallas kernels  5.21 us (26%)
    all_to_all x1, starting transfers between devices, shards(): lax.all_to_all(parts, ('wide', 'narrow'), 0, 0, axis_index_groups=last_fi...  7.18 us
    all_to_all x1, waiting for transfers between devices, shards(): lax.all_to_all(parts, ('wide', 'narrow'), 0, 0, axis_index_groups=last_fi...  4.24 us
    ppermute x2, waiting for transfers between devices, exchange(): return lax.ppermute(x, 'narrow', [(i, i ^ bit) for i in range(n_narrow)])  1.97 us
    pallas_call x1, Pallas kernels, shards(): pl.pallas_call(slab_kernel, in_specs=[hbm] * 4, out_specs=[vmem] * n_narr...  1.59 us
    pallas_call x1, Pallas kernels, shards(): pl.pallas_call(dens_kernel, in_specs=[vmem] * 4, out_specs=vmem, out_shap...  0.96 us
    pallas_call x1, Pallas kernels, shards(): pl.pallas_call(val_kernel, in_specs=[vmem] * 3, out_specs=vmem, out_shape...  0.94 us
    pallas_call x1, Pallas kernels, shards(): pl.pallas_call(functools.partial(product_kernel, n_narrow), in_specs=[vme...  0.85 us
    ppermute x2, starting transfers between devices, exchange(): return lax.ppermute(x, 'narrow', [(i, i ^ bit) for i in range(n_narrow)])  0.84 us
  transfers between devices with their start and end apart: 3, of which 3 were waited for; matrix products, arithmetic and copies ran while one was open for 0% of the time, Pallas kernels for 11%

profile of v3, /device:TPU:0, one launch (start us, length us, event | category | flops | bytes accessed | tf_op | source)
XLA Modules:
  0.0 19.6 jit_solution(6830940437030357679)
XLA Ops:
  0.0 0.0 copy-start.5
  0.0 0.0 copy-start
  0.0 0.0 copy-start.3
  0.0 1.6 %slab_rows.1 = (f32[2,8,128]{2,1,0:T(8,128)S(1)}, f32[2,8,128]{2,1,0:T(8,128)S(1)}) custom-call(f32[80,4096]{1,0:T(8,128)} %val_ref.3, f32[80,4096]{1,0:T(8,128)} %cond_ref.3, s32[1,512]{1,0:T(1,128)} %pv_ref.2, s32[1,512]{1,0:T(1,128)} %pc_ref.2), custom_call_target="tpu_custom_call" | custom-call | tf_op jit(solution)/shard_map/slab_rows/pallas_call | solution.py:150
  1.6 0.0 copy-start.1
  1.6 0.0 copy-start.4
  1.6 0.0 copy-start.6
  1.6 0.5 %collective-permute-start = (f32[2,8,128]{2,1,0:T(8,128)S(1)}, f32[2,8,128]{2,1,0:T(8,128)S(1)}, u32[]{:S(2)}, u32[]{:S(2)}) collective-permute-start(f32[2,8,128]{2,1,0:T(8,128)S(1)} %get-tuple-element.13), channel_id=1, source_target_pairs={{0,1},{1,0},{2,3},{3,2},{4,5},{5,4},{6,7},{7,6},{8,9},{9,8},{10,11... | collective-permute-start | bytes 24584 | tf_op jit(solution)/shard_map/ppermute | solution.py:170
  2.2 0.8 %collective-permute-done.refs_1_ = f32[2,8,128]{2,1,0:T(8,128)S(1)} collective-permute-done((f32[2,8,128]{2,1,0:T(8,128)S(1)}, f32[2,8,128]{2,1,0:T(8,128)S(1)}, u32[]{:S(2)}, u32[]{:S(2)}) %collective-permute-start) | collective-permute-done | bytes 8224 | tf_op jit(solution)/shard_map/ppermute | solution.py:170
  3.0 0.7 %spread.1 = f32[32,8,128]{2,1,0:T(8,128)} custom-call(f32[2,8,128]{2,1,0:T(8,128)S(1)} %get-tuple-element.12.refs_0_, f32[2,8,128]{2,1,0:T(8,128)S(1)} %collective-permute-done.refs_1_), custom_call_target="tpu_custom_call" | custom-call | tf_op jit(solution)/shard_map/spread/pallas_call | solution.py:172
  3.6 7.2 %all-to-all-start = ((f32[32,8,128]{2,1,0:T(8,128)}), f32[32,8,128]{2,1,0:T(8,128)S(1)}, u32[]{:S(2)}, u32[]{:S(2)}) async-start(f32[32,8,128]{2,1,0:T(8,128)} %spread.1), calls=%async_computation | async-start | bytes 262144 | tf_op jit(solution)/shard_map/all_to_all | solution.py:182
  10.8 0.0 copy-done.5
  10.9 0.0 copy-done
  10.9 0.0 copy-done.3
  10.9 0.9 %val_columns.1.v_ref = f32[88,512]{1,0:T(8,128)S(1)} custom-call(f32[80,4096]{1,0:T(8,128)S(1)} %copy-done, f32[1,4096]{1,0:T(1,128)S(1)} %bitcast.5, s32[1,512]{1,0:T(1,128)S(1)} %copy-done.5), custom_call_target="tpu_custom_call" | custom-call | tf_op jit(solution)/shard_map/val_columns/pallas_call | solution.py:183
  11.8 0.0 copy-start.2
  11.8 0.0 copy-done.1
  11.8 0.0 copy-done.4
  11.9 0.0 copy-done.6
  11.9 1.0 %densities.1.refs_0_ = f32[80,512]{1,0:T(8,128)S(1)} custom-call(f32[80,4096]{1,0:T(8,128)S(1)} %copy-done.1, f32[1,4096]{1,0:T(1,128)S(1)} %bitcast.6, s32[1,512]{1,0:T(1,128)S(1)} %copy-done.6, f32[88,512]{1,0:T(8,128)S(1)} %val_columns.1.v_ref), custom_call_target="tpu_custom_call" | custom-call | tf_op jit(solution)/shard_map/densities/pallas_call | solution.py:191
  12.8 0.3 %collective-permute-start.1 = (f32[80,512]{1,0:T(8,128)S(1)}, f32[80,512]{1,0:T(8,128)S(1)}, u32[]{:S(2)}, u32[]{:S(2)}) collective-permute-start(f32[80,512]{1,0:T(8,128)S(1)} %densities.1.refs_0_), channel_id=1, source_target_pairs={{0,1},{1,0},{2,3},{3,2},{4,5},{5,4},{6,7},{7,6},{8,9},{9,8},{10,11... | collective-permute-start | bytes 491528 | tf_op jit(solution)/shard_map/ppermute | solution.py:170
  13.1 1.1 %collective-permute-done.1.refs_1_ = f32[80,512]{1,0:T(8,128)S(1)} collective-permute-done((f32[80,512]{1,0:T(8,128)S(1)}, f32[80,512]{1,0:T(8,128)S(1)}, u32[]{:S(2)}, u32[]{:S(2)}) %collective-permute-start.1) | collective-permute-done | bytes 163872 | tf_op jit(solution)/shard_map/ppermute | solution.py:170
  14.3 0.2 %columns.1 = (bf16[512,160]{1,0:T(8,128)(2,1)S(1)}, bf16[512,160]{1,0:T(8,128)(2,1)S(1)}) custom-call(f32[80,512]{1,0:T(8,128)S(1)} %densities.1.refs_0_, f32[80,512]{1,0:T(8,128)S(1)} %collective-permute-done.1.refs_1_), custom_call_target="tpu_custom_call" | custom-call | tf_op jit(solution)/shard_map/columns/pallas_call | solution.py:200
  14.5 4.2 %all-to-all-done.slab_ref = f32[32,8,128]{2,1,0:T(8,128)S(1)} async-done(((f32[32,8,128]{2,1,0:T(8,128)}), f32[32,8,128]{2,1,0:T(8,128)S(1)}, u32[]{:S(2)}, u32[]{:S(2)}) %all-to-all-start) | async-done | bytes 131104 | tf_op jit(solution)/shard_map/all_to_all | solution.py:182
  18.8 0.0 copy-done.2
  18.8 0.8 %product.1 = f32[64,160]{1,0:T(8,128)} custom-call(f32[64,160]{1,0:T(8,128)S(1)} %bitcast.4, f32[32,8,128]{2,1,0:T(8,128)S(1)} %all-to-all-done.slab_ref, bf16[512,160]{1,0:T(8,128)(2,1)S(1)} %get-tuple-element.17.hi_ref, bf16[512,160]{1,0:T(8,128)(2,1)S(1)} %get-tuple-element.18.lo_ref), custom_call_target="tpu_custom_call" | custom-call | tf_op jit(solution)/shard_map/product/pallas_call | solution.py:208
Async XLA Ops:
  0.0 10.8 %copy-start.5 = (s32[1,512]{1,0:T(1,128)S(1)}, s32[1,512]{1,0:T(1,128)}, u32[]{:S(2)}) copy-start(s32[1,512]{1,0:T(1,128)} %pv_ref.2) | copy-start | bytes 6148
  0.0 10.9 %copy-start = (f32[80,4096]{1,0:T(8,128)S(1)}, f32[80,4096]{1,0:T(8,128)}, u32[]{:S(2)}) copy-start(f32[80,4096]{1,0:T(8,128)} %val_ref.3) | copy-start | bytes 3932164
  0.0 10.9 %copy-start.3 = (f32[4096]{0:T(1024)S(1)}, f32[4096]{0:T(1024)}, u32[]{:S(2)}) copy-start(f32[4096]{0:T(1024)} %param.10) | copy-start | bytes 49156
  1.6 10.2 %copy-start.1 = (f32[80,4096]{1,0:T(8,128)S(1)}, f32[80,4096]{1,0:T(8,128)}, u32[]{:S(2)}) copy-start(f32[80,4096]{1,0:T(8,128)} %cond_ref.3) | copy-start | bytes 3932164
  1.6 10.2 %copy-start.4 = (f32[4096]{0:T(1024)S(1)}, f32[4096]{0:T(1024)}, u32[]{:S(2)}) copy-start(f32[4096]{0:T(1024)} %param.11) | copy-start | bytes 49156
  1.6 10.2 %copy-start.6 = (s32[1,512]{1,0:T(1,128)S(1)}, s32[1,512]{1,0:T(1,128)}, u32[]{:S(2)}) copy-start(s32[1,512]{1,0:T(1,128)} %pc_ref.2) | copy-start | bytes 6148
  1.6 1.4 %collective-permute-start = (f32[2,8,128]{2,1,0:T(8,128)S(1)}, f32[2,8,128]{2,1,0:T(8,128)S(1)}, u32[]{:S(2)}, u32[]{:S(2)}) collective-permute-start(f32[2,8,128]{2,1,0:T(8,128)S(1)} %get-tuple-element.13), channel_id=1, source_target_pairs={{0,1},{1,0},{2,3},{3,2},{4,5},{5,4},{6,7},{7,6},{8,9},{9,8},{10,11... | collective-permute-start | bytes 24584 | tf_op jit(solution)/shard_map/ppermute | solution.py:170
  3.6 15.1 %all-to-all-start = ((f32[32,8,128]{2,1,0:T(8,128)}), f32[32,8,128]{2,1,0:T(8,128)S(1)}, u32[]{:S(2)}, u32[]{:S(2)}) async-start(f32[32,8,128]{2,1,0:T(8,128)} %spread.1), calls=%async_computation | async-start | bytes 262144 | tf_op jit(solution)/shard_map/all_to_all | solution.py:182
  11.8 6.9 %copy-start.2 = (f32[160,64]{0,1:T(8,128)S(1)}, f32[160,64]{0,1:T(8,128)}, u32[]{:S(2)}) copy-start(f32[160,64]{0,1:T(8,128)} %param.7) | copy-start | bytes 122884
  12.8 1.5 %collective-permute-start.1 = (f32[80,512]{1,0:T(8,128)S(1)}, f32[80,512]{1,0:T(8,128)S(1)}, u32[]{:S(2)}, u32[]{:S(2)}) collective-permute-start(f32[80,512]{1,0:T(8,128)S(1)} %densities.1.refs_0_), channel_id=1, source_target_pairs={{0,1},{1,0},{2,3},{3,2},{4,5},{5,4},{6,7},{7,6},{8,9},{9,8},{10,11... | collective-permute-start | bytes 491528 | tf_op jit(solution)/shard_map/ppermute | solution.py:170

commit v4 on v3

--- a/solution.py
+++ b/solution.py
@@ -43,11 +43,12 @@
     return out
 
 
-def pick_few(rows, hot, idx):
-    terms = split(by_chunk(rows, CHUNK), 3)
+def pick_few(rows, idx):
+    hot = one_hot(idx, CHUNK)
+    terms = split(by_chunk(rows, CHUNK), 2)
     m = terms[0].shape[0]
     every = jnp.dot(jnp.concatenate(terms, axis=0), hot, preferred_element_type=jnp.float32)
-    return own_chunk(every[:m] + (every[m : 2 * m] + every[2 * m :]), idx, CHUNK, rows.shape[0])
+    return own_chunk(every[:m] + every[m:], idx, CHUNK, rows.shape[0])
 
 
 def pick_many(rows, idx):
@@ -57,27 +58,33 @@
     return own_chunk(every, idx, 2 * CHUNK, rows.shape[0])
 
 
-def slab_kernel(val_ref, cond_ref, pv_ref, pc_ref, *refs):
-    *out_refs, val, cond, pv, pc, sems = refs
-    moves = ((pv_ref, pv), (pc_ref, pc), (val_ref.at[pl.ds(0, ROWS)], val), (cond_ref.at[pl.ds(0, ROWS)], cond))
+def slab_tiles(dens, out_refs):
+    n_narrow = out_refs[0].shape[0]
+    sub, share = SLAB_DEV // n_narrow, dens.shape[1] // len(out_refs)
+    for n, out_ref in enumerate(out_refs):
+        for to in range(n_narrow):
+            out_ref[to] = by_chunk(dens[to * sub : (to + 1) * sub, n * share : (n + 1) * share], LANES)
+
+
+def others_kernel(val_ref, cond_ref, pv_ref, pc_ref, val, cond, pv, pc, *refs):
+    *out_refs, sems = refs
+    moves = ((val_ref.at[pl.ds(0, ROWS)], val), (pv_ref, pv), (cond_ref.at[pl.ds(0, ROWS)], cond), (pc_ref, pc))
     copies = [pltpu.make_async_copy(src, dst, sems.at[i]) for i, (src, dst) in enumerate(moves)]
     for copy in copies:
         copy.start()
+    own = pv.shape[1] // (len(out_refs) + 1)
+    copies[1].wait()
     copies[0].wait()
-    pv = pv[...]
-    hot_v = one_hot(pv, CHUNK)
-    copies[1].wait()
-    pc = pc[...]
-    hot_c = one_hot(pc, CHUNK)
+    dens = pick_few(val[...], pv[:, own:])
+    copies[3].wait()
     copies[2].wait()
-    dens = pick_few(val[...], hot_v, pv)
-    copies[3].wait()
-    dens = dens * pick_few(cond[...], hot_c, pc)
-    n_narrow = len(out_refs)
-    sub, share = SLAB_DEV // n_narrow, dens.shape[1] // n_narrow
-    for n, out_ref in enumerate(out_refs):
-        for to in range(n_narrow):
-            out_ref[to] = by_chunk(dens[to * sub : (to + 1) * sub, n * share : (n + 1) * share], LANES)
+    slab_tiles(dens * pick_few(cond[...], pc[:, own:]), out_refs)
+
+
+def own_kernel(val_ref, cond_ref, pv_ref, pc_ref, out_ref):
+    own = pv_ref.shape[1] // out_ref.shape[0]
+    dens = pick_few(val_ref[...], pv_ref[:, :own]) * pick_few(cond_ref[...], pc_ref[:, :own])
+    slab_tiles(dens, [out_ref])
 
 
 def spread_kernel(*refs):
@@ -88,22 +95,27 @@
     for n in range(1, n_narrow):
         share[0] = jnp.where(narrow == n, share[n], share[0])
     for place in range(out_ref.shape[0]):
-        out_ref[out_ref.shape[0] - 1 - place] = share[0][place % n_narrow]
-
-
-def with_energy(orb_ref, e_ref):
-    return jnp.concatenate([orb_ref[...], jnp.broadcast_to(e_ref[...], (ROWS, e_ref.shape[1]))], axis=0)
-
-
-def val_kernel(val_ref, ev_ref, pv_ref, out_ref):
-    out_ref[...] = pick_many(with_energy(val_ref, ev_ref), pv_ref[...])
-
-
-def dens_kernel(cond_ref, ec_ref, pc_ref, v_ref, out_ref):
+        out_ref[place] = share[0][place % n_narrow]
+
+
+def with_energy(orb, e):
+    return jnp.concatenate([orb[...], jnp.broadcast_to(e[...], (ROWS, e.shape[1]))], axis=0)
+
+
+def dens_kernel(val_ref, cond_ref, ev_ref, ec_ref, pv_ref, pc_ref, out_ref, val, cond, ev, ec, pv, pc, sems):
+    moves = ((val_ref, val), (ev_ref, ev), (pv_ref, pv), (cond_ref, cond), (ec_ref, ec), (pc_ref, pc))
+    copies = [pltpu.make_async_copy(src, dst, sems.at[i]) for i, (src, dst) in enumerate(moves)]
+    for copy in copies:
+        copy.start()
     r = out_ref.shape[0]
-    c = pick_many(with_energy(cond_ref, ec_ref), pc_ref[...])
-    weight = 1.0 / (c[r : r + 1] - v_ref[r : r + 1])
-    out_ref[...] = v_ref[:r] * c[:r] * weight
+    for copy in copies[:3]:
+        copy.wait()
+    v = pick_many(with_energy(val, ev), pv[...])
+    for copy in copies[3:]:
+        copy.wait()
+    c = pick_many(with_energy(cond, ec), pc[...])
+    weight = 1.0 / (c[r : r + 1] - v[r : r + 1])
+    out_ref[...] = v[:r] * c[:r] * weight
 
 
 def by_source(parts, me):
@@ -126,7 +138,7 @@
     lanes, blocks = [], slab_ref.shape[0]
     for n in range(n_narrow):
         for at in range(0, slab_ref.shape[1], sub):
-            lanes.append([slab_ref[blocks - 1 - w, at : at + sub] for w in range(n, blocks, n_narrow)])
+            lanes.append([slab_ref[w, at : at + sub] for w in range(n, blocks, n_narrow)])
     slab = jnp.concatenate([jnp.concatenate(rows, axis=0) for rows in lanes], axis=1)
     s_hi, s_lo = split(slab, 2)
     m = slab.shape[0]
@@ -147,24 +159,26 @@
     vmem = pl.BlockSpec(memory_space=pltpu.VMEM)
     hbm = pl.BlockSpec(memory_space=pltpu.HBM)
     share = jax.ShapeDtypeStruct((n_narrow, tile_rows, LANES), jnp.float32)
-    mine = pl.pallas_call(
-        slab_kernel,
+    rows_type = jax.ShapeDtypeStruct((ROWS, bands), jnp.float32)
+    pairs_type = jax.ShapeDtypeStruct((1, pairs), jnp.int32)
+    first = pl.pallas_call(
+        others_kernel,
         in_specs=[hbm] * 4,
-        out_specs=[vmem] * n_narrow,
-        out_shape=[share] * n_narrow,
-        scratch_shapes=[
-            pltpu.VMEM((ROWS, bands), jnp.float32),
-            pltpu.VMEM((ROWS, bands), jnp.float32),
-            pltpu.VMEM((1, pairs), jnp.int32),
-            pltpu.VMEM((1, pairs), jnp.int32),
-            pltpu.SemaphoreType.DMA((4,)),
-        ],
-        compiler_params=params(16),
-        name="slab_rows",
+        out_specs=[vmem] * (3 + n_narrow),
+        out_shape=[rows_type, rows_type, pairs_type, pairs_type] + [share] * (n_narrow - 1),
+        scratch_shapes=[pltpu.SemaphoreType.DMA((4,))],
+        compiler_params=params(16),
+        name="slab_rows_others",
     )(*(in_hbm(x) for x in (val_orb, cond_orb, pair_val, pair_cond)))
-
-    def exchange(x, axis, bit):
-        return lax.ppermute(x, axis, [(i, i ^ bit) for i in range(lax.axis_size(axis))])
+    kept, others = first[:4], first[4:]
+    own_share = pl.pallas_call(
+        own_kernel,
+        in_specs=[vmem] * 4,
+        out_specs=vmem,
+        out_shape=share,
+        compiler_params=params(16),
+        name="slab_rows_own",
+    )(*kept)
 
     def exchange(x, bit):
         return lax.ppermute(x, "narrow", [(i, i ^ bit) for i in range(n_narrow)])
@@ -176,26 +190,19 @@
         out_shape=jax.ShapeDtypeStruct((n_wide * n_narrow, tile_rows, LANES), jnp.float32),
         compiler_params=params(16),
         name="spread",
-    )(mine[0], *(exchange(mine[n], n) for n in range(1, n_narrow)))
+    )(own_share, *(exchange(x, n) for n, x in enumerate(others, 1)))
     pair_val, pair_cond, parts = lax.optimization_barrier((pair_val, pair_cond, parts))
-    last_first = [list(range(n_wide * n_narrow))[::-1]]
-    slab = lax.all_to_all(parts, ("wide", "narrow"), 0, 0, axis_index_groups=last_first, tiled=True)
-    v = pl.pallas_call(
-        val_kernel,
-        in_specs=[vmem] * 3,
-        out_specs=vmem,
-        out_shape=jax.ShapeDtypeStruct((rows + ROWS, pairs), jnp.float32),
-        compiler_params=params(24),
-        name="val_columns",
-    )(val_orb, e_val[None, :], pair_val)
+    slab = lax.all_to_all(parts, ("wide", "narrow"), 0, 0, tiled=True)
+    operands = [val_orb, cond_orb, e_val[None, :], e_cond[None, :], pair_val, pair_cond]
     own = pl.pallas_call(
         dens_kernel,
-        in_specs=[vmem] * 4,
+        in_specs=[hbm] * len(operands),
         out_specs=vmem,
         out_shape=jax.ShapeDtypeStruct((rows, pairs), jnp.float32),
-        compiler_params=params(24),
+        scratch_shapes=[pltpu.VMEM(x.shape, x.dtype) for x in operands] + [pltpu.SemaphoreType.DMA((len(operands),))],
+        compiler_params=params(32),
         name="densities",
-    )(cond_orb, e_cond[None, :], pair_cond, v)
+    )(*(in_hbm(x) for x in operands))
     columns = [own] + [exchange(own, n) for n in range(1, n_narrow)]
     terms = pl.pallas_call(
         columns_kernel,

time: 19.8 us -> 19.9 us (level)
  Pallas kernels: 5.21 us -> 6.69 us
  waiting for transfers between devices: 6.21 us -> 4.9 us
    pallas_call x3, Pallas kernels: 3.49 us -> 4.97 us  [the longest x1 3.36 us: shards(): pl.pallas_call(dens_kernel, in_specs=[hbm] * len(operands), out_specs=vme...]
    all_to_all x1, waiting for transfers between devices: 4.24 us -> 3.17 us  [shards(): slab = lax.all_to_all(parts, ('wide', 'narrow'), 0, 0, tiled=True)]
    ppermute x2, waiting for transfers between devices: 1.97 us -> 1.73 us  [exchange(): return lax.ppermute(x, 'narrow', [(i, i ^ bit) for i in range(n_narrow)])]
  transfers between devices with their start and end apart: 3 -> 3, of which waited for: 3 -> 3; matrix products, arithmetic and copies ran while one was open for 0% -> 0% of each run, Pallas kernels for 11% -> 19%
where the time goes in v4:
time: 19.9 us; the launch traced here: 19.7 us
  starting transfers between devices  8.02 us (40%)
  Pallas kernels  6.69 us (34%)
  waiting for transfers between devices  4.9 us (25%)
    all_to_all x1, starting transfers between devices, shards(): slab = lax.all_to_all(parts, ('wide', 'narrow'), 0, 0, tiled=True)  7.19 us
    pallas_call x1, Pallas kernels, shards(): pl.pallas_call(dens_kernel, in_specs=[hbm] * len(operands), out_specs=vme...  3.36 us
    all_to_all x1, waiting for transfers between devices, shards(): slab = lax.all_to_all(parts, ('wide', 'narrow'), 0, 0, tiled=True)  3.17 us
    ppermute x2, waiting for transfers between devices, exchange(): return lax.ppermute(x, 'narrow', [(i, i ^ bit) for i in range(n_narrow)])  1.73 us
    pallas_call x1, Pallas kernels, shards(): pl.pallas_call(others_kernel, in_specs=[hbm] * 4, out_specs=[vmem] * (3 +...  1.38 us
    pallas_call x1, Pallas kernels, shards(): pl.pallas_call(functools.partial(product_kernel, n_narrow), in_specs=[vme...  0.85 us
    ppermute x2, starting transfers between devices, exchange(): return lax.ppermute(x, 'narrow', [(i, i ^ bit) for i in range(n_narrow)])  0.83 us
    pallas_call x1, Pallas kernels, shards(): pl.pallas_call(spread_kernel, in_specs=[vmem] * n_narrow, out_specs=vmem,...  0.66 us
  transfers between devices with their start and end apart: 3, of which 3 were waited for; matrix products, arithmetic and copies ran while one was open for 0% of the time, Pallas kernels for 19%

profile of v4, /device:TPU:0, one launch (start us, length us, event | category | flops | bytes accessed | tf_op | source)
XLA Modules:
  0.0 19.7 jit_solution(5012259021002780824)
XLA Ops:
  0.0 1.4 %slab_rows_others.1 = (f32[8,4096]{1,0:T(8,128)S(1)}, f32[8,4096]{1,0:T(8,128)S(1)}, s32[1,512]{1,0:T(1,128)S(1)}, s32[1,512]{1,0:T(1,128)S(1)}, f32[2,8,128]{2,1,0:T(8,128)S(1)}) custom-call(f32[80,4096]{1,0:T(8,128)} %val_ref.3, f32[80,4096]{1,0:T(8,128)} %cond_ref.3, s32[1,512]{1,0:T(1,128)} %pv_ref.2, s32[1,512]{1,0:T(1,128)} %pc_ref.2), custom_call_target="tpu_custom_call" | custom-call | tf_op jit(solution)/shard_map/slab_rows_others/pallas_call | solution.py:164
  1.4 0.5 %collective-permute-start = (f32[2,8,128]{2,1,0:T(8,128)S(1)}, f32[2,8,128]{2,1,0:T(8,128)S(1)}, u32[]{:S(2)}, u32[]{:S(2)}) collective-permute-start(f32[2,8,128]{2,1,0:T(8,128)S(1)} %get-tuple-element.19), channel_id=1, source_target_pairs={{0,1},{1,0},{2,3},{3,2},{4,5},{5,4},{6,7},{7,6},{8,9},{9,8},{10,11... | collective-permute-start | bytes 24584 | tf_op jit(solution)/shard_map/ppermute | solution.py:184
  1.9 0.2 %slab_rows_own.1.refs_0_ = f32[2,8,128]{2,1,0:T(8,128)S(1)} custom-call(f32[8,4096]{1,0:T(8,128)S(1)} %get-tuple-element.15.val_ref, f32[8,4096]{1,0:T(8,128)S(1)} %get-tuple-element.16.cond_ref, s32[1,512]{1,0:T(1,128)S(1)} %get-tuple-element.17.pv_ref, s32[1,512]{1,0:T(1,128)S(1)} %get-tuple-element.18.pc_ref), custom_call_target="tpu_custom_call" | custom-call | tf_op jit(solution)/shard_map/slab_rows_own/pallas_call | solution.py:174
  2.1 0.6 %collective-permute-done.refs_1_ = f32[2,8,128]{2,1,0:T(8,128)S(1)} collective-permute-done((f32[2,8,128]{2,1,0:T(8,128)S(1)}, f32[2,8,128]{2,1,0:T(8,128)S(1)}, u32[]{:S(2)}, u32[]{:S(2)}) %collective-permute-start) | collective-permute-done | bytes 8224 | tf_op jit(solution)/shard_map/ppermute | solution.py:184
  2.7 0.7 %spread.1 = f32[32,8,128]{2,1,0:T(8,128)} custom-call(f32[2,8,128]{2,1,0:T(8,128)S(1)} %slab_rows_own.1.refs_0_, f32[2,8,128]{2,1,0:T(8,128)S(1)} %collective-permute-done.refs_1_), custom_call_target="tpu_custom_call" | custom-call | tf_op jit(solution)/shard_map/spread/pallas_call | solution.py:186
  3.4 7.2 %all-to-all-start = ((f32[32,8,128]{2,1,0:T(8,128)}), f32[32,8,128]{2,1,0:T(8,128)S(1)}, u32[]{:S(2)}, u32[]{:S(2)}) async-start(f32[32,8,128]{2,1,0:T(8,128)} %spread.1), calls=%async_computation | async-start | bytes 262144 | tf_op jit(solution)/shard_map/all_to_all | solution.py:195
  10.6 0.0 copy-start
  10.6 3.4 %densities.1.refs_0_ = f32[80,512]{1,0:T(8,128)S(1)} custom-call(f32[80,4096]{1,0:T(8,128)} %val_ref.3, f32[80,4096]{1,0:T(8,128)} %cond_ref.3, f32[1,4096]{1,0:T(1,128)} %bitcast.5, f32[1,4096]{1,0:T(1,128)} %bitcast.6, s32[1,512]{1,0:T(1,128)} %pv_ref.2, s32[1,512]{1,0:T(1,128)} %pc_ref.2), custom_call_target="tpu_custom_call" | custom-call | tf_op jit(solution)/shard_map/densities/pallas_call | solution.py:197
  14.0 0.3 %collective-permute-start.1 = (f32[80,512]{1,0:T(8,128)S(1)}, f32[80,512]{1,0:T(8,128)S(1)}, u32[]{:S(2)}, u32[]{:S(2)}) collective-permute-start(f32[80,512]{1,0:T(8,128)S(1)} %densities.1.refs_0_), channel_id=1, source_target_pairs={{0,1},{1,0},{2,3},{3,2},{4,5},{5,4},{6,7},{7,6},{8,9},{9,8},{10,11... | collective-permute-start | bytes 491528 | tf_op jit(solution)/shard_map/ppermute | solution.py:184
  14.3 1.1 %collective-permute-done.1.refs_1_ = f32[80,512]{1,0:T(8,128)S(1)} collective-permute-done((f32[80,512]{1,0:T(8,128)S(1)}, f32[80,512]{1,0:T(8,128)S(1)}, u32[]{:S(2)}, u32[]{:S(2)}) %collective-permute-start.1) | collective-permute-done | bytes 163872 | tf_op jit(solution)/shard_map/ppermute | solution.py:184
  15.4 0.2 %columns.1 = (bf16[512,160]{1,0:T(8,128)(2,1)S(1)}, bf16[512,160]{1,0:T(8,128)(2,1)S(1)}) custom-call(f32[80,512]{1,0:T(8,128)S(1)} %densities.1.refs_0_, f32[80,512]{1,0:T(8,128)S(1)} %collective-permute-done.1.refs_1_), custom_call_target="tpu_custom_call" | custom-call | tf_op jit(solution)/shard_map/columns/pallas_call | solution.py:207
  15.6 3.2 %all-to-all-done.slab_ref = f32[32,8,128]{2,1,0:T(8,128)S(1)} async-done(((f32[32,8,128]{2,1,0:T(8,128)}), f32[32,8,128]{2,1,0:T(8,128)S(1)}, u32[]{:S(2)}, u32[]{:S(2)}) %all-to-all-start) | async-done | bytes 131104 | tf_op jit(solution)/shard_map/all_to_all | solution.py:195
  18.8 0.0 copy-done
  18.8 0.8 %product.1 = f32[64,160]{1,0:T(8,128)} custom-call(f32[64,160]{1,0:T(8,128)S(1)} %bitcast.4, f32[32,8,128]{2,1,0:T(8,128)S(1)} %all-to-all-done.slab_ref, bf16[512,160]{1,0:T(8,128)(2,1)S(1)} %get-tuple-element.23.hi_ref, bf16[512,160]{1,0:T(8,128)(2,1)S(1)} %get-tuple-element.24.lo_ref), custom_call_target="tpu_custom_call" | custom-call | tf_op jit(solution)/shard_map/product/pallas_call | solution.py:215
Async XLA Ops:
  1.4 1.3 %collective-permute-start = (f32[2,8,128]{2,1,0:T(8,128)S(1)}, f32[2,8,128]{2,1,0:T(8,128)S(1)}, u32[]{:S(2)}, u32[]{:S(2)}) collective-permute-start(f32[2,8,128]{2,1,0:T(8,128)S(1)} %get-tuple-element.19), channel_id=1, source_target_pairs={{0,1},{1,0},{2,3},{3,2},{4,5},{5,4},{6,7},{7,6},{8,9},{9,8},{10,11... | collective-permute-start | bytes 24584 | tf_op jit(solution)/shard_map/ppermute | solution.py:184
  3.4 15.4 %all-to-all-start = ((f32[32,8,128]{2,1,0:T(8,128)}), f32[32,8,128]{2,1,0:T(8,128)S(1)}, u32[]{:S(2)}, u32[]{:S(2)}) async-start(f32[32,8,128]{2,1,0:T(8,128)} %spread.1), calls=%async_computation | async-start | bytes 262144 | tf_op jit(solution)/shard_map/all_to_all | solution.py:195
  10.6 8.2 %copy-start = (f32[160,64]{0,1:T(8,128)S(1)}, f32[160,64]{0,1:T(8,128)}, u32[]{:S(2)}) copy-start(f32[160,64]{0,1:T(8,128)} %param.7) | copy-start | bytes 122884
  14.0 1.5 %collective-permute-start.1 = (f32[80,512]{1,0:T(8,128)S(1)}, f32[80,512]{1,0:T(8,128)S(1)}, u32[]{:S(2)}, u32[]{:S(2)}) collective-permute-start(f32[80,512]{1,0:T(8,128)S(1)} %densities.1.refs_0_), channel_id=1, source_target_pairs={{0,1},{1,0},{2,3},{3,2},{4,5},{5,4},{6,7},{7,6},{8,9},{9,8},{10,11... | collective-permute-start | bytes 491528 | tf_op jit(solution)/shard_map/ppermute | solution.py:184

commit v5 on v2

--- a/solution.py
+++ b/solution.py
@@ -9,7 +9,8 @@
 
 SLAB_DEV = 8
 ROWS = 8
-LANES = 128
+RADIX = 4
+ORDER = (0, 2, 3, 1)
 CHUNK = 256
 MIB = 1 << 20
 
@@ -43,11 +44,12 @@
     return out
 
 
-def pick_few(rows, hot, idx):
-    terms = split(by_chunk(rows, CHUNK), 3)
+def pick_few(rows, idx):
+    hot = one_hot(idx, CHUNK)
+    terms = split(by_chunk(rows, CHUNK), 2)
     m = terms[0].shape[0]
     every = jnp.dot(jnp.concatenate(terms, axis=0), hot, preferred_element_type=jnp.float32)
-    return own_chunk(every[:m] + (every[m : 2 * m] + every[2 * m :]), idx, CHUNK, rows.shape[0])
+    return own_chunk(every[:m] + every[m:], idx, CHUNK, rows.shape[0])
 
 
 def pick_many(rows, idx):
@@ -57,38 +59,20 @@
     return own_chunk(every, idx, 2 * CHUNK, rows.shape[0])
 
 
-def slab_kernel(val_ref, cond_ref, pv_ref, pc_ref, *refs):
-    *out_refs, val, cond, pv, pc, sems = refs
-    moves = ((pv_ref, pv), (pc_ref, pc), (val_ref.at[pl.ds(0, ROWS)], val), (cond_ref.at[pl.ds(0, ROWS)], cond))
+def slab_kernel(val_ref, cond_ref, pv_ref, pc_ref, out_ref, val, cond, pv, pc, sems):
+    moves = ((val_ref.at[pl.ds(0, ROWS)], val), (pv_ref, pv), (cond_ref.at[pl.ds(0, ROWS)], cond), (pc_ref, pc))
     copies = [pltpu.make_async_copy(src, dst, sems.at[i]) for i, (src, dst) in enumerate(moves)]
     for copy in copies:
         copy.start()
+    copies[1].wait()
     copies[0].wait()
-    pv = pv[...]
-    hot_v = one_hot(pv, CHUNK)
-    copies[1].wait()
-    pc = pc[...]
-    hot_c = one_hot(pc, CHUNK)
+    dens = pick_few(val[...], pv[...])
+    copies[3].wait()
     copies[2].wait()
-    dens = pick_few(val[...], hot_v, pv)
-    copies[3].wait()
-    dens = dens * pick_few(cond[...], hot_c, pc)
-    n_narrow = len(out_refs)
-    sub, share = SLAB_DEV // n_narrow, dens.shape[1] // n_narrow
-    for n, out_ref in enumerate(out_refs):
-        for to in range(n_narrow):
-            out_ref[to] = by_chunk(dens[to * sub : (to + 1) * sub, n * share : (n + 1) * share], LANES)
-
-
-def spread_kernel(*refs):
-    *share_refs, out_ref = refs
-    narrow = lax.axis_index("narrow")
-    n_narrow = len(share_refs)
-    share = [ref[...] for ref in share_refs]
-    for n in range(1, n_narrow):
-        share[0] = jnp.where(narrow == n, share[n], share[0])
-    for place in range(out_ref.shape[0]):
-        out_ref[place] = share[0][place % n_narrow]
+    dens = dens * pick_few(cond[...], pc[...])
+    sub = out_ref.shape[1]
+    for n in range(out_ref.shape[0]):
+        out_ref[n] = dens[n * sub : (n + 1) * sub]
 
 
 def with_energy(orb_ref, e_ref):
@@ -121,18 +105,17 @@
     hi_ref[...], lo_ref[...] = split(jnp.concatenate(cols, axis=0).T, 2)
 
 
-def product_kernel(n_narrow, chi_ref, slab_ref, hi_ref, lo_ref, out_ref):
-    sub = SLAB_DEV // n_narrow
-    lanes = []
-    for n in range(n_narrow):
-        for at in range(0, slab_ref.shape[1], sub):
-            lanes.append([slab_ref[w, at : at + sub] for w in range(n, slab_ref.shape[0], n_narrow)])
-    slab = jnp.concatenate([jnp.concatenate(rows, axis=0) for rows in lanes], axis=1)
-    s_hi, s_lo = split(slab, 2)
-    m = slab.shape[0]
+def product_kernel(strides, sub, chi_ref, hi_ref, lo_ref, *refs):
+    *rows_refs, out_ref = refs
+    s_hi, s_lo = split(jnp.concatenate([ref[...] for ref in rows_refs], axis=0), 2)
+    m = s_hi.shape[0]
     by_hi = jnp.dot(jnp.concatenate([s_hi, s_lo], axis=0), hi_ref[...], preferred_element_type=jnp.float32)
     by_lo = jnp.dot(s_hi, lo_ref[...], preferred_element_type=jnp.float32)
-    out_ref[...] = chi_ref[...] + (by_hi[:m] + (by_hi[m:] + by_lo))
+    total = by_hi[:m] + (by_hi[m:] + by_lo)
+    blocks = m // sub
+    held = {sum(s * ORDER[j // RADIX**i % RADIX] for i, s in enumerate(strides)): j for j in range(blocks)}
+    parts = [total[held[x] * sub : (held[x] + 1) * sub] for x in range(blocks)]
+    out_ref[...] = chi_ref[...] + jnp.concatenate(by_source(parts, lax.axis_index("wide")), axis=0)
 
 
 def in_hbm(x):
@@ -143,15 +126,13 @@
     n_wide, n_narrow = lax.axis_size("wide"), lax.axis_size("narrow")
     row_sub = SLAB_DEV // n_narrow
     pairs, rows, bands = pair_val.shape[1], val_orb.shape[0], val_orb.shape[1]
-    tile_rows = row_sub * (pairs // n_narrow // LANES)
     vmem = pl.BlockSpec(memory_space=pltpu.VMEM)
     hbm = pl.BlockSpec(memory_space=pltpu.HBM)
-    share = jax.ShapeDtypeStruct((n_narrow, tile_rows, LANES), jnp.float32)
     mine = pl.pallas_call(
         slab_kernel,
         in_specs=[hbm] * 4,
-        out_specs=[vmem] * n_narrow,
-        out_shape=[share] * n_narrow,
+        out_specs=vmem,
+        out_shape=jax.ShapeDtypeStruct((n_narrow, row_sub, pairs), jnp.float32),
         scratch_shapes=[
             pltpu.VMEM((ROWS, bands), jnp.float32),
             pltpu.VMEM((ROWS, bands), jnp.float32),
@@ -163,22 +144,26 @@
         name="slab_rows",
     )(*(in_hbm(x) for x in (val_orb, cond_orb, pair_val, pair_cond)))
 
-    def exchange(x, axis, bit):
-        return lax.ppermute(x, axis, [(i, i ^ bit) for i in range(lax.axis_size(axis))])
-
     def exchange(x, bit):
         return lax.ppermute(x, "narrow", [(i, i ^ bit) for i in range(n_narrow)])
 
-    parts = pl.pallas_call(
-        spread_kernel,
-        in_specs=[vmem] * n_narrow,
-        out_specs=vmem,
-        out_shape=pltpu.VMEM((n_wide * n_narrow, tile_rows, LANES), jnp.float32),
-        compiler_params=params(4),
-        name="spread",
-    )(mine[0], *(exchange(mine[n], n) for n in range(1, n_narrow)))
-    pair_val, pair_cond, parts = lax.optimization_barrier((pair_val, pair_cond, parts))
-    slab = lax.all_to_all(parts, ("wide", "narrow"), 0, 0, tiled=True)
+    across = n_narrow - 1
+
+    def between_chips(x, bit):
+        pairs_of = [(w * n_narrow + n, (w ^ bit) * n_narrow + n ^ across) for w in range(n_wide) for n in range(n_narrow)]
+        return lax.ppermute(x, ("wide", "narrow"), pairs_of)
+
+    strides = []
+    while RADIX ** (len(strides) + 1) <= n_wide:
+        strides.append(n_wide // RADIX ** (len(strides) + 1))
+    start = across if len(strides) % 2 else 0
+    narrow = lax.axis_index("narrow")
+    sent, own_block = mine[start], mine[start ^ across]
+    for n in range(1, n_narrow):
+        got = exchange(mine, n)
+        sent = jnp.where(narrow == n, got[n ^ start], sent)
+        own_block = jnp.where(narrow == n, got[n ^ start ^ across], own_block)
+    pair_val, pair_cond, sent = lax.optimization_barrier((pair_val, pair_cond, sent))
     v = pl.pallas_call(
         val_kernel,
         in_specs=[vmem] * 3,
@@ -195,6 +180,14 @@
         compiler_params=params(24),
         name="densities",
     )(cond_orb, e_cond[None, :], pair_cond, v)
+    got = [sent]
+    for stride in strides:
+        if stride == strides[0]:
+            got = [own_block] + [between_chips(sent, d * stride) for d in ORDER[1:]]
+            *got, own = lax.optimization_barrier((*got, own))
+        else:
+            sent = jnp.concatenate(got, axis=0)
+            got = [exchange(sent, across)] + [between_chips(sent, d * stride) for d in ORDER[1:]]
     columns = [own] + [exchange(own, n) for n in range(1, n_narrow)]
     terms = pl.pallas_call(
         columns_kernel,
@@ -205,13 +198,13 @@
         name="columns",
     )(*columns)
     out = pl.pallas_call(
-        functools.partial(product_kernel, n_narrow),
-        in_specs=[vmem] * 4,
+        functools.partial(product_kernel, tuple(strides), row_sub),
+        in_specs=[vmem] * (3 + len(got)),
         out_specs=vmem,
         out_shape=jax.ShapeDtypeStruct(chi_in.shape[::-1], jnp.float32),
         compiler_params=params(16),
         name="product",
-    )(chi_in.T, slab, *terms)
+    )(chi_in.T, *terms, *got)
     return out.T
 
 

time: 20.1 us -> 19.1 us (0.950)
  waiting for transfers between devices: 6.53 us -> 4.83 us
  starting transfers between devices: 8.02 us -> 9.48 us
  Pallas kernels: 5.21 us -> 4.5 us
    ppermute x0 -> x6, starting transfers between devices: none -> 8.39 us  [between_chips(): return lax.ppermute(x, ('wide', 'narrow'), pairs_of)]
    all_to_all x1 -> x0, starting transfers between devices: 7.18 us -> none  [shards(): slab = lax.all_to_all(parts, ('wide', 'narrow'), 0, 0, tiled=True)]
    all_to_all x1 -> x0, waiting for transfers between devices: 4.56 us -> none  [shards(): slab = lax.all_to_all(parts, ('wide', 'narrow'), 0, 0, tiled=True)]
    ppermute x0 -> x6, waiting for transfers between devices: none -> 3.99 us  [between_chips(): return lax.ppermute(x, ('wide', 'narrow'), pairs_of)]
    ppermute x2 -> x3, waiting for transfers between devices: 1.97 us -> 0.84 us  [exchange(): return lax.ppermute(x, 'narrow', [(i, i ^ bit) for i in range(n_narrow)])]
    pallas_call x3 -> x2, Pallas kernels: 3.09 us -> 2.39 us  [the longest x1 1.52 us: shards(): pl.pallas_call(slab_kernel, in_specs=[hbm] * 4, out_specs=vmem, out_shape...]
    ppermute x2 -> x3, starting transfers between devices: 0.84 us -> 1.1 us  [exchange(): return lax.ppermute(x, 'narrow', [(i, i ^ bit) for i in range(n_narrow)])]
  transfers between devices with their start and end apart: 3 -> 9, of which waited for: 3 -> 4; matrix products, arithmetic and copies ran while one was open for 0% -> 0% of each run, Pallas kernels for 11% -> 11%
where the time goes in v5:
time: 19.1 us; the launch traced here: 19 us
  starting transfers between devices  9.48 us (50%)
  waiting for transfers between devices  4.83 us (25%)
  Pallas kernels  4.5 us (24%)
    ppermute x6, starting transfers between devices, between_chips(): return lax.ppermute(x, ('wide', 'narrow'), pairs_of)  8.39 us
    ppermute x6, waiting for transfers between devices, between_chips(): return lax.ppermute(x, ('wide', 'narrow'), pairs_of)  3.99 us
    pallas_call x1, Pallas kernels, shards(): pl.pallas_call(slab_kernel, in_specs=[hbm] * 4, out_specs=vmem, out_shape...  1.52 us
    ppermute x3, starting transfers between devices, exchange(): return lax.ppermute(x, 'narrow', [(i, i ^ bit) for i in range(n_narrow)])  1.1 us
    pallas_call x1, Pallas kernels, shards(): pl.pallas_call(dens_kernel, in_specs=[vmem] * 4, out_specs=vmem, out_shap...  0.96 us
    pallas_call x1, Pallas kernels, shards(): pl.pallas_call(val_kernel, in_specs=[vmem] * 3, out_specs=vmem, out_shape...  0.94 us
    pallas_call x1, Pallas kernels, shards(): pl.pallas_call(functools.partial(product_kernel, tuple(strides), row_sub)...  0.87 us
    ppermute x3, waiting for transfers between devices, exchange(): return lax.ppermute(x, 'narrow', [(i, i ^ bit) for i in range(n_narrow)])  0.84 us
  transfers between devices with their start and end apart: 9, of which 4 were waited for; matrix products, arithmetic and copies ran while one was open for 0% of the time, Pallas kernels for 11%

profile of v5, /device:TPU:0, one launch (start us, length us, event | category | flops | bytes accessed | tf_op | source)
XLA Modules:
  0.0 19.0 jit_solution(17842553117456486435)
XLA Ops:
  0.0 0.0 copy-start
  0.0 0.0 copy-start.5
  0.0 0.0 copy-start.3
  0.0 1.5 %slab_rows.1 = f32[2,4,512]{2,1,0:T(4,128)S(1)} custom-call(f32[80,4096]{1,0:T(8,128)} %val_ref.3, f32[80,4096]{1,0:T(8,128)} %cond_ref.3, s32[1,512]{1,0:T(1,128)} %pv_ref.2, s32[1,512]{1,0:T(1,128)} %pc_ref.2), custom_call_target="tpu_custom_call" | custom-call | tf_op jit(solution)/shard_map/slab_rows/pallas_call | solution.py:131
  1.5 0.0 copy-start.1
  1.5 0.0 copy-start.4
  1.6 0.0 copy-start.6
  1.6 0.5 %collective-permute-start = (f32[2,4,512]{2,1,0:T(4,128)S(1)}, f32[2,4,512]{2,1,0:T(4,128)S(1)}, u32[]{:S(2)}, u32[]{:S(2)}) collective-permute-start(f32[2,4,512]{2,1,0:T(4,128)S(1)} %slab_rows.1), channel_id=1, source_target_pairs={{0,1},{1,0},{2,3},{3,2},{4,5},{5,4},{6,7},{7,6},{8,9},{9,8},{10,11... | collective-permute-start | bytes 49160 | tf_op jit(solution)/shard_map/ppermute | solution.py:148
  2.1 0.8 %collective-permute-done = f32[2,4,512]{2,1,0:T(4,128)S(1)} collective-permute-done((f32[2,4,512]{2,1,0:T(4,128)S(1)}, f32[2,4,512]{2,1,0:T(4,128)S(1)}, u32[]{:S(2)}, u32[]{:S(2)}) %collective-permute-start) | collective-permute-done | bytes 16416 | tf_op jit(solution)/shard_map/ppermute | solution.py:148
  2.9 3.7 %collective-permute-start.1 = (f32[4,512]{1,0:T(4,128)S(1)}, f32[4,512]{1,0:T(4,128)S(1)}, u32[]{:S(2)}, u32[]{:S(2)}) collective-permute-start(f32[4,512]{1,0:T(4,128)S(1)} %get-tuple-element.15), channel_id=1, source_target_pairs={{0,17},{1,16},{2,19},{3,18},{4,21},{5,20},{6,23},{7,22},{8,25},{9,... | collective-permute-start | bytes 24584 | tf_op jit(solution)/shard_map/ppermute | solution.py:154
  6.6 1.3 %collective-permute-start.2 = (f32[4,512]{1,0:T(4,128)S(1)}, f32[4,512]{1,0:T(4,128)S(1)}, u32[]{:S(2)}, u32[]{:S(2)}) collective-permute-start(f32[4,512]{1,0:T(4,128)S(1)} %get-tuple-element.15), channel_id=1, source_target_pairs={{0,25},{1,24},{2,27},{3,26},{4,29},{5,28},{6,31},{7,30},{8,17},{9,... | collective-permute-start | bytes 24584 | tf_op jit(solution)/shard_map/ppermute | solution.py:154
  7.9 0.2 %collective-permute-start.3 = (f32[4,512]{1,0:T(4,128)S(1)}, f32[4,512]{1,0:T(4,128)S(1)}, u32[]{:S(2)}, u32[]{:S(2)}) collective-permute-start(f32[4,512]{1,0:T(4,128)S(1)} %get-tuple-element.15), channel_id=1, source_target_pairs={{0,9},{1,8},{2,11},{3,10},{4,13},{5,12},{6,15},{7,14},{8,1},{9,0},... | collective-permute-start | bytes 24584 | tf_op jit(solution)/shard_map/ppermute | solution.py:154
  8.2 0.0 copy-done
  8.2 0.0 copy-done.5
  8.2 0.0 copy-done.3
  8.2 0.9 %val_columns.1.v_ref = f32[88,512]{1,0:T(8,128)S(1)} custom-call(f32[80,4096]{1,0:T(8,128)S(1)} %copy-done, f32[1,4096]{1,0:T(1,128)S(1)} %bitcast.9, s32[1,512]{1,0:T(1,128)S(1)} %copy-done.5), custom_call_target="tpu_custom_call" | custom-call | tf_op jit(solution)/shard_map/val_columns/pallas_call | solution.py:167
  9.1 0.0 copy-start.2
  9.1 0.0 copy-done.1
  9.1 0.0 copy-done.4
  9.2 0.0 copy-done.6
  9.2 1.0 %densities.1.refs_0_ = f32[80,512]{1,0:T(8,128)S(1)} custom-call(f32[80,4096]{1,0:T(8,128)S(1)} %copy-done.1, f32[1,4096]{1,0:T(1,128)S(1)} %bitcast.10, s32[1,512]{1,0:T(1,128)S(1)} %copy-done.6, f32[88,512]{1,0:T(8,128)S(1)} %val_columns.1.v_ref), custom_call_target="tpu_custom_call" | custom-call | tf_op jit(solution)/shard_map/densities/pallas_call | solution.py:175
  10.1 0.0 collective-permute-done.1
  10.1 1.4 %collective-permute-done.2 = f32[4,512]{1,0:T(4,128)S(1)} collective-permute-done((f32[4,512]{1,0:T(4,128)S(1)}, f32[4,512]{1,0:T(4,128)S(1)}, u32[]{:S(2)}, u32[]{:S(2)}) %collective-permute-start.2) | collective-permute-done | bytes 8224 | tf_op jit(solution)/shard_map/ppermute | solution.py:154
  11.5 0.0 collective-permute-done.3
  11.5 0.3 %collective-permute-start.4 = (f32[80,512]{1,0:T(8,128)S(1)}, f32[80,512]{1,0:T(8,128)S(1)}, u32[]{:S(2)}, u32[]{:S(2)}) collective-permute-start(f32[80,512]{1,0:T(8,128)S(1)} %densities.1.refs_0_), channel_id=1, source_target_pairs={{0,1},{1,0},{2,3},{3,2},{4,5},{5,4},{6,7},{7,6},{8,9},{9,8},{10,11... | collective-permute-start | bytes 491528 | tf_op jit(solution)/shard_map/ppermute | solution.py:148
  11.9 0.2 %collective-permute-start.5 = (f32[16,512]{1,0:T(8,128)S(1)}, f32[16,512]{1,0:T(8,128)S(1)}, u32[]{:S(2)}, u32[]{:S(2)}) collective-permute-start(f32[16,512]{1,0:T(8,128)S(1)} %pad_maximum_fusion), channel_id=1, source_target_pairs={{0,1},{1,0},{2,3},{3,2},{4,5},{5,4},{6,7},{7,6},{8,9},{9,8},{10,11... | collective-permute-start | bytes 98312 | tf_op jit(solution)/shard_map/ppermute | solution.py:148
  12.1 1.5 %collective-permute-start.6 = (f32[16,512]{1,0:T(8,128)S(1)}, f32[16,512]{1,0:T(8,128)S(1)}, u32[]{:S(2)}, u32[]{:S(2)}) collective-permute-start(f32[16,512]{1,0:T(8,128)S(1)} %pad_maximum_fusion), channel_id=1, source_target_pairs={{0,5},{1,4},{2,7},{3,6},{4,1},{5,0},{6,3},{7,2},{8,13},{9,12},{10,... | collective-permute-start | bytes 98312 | tf_op jit(solution)/shard_map/ppermute | solution.py:154
  13.6 1.2 %collective-permute-start.7 = (f32[16,512]{1,0:T(8,128)S(1)}, f32[16,512]{1,0:T(8,128)S(1)}, u32[]{:S(2)}, u32[]{:S(2)}) collective-permute-start(f32[16,512]{1,0:T(8,128)S(1)} %pad_maximum_fusion), channel_id=1, source_target_pairs={{0,7},{1,6},{2,5},{3,4},{4,3},{5,2},{6,1},{7,0},{8,15},{9,14},{10,... | collective-permute-start | bytes 98312 | tf_op jit(solution)/shard_map/ppermute | solution.py:154
  14.8 0.5 %collective-permute-start.8 = (f32[16,512]{1,0:T(8,128)S(1)}, f32[16,512]{1,0:T(8,128)S(1)}, u32[]{:S(2)}, u32[]{:S(2)}) collective-permute-start(f32[16,512]{1,0:T(8,128)S(1)} %pad_maximum_fusion), channel_id=1, source_target_pairs={{0,3},{1,2},{2,1},{3,0},{4,7},{5,6},{6,5},{7,4},{8,11},{9,10},{10,... | collective-permute-start | bytes 98312 | tf_op jit(solution)/shard_map/ppermute | solution.py:154
  15.3 0.0 collective-permute-done.4.refs_1_
  15.3 0.2 %columns.1 = (bf16[512,160]{1,0:T(8,128)(2,1)S(1)}, bf16[512,160]{1,0:T(8,128)(2,1)S(1)}) custom-call(f32[80,512]{1,0:T(8,128)S(1)} %densities.1.refs_0_, f32[80,512]{1,0:T(8,128)S(1)} %collective-permute-done.4.refs_1_), custom_call_target="tpu_custom_call" | custom-call | tf_op jit(solution)/shard_map/columns/pallas_call | solution.py:192
  15.5 0.0 collective-permute-done.5.refs_0_
  15.5 0.0 collective-permute-done.6.refs_1_
  15.5 2.3 %collective-permute-done.7.refs_2_ = f32[16,512]{1,0:T(8,128)S(1)} collective-permute-done((f32[16,512]{1,0:T(8,128)S(1)}, f32[16,512]{1,0:T(8,128)S(1)}, u32[]{:S(2)}, u32[]{:S(2)}) %collective-permute-start.7) | collective-permute-done | bytes 32800 | tf_op jit(solution)/shard_map/ppermute | solution.py:154
  17.8 0.3 %collective-permute-done.8.refs_3_ = f32[16,512]{1,0:T(8,128)S(1)} collective-permute-done((f32[16,512]{1,0:T(8,128)S(1)}, f32[16,512]{1,0:T(8,128)S(1)}, u32[]{:S(2)}, u32[]{:S(2)}) %collective-permute-start.8) | collective-permute-done | bytes 32800 | tf_op jit(solution)/shard_map/ppermute | solution.py:154
  18.1 0.0 copy-done.2
  18.1 0.9 %product.1 = f32[64,160]{1,0:T(8,128)} custom-call(f32[64,160]{1,0:T(8,128)S(1)} %bitcast.8, bf16[512,160]{1,0:T(8,128)(2,1)S(1)} %get-tuple-element.19.hi_ref, bf16[512,160]{1,0:T(8,128)(2,1)S(1)} %get-tuple-element.20.lo_ref, f32[16,512]{1,0:T(8,128)S(1)} %collective-permute-done.5.refs_0_, f32[16,512]{1,0:T(8,128)S(1)} %collective-permute-done.6.refs_1_, ...), custom_call_target="tpu_custom_call" | custom-call | tf_op jit(solution)/shard_map/product/pallas_call | solution.py:200
  (2 shorter events, 0.0 us)
Async XLA Ops:
  0.0 8.2 %copy-start = (f32[80,4096]{1,0:T(8,128)S(1)}, f32[80,4096]{1,0:T(8,128)}, u32[]{:S(2)}) copy-start(f32[80,4096]{1,0:T(8,128)} %val_ref.3) | copy-start | bytes 3932164
  0.0 8.2 %copy-start.5 = (s32[1,512]{1,0:T(1,128)S(1)}, s32[1,512]{1,0:T(1,128)}, u32[]{:S(2)}) copy-start(s32[1,512]{1,0:T(1,128)} %pv_ref.2) | copy-start | bytes 6148
  0.0 8.2 %copy-start.3 = (f32[4096]{0:T(1024)S(1)}, f32[4096]{0:T(1024)}, u32[]{:S(2)}) copy-start(f32[4096]{0:T(1024)} %param.10) | copy-start | bytes 49156
  1.5 7.6 %copy-start.1 = (f32[80,4096]{1,0:T(8,128)S(1)}, f32[80,4096]{1,0:T(8,128)}, u32[]{:S(2)}) copy-start(f32[80,4096]{1,0:T(8,128)} %cond_ref.3) | copy-start | bytes 3932164
  1.5 7.6 %copy-start.4 = (f32[4096]{0:T(1024)S(1)}, f32[4096]{0:T(1024)}, u32[]{:S(2)}) copy-start(f32[4096]{0:T(1024)} %param.11) | copy-start | bytes 49156
  1.6 7.6 %copy-start.6 = (s32[1,512]{1,0:T(1,128)S(1)}, s32[1,512]{1,0:T(1,128)}, u32[]{:S(2)}) copy-start(s32[1,512]{1,0:T(1,128)} %pc_ref.2) | copy-start | bytes 6148
  1.6 1.4 %collective-permute-start = (f32[2,4,512]{2,1,0:T(4,128)S(1)}, f32[2,4,512]{2,1,0:T(4,128)S(1)}, u32[]{:S(2)}, u32[]{:S(2)}) collective-permute-start(f32[2,4,512]{2,1,0:T(4,128)S(1)} %slab_rows.1), channel_id=1, source_target_pairs={{0,1},{1,0},{2,3},{3,2},{4,5},{5,4},{6,7},{7,6},{8,9},{9,8},{10,11... | collective-permute-start | bytes 49160 | tf_op jit(solution)/shard_map/ppermute | solution.py:148
  2.9 7.2 %collective-permute-start.1 = (f32[4,512]{1,0:T(4,128)S(1)}, f32[4,512]{1,0:T(4,128)S(1)}, u32[]{:S(2)}, u32[]{:S(2)}) collective-permute-start(f32[4,512]{1,0:T(4,128)S(1)} %get-tuple-element.15), channel_id=1, source_target_pairs={{0,17},{1,16},{2,19},{3,18},{4,21},{5,20},{6,23},{7,22},{8,25},{9,... | collective-permute-start | bytes 24584 | tf_op jit(solution)/shard_map/ppermute | solution.py:154
  6.6 4.9 %collective-permute-start.2 = (f32[4,512]{1,0:T(4,128)S(1)}, f32[4,512]{1,0:T(4,128)S(1)}, u32[]{:S(2)}, u32[]{:S(2)}) collective-permute-start(f32[4,512]{1,0:T(4,128)S(1)} %get-tuple-element.15), channel_id=1, source_target_pairs={{0,25},{1,24},{2,27},{3,26},{4,29},{5,28},{6,31},{7,30},{8,17},{9,... | collective-permute-start | bytes 24584 | tf_op jit(solution)/shard_map/ppermute | solution.py:154
  7.9 3.6 %collective-permute-start.3 = (f32[4,512]{1,0:T(4,128)S(1)}, f32[4,512]{1,0:T(4,128)S(1)}, u32[]{:S(2)}, u32[]{:S(2)}) collective-permute-start(f32[4,512]{1,0:T(4,128)S(1)} %get-tuple-element.15), channel_id=1, source_target_pairs={{0,9},{1,8},{2,11},{3,10},{4,13},{5,12},{6,15},{7,14},{8,1},{9,0},... | collective-permute-start | bytes 24584 | tf_op jit(solution)/shard_map/ppermute | solution.py:154
  9.1 9.0 %copy-start.2 = (f32[160,64]{0,1:T(8,128)S(1)}, f32[160,64]{0,1:T(8,128)}, u32[]{:S(2)}) copy-start(f32[160,64]{0,1:T(8,128)} %param.7) | copy-start | bytes 122884
  11.5 3.8 %collective-permute-start.4 = (f32[80,512]{1,0:T(8,128)S(1)}, f32[80,512]{1,0:T(8,128)S(1)}, u32[]{:S(2)}, u32[]{:S(2)}) collective-permute-start(f32[80,512]{1,0:T(8,128)S(1)} %densities.1.refs_0_), channel_id=1, source_target_pairs={{0,1},{1,0},{2,3},{3,2},{4,5},{5,4},{6,7},{7,6},{8,9},{9,8},{10,11... | collective-permute-start | bytes 491528 | tf_op jit(solution)/shard_map/ppermute | solution.py:148
  11.9 3.6 %collective-permute-start.5 = (f32[16,512]{1,0:T(8,128)S(1)}, f32[16,512]{1,0:T(8,128)S(1)}, u32[]{:S(2)}, u32[]{:S(2)}) collective-permute-start(f32[16,512]{1,0:T(8,128)S(1)} %pad_maximum_fusion), channel_id=1, source_target_pairs={{0,1},{1,0},{2,3},{3,2},{4,5},{5,4},{6,7},{7,6},{8,9},{9,8},{10,11... | collective-permute-start | bytes 98312 | tf_op jit(solution)/shard_map/ppermute | solution.py:148
  12.1 3.4 %collective-permute-start.6 = (f32[16,512]{1,0:T(8,128)S(1)}, f32[16,512]{1,0:T(8,128)S(1)}, u32[]{:S(2)}, u32[]{:S(2)}) collective-permute-start(f32[16,512]{1,0:T(8,128)S(1)} %pad_maximum_fusion), channel_id=1, source_target_pairs={{0,5},{1,4},{2,7},{3,6},{4,1},{5,0},{6,3},{7,2},{8,13},{9,12},{10,... | collective-permute-start | bytes 98312 | tf_op jit(solution)/shard_map/ppermute | solution.py:154
  13.6 4.2 %collective-permute-start.7 = (f32[16,512]{1,0:T(8,128)S(1)}, f32[16,512]{1,0:T(8,128)S(1)}, u32[]{:S(2)}, u32[]{:S(2)}) collective-permute-start(f32[16,512]{1,0:T(8,128)S(1)} %pad_maximum_fusion), channel_id=1, source_target_pairs={{0,7},{1,6},{2,5},{3,4},{4,3},{5,2},{6,1},{7,0},{8,15},{9,14},{10,... | collective-permute-start | bytes 98312 | tf_op jit(solution)/shard_map/ppermute | solution.py:154
  14.8 3.3 %collective-permute-start.8 = (f32[16,512]{1,0:T(8,128)S(1)}, f32[16,512]{1,0:T(8,128)S(1)}, u32[]{:S(2)}, u32[]{:S(2)}) collective-permute-start(f32[16,512]{1,0:T(8,128)S(1)} %pad_maximum_fusion), channel_id=1, source_target_pairs={{0,3},{1,2},{2,1},{3,0},{4,7},{5,6},{6,5},{7,4},{8,11},{9,10},{10,... | collective-permute-start | bytes 98312 | tf_op jit(solution)/shard_map/ppermute | solution.py:154

commit v6 on v5

--- a/solution.py
+++ b/solution.py
@@ -180,6 +180,7 @@
         compiler_params=params(24),
         name="densities",
     )(cond_orb, e_cond[None, :], pair_cond, v)
+    columns = [own] + [exchange(own, n) for n in range(1, n_narrow)]
     got = [sent]
     for stride in strides:
         if stride == strides[0]:
@@ -187,8 +188,9 @@
             *got, own = lax.optimization_barrier((*got, own))
         else:
             sent = jnp.concatenate(got, axis=0)
-            got = [exchange(sent, across)] + [between_chips(sent, d * stride) for d in ORDER[1:]]
-    columns = [own] + [exchange(own, n) for n in range(1, n_narrow)]
+            got = [between_chips(sent, d * stride) for d in ORDER[1:]]
+            sent, got[0] = lax.optimization_barrier((sent, got[0]))
+            got = [exchange(sent, across)] + got
     terms = pl.pallas_call(
         columns_kernel,
         in_specs=[vmem] * n_narrow,

time: 19.1 us -> 18.6 us (0.974)
  waiting for transfers between devices: 4.83 us -> 4.27 us
    ppermute x6, waiting for transfers between devices: 3.99 us -> 3.43 us  [between_chips(): return lax.ppermute(x, ('wide', 'narrow'), pairs_of)]
  transfers between devices with their start and end apart: 9 -> 9, of which waited for: 4 -> 5; matrix products, arithmetic and copies ran while one was open for 0% -> 0% of each run, Pallas kernels for 11% -> 11%
where the time goes in v6:
time: 18.6 us; the launch traced here: 18.5 us
  starting transfers between devices  9.55 us (51%)
  Pallas kernels  4.5 us (24%)
  waiting for transfers between devices  4.27 us (23%)
    ppermute x6, starting transfers between devices, between_chips(): return lax.ppermute(x, ('wide', 'narrow'), pairs_of)  8.45 us
    ppermute x6, waiting for transfers between devices, between_chips(): return lax.ppermute(x, ('wide', 'narrow'), pairs_of)  3.43 us
    pallas_call x1, Pallas kernels, shards(): pl.pallas_call(slab_kernel, in_specs=[hbm] * 4, out_specs=vmem, out_shape...  1.52 us
    ppermute x3, starting transfers between devices, exchange(): return lax.ppermute(x, 'narrow', [(i, i ^ bit) for i in range(n_narrow)])  1.1 us
    pallas_call x1, Pallas kernels, shards(): pl.pallas_call(dens_kernel, in_specs=[vmem] * 4, out_specs=vmem, out_shap...  0.96 us
    pallas_call x1, Pallas kernels, shards(): pl.pallas_call(val_kernel, in_specs=[vmem] * 3, out_specs=vmem, out_shape...  0.94 us
    pallas_call x1, Pallas kernels, shards(): pl.pallas_call(functools.partial(product_kernel, tuple(strides), row_sub)...  0.87 us
    ppermute x3, waiting for transfers between devices, exchange(): return lax.ppermute(x, 'narrow', [(i, i ^ bit) for i in range(n_narrow)])  0.84 us
  transfers between devices with their start and end apart: 9, of which 5 were waited for; matrix products, arithmetic and copies ran while one was open for 0% of the time, Pallas kernels for 11%

profile of v6, /device:TPU:0, one launch (start us, length us, event | category | flops | bytes accessed | tf_op | source)
XLA Modules:
  0.0 18.5 jit_solution(7214552849085102072)
XLA Ops:
  0.0 0.0 copy-start.5
  0.0 0.0 copy-start
  0.0 0.0 copy-start.3
  0.0 1.5 %slab_rows.1 = f32[2,4,512]{2,1,0:T(4,128)S(1)} custom-call(f32[80,4096]{1,0:T(8,128)} %val_ref.3, f32[80,4096]{1,0:T(8,128)} %cond_ref.3, s32[1,512]{1,0:T(1,128)} %pv_ref.2, s32[1,512]{1,0:T(1,128)} %pc_ref.2), custom_call_target="tpu_custom_call" | custom-call | tf_op jit(solution)/shard_map/slab_rows/pallas_call | solution.py:131
  1.5 0.0 copy-start.1
  1.6 0.0 copy-start.4
  1.6 0.0 copy-start.6
  1.6 0.5 %collective-permute-start = (f32[2,4,512]{2,1,0:T(4,128)S(1)}, f32[2,4,512]{2,1,0:T(4,128)S(1)}, u32[]{:S(2)}, u32[]{:S(2)}) collective-permute-start(f32[2,4,512]{2,1,0:T(4,128)S(1)} %slab_rows.1), channel_id=1, source_target_pairs={{0,1},{1,0},{2,3},{3,2},{4,5},{5,4},{6,7},{7,6},{8,9},{9,8},{10,11... | collective-permute-start | bytes 49160 | tf_op jit(solution)/shard_map/ppermute | solution.py:148
  2.1 0.8 %collective-permute-done = f32[2,4,512]{2,1,0:T(4,128)S(1)} collective-permute-done((f32[2,4,512]{2,1,0:T(4,128)S(1)}, f32[2,4,512]{2,1,0:T(4,128)S(1)}, u32[]{:S(2)}, u32[]{:S(2)}) %collective-permute-start) | collective-permute-done | bytes 16416 | tf_op jit(solution)/shard_map/ppermute | solution.py:148
  2.9 3.7 %collective-permute-start.2 = (f32[4,512]{1,0:T(4,128)S(1)}, f32[4,512]{1,0:T(4,128)S(1)}, u32[]{:S(2)}, u32[]{:S(2)}) collective-permute-start(f32[4,512]{1,0:T(4,128)S(1)} %get-tuple-element.20), channel_id=1, source_target_pairs={{0,17},{1,16},{2,19},{3,18},{4,21},{5,20},{6,23},{7,22},{8,25},{9,... | collective-permute-start | bytes 24584 | tf_op jit(solution)/shard_map/ppermute | solution.py:154
  6.6 1.3 %collective-permute-start.3 = (f32[4,512]{1,0:T(4,128)S(1)}, f32[4,512]{1,0:T(4,128)S(1)}, u32[]{:S(2)}, u32[]{:S(2)}) collective-permute-start(f32[4,512]{1,0:T(4,128)S(1)} %get-tuple-element.20), channel_id=1, source_target_pairs={{0,25},{1,24},{2,27},{3,26},{4,29},{5,28},{6,31},{7,30},{8,17},{9,... | collective-permute-start | bytes 24584 | tf_op jit(solution)/shard_map/ppermute | solution.py:154
  7.9 0.2 %collective-permute-start.4 = (f32[4,512]{1,0:T(4,128)S(1)}, f32[4,512]{1,0:T(4,128)S(1)}, u32[]{:S(2)}, u32[]{:S(2)}) collective-permute-start(f32[4,512]{1,0:T(4,128)S(1)} %get-tuple-element.20), channel_id=1, source_target_pairs={{0,9},{1,8},{2,11},{3,10},{4,13},{5,12},{6,15},{7,14},{8,1},{9,0},... | collective-permute-start | bytes 24584 | tf_op jit(solution)/shard_map/ppermute | solution.py:154
  8.2 0.0 copy-done.5
  8.2 0.0 copy-done
  8.2 0.0 copy-done.3
  8.2 0.9 %val_columns.1.v_ref = f32[88,512]{1,0:T(8,128)S(1)} custom-call(f32[80,4096]{1,0:T(8,128)S(1)} %copy-done, f32[1,4096]{1,0:T(1,128)S(1)} %bitcast.9, s32[1,512]{1,0:T(1,128)S(1)} %copy-done.5), custom_call_target="tpu_custom_call" | custom-call | tf_op jit(solution)/shard_map/val_columns/pallas_call | solution.py:167
  9.1 0.0 copy-start.2
  9.1 0.0 copy-done.1
  9.2 0.0 copy-done.4
  9.2 0.0 copy-done.6
  9.2 1.0 %densities.1.refs_0_ = f32[80,512]{1,0:T(8,128)S(1)} custom-call(f32[80,4096]{1,0:T(8,128)S(1)} %copy-done.1, f32[1,4096]{1,0:T(1,128)S(1)} %bitcast.10, s32[1,512]{1,0:T(1,128)S(1)} %copy-done.6, f32[88,512]{1,0:T(8,128)S(1)} %val_columns.1.v_ref), custom_call_target="tpu_custom_call" | custom-call | tf_op jit(solution)/shard_map/densities/pallas_call | solution.py:175
  10.1 0.2 %collective-permute-start.1 = (f32[80,512]{1,0:T(8,128)S(1)}, f32[80,512]{1,0:T(8,128)S(1)}, u32[]{:S(2)}, u32[]{:S(2)}) collective-permute-start(f32[80,512]{1,0:T(8,128)S(1)} %densities.1.refs_0_), channel_id=1, source_target_pairs={{0,1},{1,0},{2,3},{3,2},{4,5},{5,4},{6,7},{7,6},{8,9},{9,8},{10,11... | collective-permute-start | bytes 491528 | tf_op jit(solution)/shard_map/ppermute | solution.py:148
  10.4 0.0 collective-permute-done.2
  10.4 1.1 %collective-permute-done.3 = f32[4,512]{1,0:T(4,128)S(1)} collective-permute-done((f32[4,512]{1,0:T(4,128)S(1)}, f32[4,512]{1,0:T(4,128)S(1)}, u32[]{:S(2)}, u32[]{:S(2)}) %collective-permute-start.3) | collective-permute-done | bytes 8224 | tf_op jit(solution)/shard_map/ppermute | solution.py:154
  11.5 0.0 collective-permute-done.4
  11.5 1.5 %collective-permute-start.5 = (f32[16,512]{1,0:T(8,128)S(1)}, f32[16,512]{1,0:T(8,128)S(1)}, u32[]{:S(2)}, u32[]{:S(2)}) collective-permute-start(f32[16,512]{1,0:T(8,128)S(1)} %pad_maximum_fusion), channel_id=1, source_target_pairs={{0,5},{1,4},{2,7},{3,6},{4,1},{5,0},{6,3},{7,2},{8,13},{9,12},{10,... | collective-permute-start | bytes 98312 | tf_op jit(solution)/shard_map/ppermute | solution.py:154
  13.1 1.2 %collective-permute-start.7 = (f32[16,512]{1,0:T(8,128)S(1)}, f32[16,512]{1,0:T(8,128)S(1)}, u32[]{:S(2)}, u32[]{:S(2)}) collective-permute-start(f32[16,512]{1,0:T(8,128)S(1)} %pad_maximum_fusion), channel_id=1, source_target_pairs={{0,7},{1,6},{2,5},{3,4},{4,3},{5,2},{6,1},{7,0},{8,15},{9,14},{10,... | collective-permute-start | bytes 98312 | tf_op jit(solution)/shard_map/ppermute | solution.py:154
  14.3 0.5 %collective-permute-start.8 = (f32[16,512]{1,0:T(8,128)S(1)}, f32[16,512]{1,0:T(8,128)S(1)}, u32[]{:S(2)}, u32[]{:S(2)}) collective-permute-start(f32[16,512]{1,0:T(8,128)S(1)} %pad_maximum_fusion), channel_id=1, source_target_pairs={{0,3},{1,2},{2,1},{3,0},{4,7},{5,6},{6,5},{7,4},{8,11},{9,10},{10,... | collective-permute-start | bytes 98312 | tf_op jit(solution)/shard_map/ppermute | solution.py:154
  14.8 0.2 collective-permute-done.5.refs_1_
  14.9 0.3 %collective-permute-start.6 = (f32[16,512]{1,0:T(8,128)S(1)}, f32[16,512]{1,0:T(8,128)S(1)}, u32[]{:S(2)}, u32[]{:S(2)}) collective-permute-start(f32[16,512]{1,0:T(8,128)S(1)} %pad_maximum_fusion), channel_id=1, source_target_pairs={{0,1},{1,0},{2,3},{3,2},{4,5},{5,4},{6,7},{7,6},{8,9},{9,8},{10,11... | collective-permute-start | bytes 98312 | tf_op jit(solution)/shard_map/ppermute | solution.py:148
  15.3 0.0 collective-permute-done.1.refs_1_
  15.3 0.2 %columns.1 = (bf16[512,160]{1,0:T(8,128)(2,1)S(1)}, bf16[512,160]{1,0:T(8,128)(2,1)S(1)}) custom-call(f32[80,512]{1,0:T(8,128)S(1)} %densities.1.refs_0_, f32[80,512]{1,0:T(8,128)S(1)} %collective-permute-done.1.refs_1_), custom_call_target="tpu_custom_call" | custom-call | tf_op jit(solution)/shard_map/columns/pallas_call | solution.py:194
  15.5 1.8 %collective-permute-done.7.refs_2_ = f32[16,512]{1,0:T(8,128)S(1)} collective-permute-done((f32[16,512]{1,0:T(8,128)S(1)}, f32[16,512]{1,0:T(8,128)S(1)}, u32[]{:S(2)}, u32[]{:S(2)}) %collective-permute-start.7) | collective-permute-done | bytes 32800 | tf_op jit(solution)/shard_map/ppermute | solution.py:154
  17.3 0.3 %collective-permute-done.8.refs_3_ = f32[16,512]{1,0:T(8,128)S(1)} collective-permute-done((f32[16,512]{1,0:T(8,128)S(1)}, f32[16,512]{1,0:T(8,128)S(1)}, u32[]{:S(2)}, u32[]{:S(2)}) %collective-permute-start.8) | collective-permute-done | bytes 32800 | tf_op jit(solution)/shard_map/ppermute | solution.py:154
  17.6 0.0 collective-permute-done.6.refs_0_
  17.6 0.0 copy-done.2
  17.6 0.9 %product.1 = f32[64,160]{1,0:T(8,128)} custom-call(f32[64,160]{1,0:T(8,128)S(1)} %bitcast.8, bf16[512,160]{1,0:T(8,128)(2,1)S(1)} %get-tuple-element.18.hi_ref, bf16[512,160]{1,0:T(8,128)(2,1)S(1)} %get-tuple-element.19.lo_ref, f32[16,512]{1,0:T(8,128)S(1)} %collective-permute-done.6.refs_0_, f32[16,512]{1,0:T(8,128)S(1)} %collective-permute-done.5.refs_1_, ...), custom_call_target="tpu_custom_call" | custom-call | tf_op jit(solution)/shard_map/product/pallas_call | solution.py:202
  (2 shorter events, 0.0 us)
Async XLA Ops:
  0.0 8.2 %copy-start.5 = (s32[1,512]{1,0:T(1,128)S(1)}, s32[1,512]{1,0:T(1,128)}, u32[]{:S(2)}) copy-start(s32[1,512]{1,0:T(1,128)} %pv_ref.2) | copy-start | bytes 6148
  0.0 8.2 %copy-start = (f32[80,4096]{1,0:T(8,128)S(1)}, f32[80,4096]{1,0:T(8,128)}, u32[]{:S(2)}) copy-start(f32[80,4096]{1,0:T(8,128)} %val_ref.3) | copy-start | bytes 3932164
  0.0 8.2 %copy-start.3 = (f32[4096]{0:T(1024)S(1)}, f32[4096]{0:T(1024)}, u32[]{:S(2)}) copy-start(f32[4096]{0:T(1024)} %param.10) | copy-start | bytes 49156
  1.5 7.6 %copy-start.1 = (f32[80,4096]{1,0:T(8,128)S(1)}, f32[80,4096]{1,0:T(8,128)}, u32[]{:S(2)}) copy-start(f32[80,4096]{1,0:T(8,128)} %cond_ref.3) | copy-start | bytes 3932164
  1.6 7.6 %copy-start.4 = (f32[4096]{0:T(1024)S(1)}, f32[4096]{0:T(1024)}, u32[]{:S(2)}) copy-start(f32[4096]{0:T(1024)} %param.11) | copy-start | bytes 49156
  1.6 7.6 %copy-start.6 = (s32[1,512]{1,0:T(1,128)S(1)}, s32[1,512]{1,0:T(1,128)}, u32[]{:S(2)}) copy-start(s32[1,512]{1,0:T(1,128)} %pc_ref.2) | copy-start | bytes 6148
  1.6 1.4 %collective-permute-start = (f32[2,4,512]{2,1,0:T(4,128)S(1)}, f32[2,4,512]{2,1,0:T(4,128)S(1)}, u32[]{:S(2)}, u32[]{:S(2)}) collective-permute-start(f32[2,4,512]{2,1,0:T(4,128)S(1)} %slab_rows.1), channel_id=1, source_target_pairs={{0,1},{1,0},{2,3},{3,2},{4,5},{5,4},{6,7},{7,6},{8,9},{9,8},{10,11... | collective-permute-start | bytes 49160 | tf_op jit(solution)/shard_map/ppermute | solution.py:148
  2.9 7.4 %collective-permute-start.2 = (f32[4,512]{1,0:T(4,128)S(1)}, f32[4,512]{1,0:T(4,128)S(1)}, u32[]{:S(2)}, u32[]{:S(2)}) collective-permute-start(f32[4,512]{1,0:T(4,128)S(1)} %get-tuple-element.20), channel_id=1, source_target_pairs={{0,17},{1,16},{2,19},{3,18},{4,21},{5,20},{6,23},{7,22},{8,25},{9,... | collective-permute-start | bytes 24584 | tf_op jit(solution)/shard_map/ppermute | solution.py:154
  6.6 4.9 %collective-permute-start.3 = (f32[4,512]{1,0:T(4,128)S(1)}, f32[4,512]{1,0:T(4,128)S(1)}, u32[]{:S(2)}, u32[]{:S(2)}) collective-permute-start(f32[4,512]{1,0:T(4,128)S(1)} %get-tuple-element.20), channel_id=1, source_target_pairs={{0,25},{1,24},{2,27},{3,26},{4,29},{5,28},{6,31},{7,30},{8,17},{9,... | collective-permute-start | bytes 24584 | tf_op jit(solution)/shard_map/ppermute | solution.py:154
  7.9 3.6 %collective-permute-start.4 = (f32[4,512]{1,0:T(4,128)S(1)}, f32[4,512]{1,0:T(4,128)S(1)}, u32[]{:S(2)}, u32[]{:S(2)}) collective-permute-start(f32[4,512]{1,0:T(4,128)S(1)} %get-tuple-element.20), channel_id=1, source_target_pairs={{0,9},{1,8},{2,11},{3,10},{4,13},{5,12},{6,15},{7,14},{8,1},{9,0},... | collective-permute-start | bytes 24584 | tf_op jit(solution)/shard_map/ppermute | solution.py:154
  9.1 8.5 %copy-start.2 = (f32[160,64]{0,1:T(8,128)S(1)}, f32[160,64]{0,1:T(8,128)}, u32[]{:S(2)}) copy-start(f32[160,64]{0,1:T(8,128)} %param.7) | copy-start | bytes 122884
  10.1 5.2 %collective-permute-start.1 = (f32[80,512]{1,0:T(8,128)S(1)}, f32[80,512]{1,0:T(8,128)S(1)}, u32[]{:S(2)}, u32[]{:S(2)}) collective-permute-start(f32[80,512]{1,0:T(8,128)S(1)} %densities.1.refs_0_), channel_id=1, source_target_pairs={{0,1},{1,0},{2,3},{3,2},{4,5},{5,4},{6,7},{7,6},{8,9},{9,8},{10,11... | collective-permute-start | bytes 491528 | tf_op jit(solution)/shard_map/ppermute | solution.py:148
  11.5 3.4 %collective-permute-start.5 = (f32[16,512]{1,0:T(8,128)S(1)}, f32[16,512]{1,0:T(8,128)S(1)}, u32[]{:S(2)}, u32[]{:S(2)}) collective-permute-start(f32[16,512]{1,0:T(8,128)S(1)} %pad_maximum_fusion), channel_id=1, source_target_pairs={{0,5},{1,4},{2,7},{3,6},{4,1},{5,0},{6,3},{7,2},{8,13},{9,12},{10,... | collective-permute-start | bytes 98312 | tf_op jit(solution)/shard_map/ppermute | solution.py:154
  13.1 4.2 %collective-permute-start.7 = (f32[16,512]{1,0:T(8,128)S(1)}, f32[16,512]{1,0:T(8,128)S(1)}, u32[]{:S(2)}, u32[]{:S(2)}) collective-permute-start(f32[16,512]{1,0:T(8,128)S(1)} %pad_maximum_fusion), channel_id=1, source_target_pairs={{0,7},{1,6},{2,5},{3,4},{4,3},{5,2},{6,1},{7,0},{8,15},{9,14},{10,... | collective-permute-start | bytes 98312 | tf_op jit(solution)/shard_map/ppermute | solution.py:154
  14.3 3.3 %collective-permute-start.8 = (f32[16,512]{1,0:T(8,128)S(1)}, f32[16,512]{1,0:T(8,128)S(1)}, u32[]{:S(2)}, u32[]{:S(2)}) collective-permute-start(f32[16,512]{1,0:T(8,128)S(1)} %pad_maximum_fusion), channel_id=1, source_target_pairs={{0,3},{1,2},{2,1},{3,0},{4,7},{5,6},{6,5},{7,4},{8,11},{9,10},{10,... | collective-permute-start | bytes 98312 | tf_op jit(solution)/shard_map/ppermute | solution.py:154
  14.9 2.7 %collective-permute-start.6 = (f32[16,512]{1,0:T(8,128)S(1)}, f32[16,512]{1,0:T(8,128)S(1)}, u32[]{:S(2)}, u32[]{:S(2)}) collective-permute-start(f32[16,512]{1,0:T(8,128)S(1)} %pad_maximum_fusion), channel_id=1, source_target_pairs={{0,1},{1,0},{2,3},{3,2},{4,5},{5,4},{6,7},{7,6},{8,9},{9,8},{10,11... | collective-permute-start | bytes 98312 | tf_op jit(solution)/shard_map/ppermute | solution.py:148

commit v7 on v6

--- a/solution.py
+++ b/solution.py
@@ -10,7 +10,7 @@
 SLAB_DEV = 8
 ROWS = 8
 RADIX = 4
-ORDER = (0, 2, 3, 1)
+STEPS = ((2, 3, 1, 0), (3, 2, 0, 1), (1, 0, 3, 2))
 CHUNK = 256
 MIB = 1 << 20
 
@@ -44,8 +44,7 @@
     return out
 
 
-def pick_few(rows, idx):
-    hot = one_hot(idx, CHUNK)
+def pick_few(rows, hot, idx):
     terms = split(by_chunk(rows, CHUNK), 2)
     m = terms[0].shape[0]
     every = jnp.dot(jnp.concatenate(terms, axis=0), hot, preferred_element_type=jnp.float32)
@@ -60,16 +59,18 @@
 
 
 def slab_kernel(val_ref, cond_ref, pv_ref, pc_ref, out_ref, val, cond, pv, pc, sems):
-    moves = ((val_ref.at[pl.ds(0, ROWS)], val), (pv_ref, pv), (cond_ref.at[pl.ds(0, ROWS)], cond), (pc_ref, pc))
+    moves = ((pv_ref, pv), (pc_ref, pc), (val_ref.at[pl.ds(0, ROWS)], val), (cond_ref.at[pl.ds(0, ROWS)], cond))
     copies = [pltpu.make_async_copy(src, dst, sems.at[i]) for i, (src, dst) in enumerate(moves)]
     for copy in copies:
-        copy.start()
+        copy.start(priority=1)
+    copies[0].wait()
+    hot_v = one_hot(pv[...], CHUNK)
     copies[1].wait()
-    copies[0].wait()
-    dens = pick_few(val[...], pv[...])
+    hot_c = one_hot(pc[...], CHUNK)
+    copies[2].wait()
+    dens = pick_few(val[...], hot_v, pv[...])
     copies[3].wait()
-    copies[2].wait()
-    dens = dens * pick_few(cond[...], pc[...])
+    dens = dens * pick_few(cond[...], hot_c, pc[...])
     sub = out_ref.shape[1]
     for n in range(out_ref.shape[0]):
         out_ref[n] = dens[n * sub : (n + 1) * sub]
@@ -105,6 +106,17 @@
     hi_ref[...], lo_ref[...] = split(jnp.concatenate(cols, axis=0).T, 2)
 
 
+def by_digit(parts, place):
+    from_place = [[here] + [step.index(here) for step in STEPS] for here in range(RADIX)]
+    out = []
+    for source in range(RADIX):
+        part = parts[from_place[0].index(source)]
+        for here in range(1, RADIX):
+            part = jnp.where(place == here, parts[from_place[here].index(source)], part)
+        out.append(part)
+    return out
+
+
 def product_kernel(strides, sub, chi_ref, hi_ref, lo_ref, *refs):
     *rows_refs, out_ref = refs
     s_hi, s_lo = split(jnp.concatenate([ref[...] for ref in rows_refs], axis=0), 2)
@@ -112,10 +124,17 @@
     by_hi = jnp.dot(jnp.concatenate([s_hi, s_lo], axis=0), hi_ref[...], preferred_element_type=jnp.float32)
     by_lo = jnp.dot(s_hi, lo_ref[...], preferred_element_type=jnp.float32)
     total = by_hi[:m] + (by_hi[m:] + by_lo)
-    blocks = m // sub
-    held = {sum(s * ORDER[j // RADIX**i % RADIX] for i, s in enumerate(strides)): j for j in range(blocks)}
-    parts = [total[held[x] * sub : (held[x] + 1) * sub] for x in range(blocks)]
-    out_ref[...] = chi_ref[...] + jnp.concatenate(by_source(parts, lax.axis_index("wide")), axis=0)
+    wide = lax.axis_index("wide")
+    parts = [total[at : at + sub] for at in range(0, m, sub)]
+    for i, stride in enumerate(strides):
+        place, low = lax.rem(lax.div(wide, stride), RADIX), RADIX**i
+        for j in range(len(parts)):
+            if j // low % RADIX == 0:
+                held = [j + k * low for k in range(RADIX)]
+                for at, part in zip(held, by_digit([parts[at] for at in held], place)):
+                    parts[at] = part
+    held = {sum(s * (j // RADIX**i % RADIX) for i, s in enumerate(strides)): j for j in range(len(parts))}
+    out_ref[...] = chi_ref[...] + jnp.concatenate([parts[held[w]] for w in range(len(parts))], axis=0)
 
 
 def in_hbm(x):
@@ -149,8 +168,12 @@
 
     across = n_narrow - 1
 
-    def between_chips(x, bit):
-        pairs_of = [(w * n_narrow + n, (w ^ bit) * n_narrow + n ^ across) for w in range(n_wide) for n in range(n_narrow)]
+    def between_chips(x, step, stride):
+        pairs_of = []
+        for w in range(n_wide):
+            place = w // stride % RADIX
+            to = w + (step[place] - place) * stride
+            pairs_of += [(w * n_narrow + n, to * n_narrow + (n ^ across)) for n in range(n_narrow)]
         return lax.ppermute(x, ("wide", "narrow"), pairs_of)
 
     strides = []
@@ -184,11 +207,11 @@
     got = [sent]
     for stride in strides:
         if stride == strides[0]:
-            got = [own_block] + [between_chips(sent, d * stride) for d in ORDER[1:]]
+            got = [own_block] + [between_chips(sent, step, stride) for step in STEPS]
             *got, own = lax.optimization_barrier((*got, own))
         else:
             sent = jnp.concatenate(got, axis=0)
-            got = [between_chips(sent, d * stride) for d in ORDER[1:]]
+            got = [between_chips(sent, step, stride) for step in STEPS]
             sent, got[0] = lax.optimization_barrier((sent, got[0]))
             got = [exchange(sent, across)] + got
     terms = pl.pallas_call(

time: 18.6 us -> 18.2 us (0.978)
  waiting for transfers between devices: 4.27 us -> 2.92 us
  starting transfers between devices: 9.55 us -> 10.5 us
    ppermute x6, waiting for transfers between devices: 3.43 us -> 2.07 us  [between_chips(): return lax.ppermute(x, ('wide', 'narrow'), pairs_of)]
    ppermute x6, starting transfers between devices: 8.45 us -> 9.36 us  [between_chips(): return lax.ppermute(x, ('wide', 'narrow'), pairs_of)]
  transfers between devices with their start and end apart: 9 -> 9, of which waited for: 5 -> 6; matrix products, arithmetic and copies ran while one was open for 0% -> 0% of each run, Pallas kernels for 11% -> 12%
where the time goes in v7:
time: 18.2 us; the launch traced here: 18.1 us
  starting transfers between devices  10.5 us (58%)
  Pallas kernels  4.51 us (25%)
  waiting for transfers between devices  2.92 us (16%)
    ppermute x6, starting transfers between devices, between_chips(): return lax.ppermute(x, ('wide', 'narrow'), pairs_of)  9.36 us
    ppermute x6, waiting for transfers between devices, between_chips(): return lax.ppermute(x, ('wide', 'narrow'), pairs_of)  2.07 us
    pallas_call x1, Pallas kernels, shards(): pl.pallas_call(slab_kernel, in_specs=[hbm] * 4, out_specs=vmem, out_shape...  1.52 us
    ppermute x3, starting transfers between devices, exchange(): return lax.ppermute(x, 'narrow', [(i, i ^ bit) for i in range(n_narrow)])  1.14 us
    pallas_call x1, Pallas kernels, shards(): pl.pallas_call(dens_kernel, in_specs=[vmem] * 4, out_specs=vmem, out_shap...  0.96 us
    pallas_call x1, Pallas kernels, shards(): pl.pallas_call(val_kernel, in_specs=[vmem] * 3, out_specs=vmem, out_shape...  0.94 us
    pallas_call x1, Pallas kernels, shards(): pl.pallas_call(functools.partial(product_kernel, tuple(strides), row_sub)...  0.88 us
    ppermute x3, waiting for transfers between devices, exchange(): return lax.ppermute(x, 'narrow', [(i, i ^ bit) for i in range(n_narrow)])  0.84 us
  transfers between devices with their start and end apart: 9, of which 6 were waited for; matrix products, arithmetic and copies ran while one was open for 0% of the time, Pallas kernels for 12%

profile of v7, /device:TPU:0, one launch (start us, length us, event | category | flops | bytes accessed | tf_op | source)
XLA Modules:
  0.0 18.1 jit_solution(3835541684610778286)
XLA Ops:
  0.0 0.0 copy-start.5
  0.0 0.0 copy-start
  0.0 0.0 copy-start.3
  0.0 1.5 %slab_rows.1 = f32[2,4,512]{2,1,0:T(4,128)S(1)} custom-call(f32[80,4096]{1,0:T(8,128)} %val_ref.3, f32[80,4096]{1,0:T(8,128)} %cond_ref.3, s32[1,512]{1,0:T(1,128)} %pv_ref.2, s32[1,512]{1,0:T(1,128)} %pc_ref.2), custom_call_target="tpu_custom_call" | custom-call | tf_op jit(solution)/shard_map/slab_rows/pallas_call | solution.py:150
  1.5 0.0 copy-start.1
  1.5 0.0 copy-start.4
  1.6 0.0 copy-start.6
  1.6 0.5 %collective-permute-start = (f32[2,4,512]{2,1,0:T(4,128)S(1)}, f32[2,4,512]{2,1,0:T(4,128)S(1)}, u32[]{:S(2)}, u32[]{:S(2)}) collective-permute-start(f32[2,4,512]{2,1,0:T(4,128)S(1)} %slab_rows.1), channel_id=1, source_target_pairs={{0,1},{1,0},{2,3},{3,2},{4,5},{5,4},{6,7},{7,6},{8,9},{9,8},{10,11... | collective-permute-start | bytes 49160 | tf_op jit(solution)/shard_map/ppermute | solution.py:167
  2.1 0.8 %collective-permute-done = f32[2,4,512]{2,1,0:T(4,128)S(1)} collective-permute-done((f32[2,4,512]{2,1,0:T(4,128)S(1)}, f32[2,4,512]{2,1,0:T(4,128)S(1)}, u32[]{:S(2)}, u32[]{:S(2)}) %collective-permute-start) | collective-permute-done | bytes 16416 | tf_op jit(solution)/shard_map/ppermute | solution.py:167
  2.9 3.7 %collective-permute-start.2 = (f32[4,512]{1,0:T(4,128)S(1)}, f32[4,512]{1,0:T(4,128)S(1)}, u32[]{:S(2)}, u32[]{:S(2)}) collective-permute-start(f32[4,512]{1,0:T(4,128)S(1)} %get-tuple-element.20), channel_id=1, source_target_pairs={{0,17},{1,16},{2,19},{3,18},{4,21},{5,20},{6,23},{7,22},{8,25},{9,... | collective-permute-start | bytes 24584 | tf_op jit(solution)/shard_map/ppermute | solution.py:177
  6.6 1.1 %collective-permute-start.3 = (f32[4,512]{1,0:T(4,128)S(1)}, f32[4,512]{1,0:T(4,128)S(1)}, u32[]{:S(2)}, u32[]{:S(2)}) collective-permute-start(f32[4,512]{1,0:T(4,128)S(1)} %get-tuple-element.20), channel_id=1, source_target_pairs={{0,25},{1,24},{2,27},{3,26},{4,29},{5,28},{6,31},{7,30},{8,17},{9,... | collective-permute-start | bytes 24584 | tf_op jit(solution)/shard_map/ppermute | solution.py:177
  7.7 0.5 %collective-permute-start.4 = (f32[4,512]{1,0:T(4,128)S(1)}, f32[4,512]{1,0:T(4,128)S(1)}, u32[]{:S(2)}, u32[]{:S(2)}) collective-permute-start(f32[4,512]{1,0:T(4,128)S(1)} %get-tuple-element.20), channel_id=1, source_target_pairs={{0,9},{1,8},{2,11},{3,10},{4,13},{5,12},{6,15},{7,14},{8,1},{9,0},... | collective-permute-start | bytes 24584 | tf_op jit(solution)/shard_map/ppermute | solution.py:177
  8.2 0.0 copy-done.5
  8.2 0.0 copy-done
  8.2 0.0 copy-done.3
  8.2 0.9 %val_columns.1.v_ref = f32[88,512]{1,0:T(8,128)S(1)} custom-call(f32[80,4096]{1,0:T(8,128)S(1)} %copy-done, f32[1,4096]{1,0:T(1,128)S(1)} %bitcast.9, s32[1,512]{1,0:T(1,128)S(1)} %copy-done.5), custom_call_target="tpu_custom_call" | custom-call | tf_op jit(solution)/shard_map/val_columns/pallas_call | solution.py:190
  9.1 0.0 copy-start.2
  9.1 0.0 copy-done.1
  9.1 0.0 copy-done.4
  9.2 0.0 copy-done.6
  9.2 1.0 %densities.1.refs_0_ = f32[80,512]{1,0:T(8,128)S(1)} custom-call(f32[80,4096]{1,0:T(8,128)S(1)} %copy-done.1, f32[1,4096]{1,0:T(1,128)S(1)} %bitcast.10, s32[1,512]{1,0:T(1,128)S(1)} %copy-done.6, f32[88,512]{1,0:T(8,128)S(1)} %val_columns.1.v_ref), custom_call_target="tpu_custom_call" | custom-call | tf_op jit(solution)/shard_map/densities/pallas_call | solution.py:198
  10.1 0.2 %collective-permute-start.1 = (f32[80,512]{1,0:T(8,128)S(1)}, f32[80,512]{1,0:T(8,128)S(1)}, u32[]{:S(2)}, u32[]{:S(2)}) collective-permute-start(f32[80,512]{1,0:T(8,128)S(1)} %densities.1.refs_0_), channel_id=1, source_target_pairs={{0,1},{1,0},{2,3},{3,2},{4,5},{5,4},{6,7},{7,6},{8,9},{9,8},{10,11... | collective-permute-start | bytes 491528 | tf_op jit(solution)/shard_map/ppermute | solution.py:167
  10.4 0.0 collective-permute-done.2
  10.4 0.2 %collective-permute-done.3 = f32[4,512]{1,0:T(4,128)S(1)} collective-permute-done((f32[4,512]{1,0:T(4,128)S(1)}, f32[4,512]{1,0:T(4,128)S(1)}, u32[]{:S(2)}, u32[]{:S(2)}) %collective-permute-start.3) | collective-permute-done | bytes 8224 | tf_op jit(solution)/shard_map/ppermute | solution.py:177
  10.6 0.2 collective-permute-done.4
  10.8 1.5 %collective-permute-start.5 = (f32[16,512]{1,0:T(8,128)S(1)}, f32[16,512]{1,0:T(8,128)S(1)}, u32[]{:S(2)}, u32[]{:S(2)}) collective-permute-start(f32[16,512]{1,0:T(8,128)S(1)} %pad_maximum_fusion), channel_id=1, source_target_pairs={{0,5},{1,4},{2,7},{3,6},{4,3},{5,2},{6,1},{7,0},{8,13},{9,12},{10,... | collective-permute-start | bytes 98312 | tf_op jit(solution)/shard_map/ppermute | solution.py:177
  12.3 1.2 %collective-permute-start.7 = (f32[16,512]{1,0:T(8,128)S(1)}, f32[16,512]{1,0:T(8,128)S(1)}, u32[]{:S(2)}, u32[]{:S(2)}) collective-permute-start(f32[16,512]{1,0:T(8,128)S(1)} %pad_maximum_fusion), channel_id=1, source_target_pairs={{0,7},{1,6},{2,5},{3,4},{4,1},{5,0},{6,3},{7,2},{8,15},{9,14},{10,... | collective-permute-start | bytes 98312 | tf_op jit(solution)/shard_map/ppermute | solution.py:177
  13.5 1.4 %collective-permute-start.8 = (f32[16,512]{1,0:T(8,128)S(1)}, f32[16,512]{1,0:T(8,128)S(1)}, u32[]{:S(2)}, u32[]{:S(2)}) collective-permute-start(f32[16,512]{1,0:T(8,128)S(1)} %pad_maximum_fusion), channel_id=1, source_target_pairs={{0,3},{1,2},{2,1},{3,0},{4,7},{5,6},{6,5},{7,4},{8,11},{9,10},{10,... | collective-permute-start | bytes 98312 | tf_op jit(solution)/shard_map/ppermute | solution.py:177
  14.9 0.1 collective-permute-done.5.refs_1_
  15.1 0.4 %collective-permute-start.6 = (f32[16,512]{1,0:T(8,128)S(1)}, f32[16,512]{1,0:T(8,128)S(1)}, u32[]{:S(2)}, u32[]{:S(2)}) collective-permute-start(f32[16,512]{1,0:T(8,128)S(1)} %pad_maximum_fusion), channel_id=1, source_target_pairs={{0,1},{1,0},{2,3},{3,2},{4,5},{5,4},{6,7},{7,6},{8,9},{9,8},{10,11... | collective-permute-start | bytes 98312 | tf_op jit(solution)/shard_map/ppermute | solution.py:167
  15.5 0.0 collective-permute-done.1.refs_1_
  15.5 0.2 %columns.1 = (bf16[512,160]{1,0:T(8,128)(2,1)S(1)}, bf16[512,160]{1,0:T(8,128)(2,1)S(1)}) custom-call(f32[80,512]{1,0:T(8,128)S(1)} %densities.1.refs_0_, f32[80,512]{1,0:T(8,128)S(1)} %collective-permute-done.1.refs_1_), custom_call_target="tpu_custom_call" | custom-call | tf_op jit(solution)/shard_map/columns/pallas_call | solution.py:217
  15.7 0.5 %collective-permute-done.7.refs_2_ = f32[16,512]{1,0:T(8,128)S(1)} collective-permute-done((f32[16,512]{1,0:T(8,128)S(1)}, f32[16,512]{1,0:T(8,128)S(1)}, u32[]{:S(2)}, u32[]{:S(2)}) %collective-permute-start.7) | collective-permute-done | bytes 32800 | tf_op jit(solution)/shard_map/ppermute | solution.py:177
  16.2 1.0 %collective-permute-done.8.refs_3_ = f32[16,512]{1,0:T(8,128)S(1)} collective-permute-done((f32[16,512]{1,0:T(8,128)S(1)}, f32[16,512]{1,0:T(8,128)S(1)}, u32[]{:S(2)}, u32[]{:S(2)}) %collective-permute-start.8) | collective-permute-done | bytes 32800 | tf_op jit(solution)/shard_map/ppermute | solution.py:177
  17.2 0.0 collective-permute-done.6.refs_0_
  17.2 0.0 copy-done.2
  17.2 0.9 %product.1 = f32[64,160]{1,0:T(8,128)} custom-call(f32[64,160]{1,0:T(8,128)S(1)} %bitcast.8, bf16[512,160]{1,0:T(8,128)(2,1)S(1)} %get-tuple-element.18.hi_ref, bf16[512,160]{1,0:T(8,128)(2,1)S(1)} %get-tuple-element.19.lo_ref, f32[16,512]{1,0:T(8,128)S(1)} %collective-permute-done.6.refs_0_, f32[16,512]{1,0:T(8,128)S(1)} %collective-permute-done.5.refs_1_, ...), custom_call_target="tpu_custom_call" | custom-call | tf_op jit(solution)/shard_map/product/pallas_call | solution.py:225
  (2 shorter events, 0.0 us)
Async XLA Ops:
  0.0 8.2 %copy-start.5 = (s32[1,512]{1,0:T(1,128)S(1)}, s32[1,512]{1,0:T(1,128)}, u32[]{:S(2)}) copy-start(s32[1,512]{1,0:T(1,128)} %pv_ref.2) | copy-start | bytes 6148
  0.0 8.2 %copy-start = (f32[80,4096]{1,0:T(8,128)S(1)}, f32[80,4096]{1,0:T(8,128)}, u32[]{:S(2)}) copy-start(f32[80,4096]{1,0:T(8,128)} %val_ref.3) | copy-start | bytes 3932164
  0.0 8.2 %copy-start.3 = (f32[4096]{0:T(1024)S(1)}, f32[4096]{0:T(1024)}, u32[]{:S(2)}) copy-start(f32[4096]{0:T(1024)} %param.10) | copy-start | bytes 49156
  1.5 7.6 %copy-start.1 = (f32[80,4096]{1,0:T(8,128)S(1)}, f32[80,4096]{1,0:T(8,128)}, u32[]{:S(2)}) copy-start(f32[80,4096]{1,0:T(8,128)} %cond_ref.3) | copy-start | bytes 3932164
  1.5 7.6 %copy-start.4 = (f32[4096]{0:T(1024)S(1)}, f32[4096]{0:T(1024)}, u32[]{:S(2)}) copy-start(f32[4096]{0:T(1024)} %param.11) | copy-start | bytes 49156
  1.6 7.6 %copy-start.6 = (s32[1,512]{1,0:T(1,128)S(1)}, s32[1,512]{1,0:T(1,128)}, u32[]{:S(2)}) copy-start(s32[1,512]{1,0:T(1,128)} %pc_ref.2) | copy-start | bytes 6148
  1.6 1.4 %collective-permute-start = (f32[2,4,512]{2,1,0:T(4,128)S(1)}, f32[2,4,512]{2,1,0:T(4,128)S(1)}, u32[]{:S(2)}, u32[]{:S(2)}) collective-permute-start(f32[2,4,512]{2,1,0:T(4,128)S(1)} %slab_rows.1), channel_id=1, source_target_pairs={{0,1},{1,0},{2,3},{3,2},{4,5},{5,4},{6,7},{7,6},{8,9},{9,8},{10,11... | collective-permute-start | bytes 49160 | tf_op jit(solution)/shard_map/ppermute | solution.py:167
  2.9 7.4 %collective-permute-start.2 = (f32[4,512]{1,0:T(4,128)S(1)}, f32[4,512]{1,0:T(4,128)S(1)}, u32[]{:S(2)}, u32[]{:S(2)}) collective-permute-start(f32[4,512]{1,0:T(4,128)S(1)} %get-tuple-element.20), channel_id=1, source_target_pairs={{0,17},{1,16},{2,19},{3,18},{4,21},{5,20},{6,23},{7,22},{8,25},{9,... | collective-permute-start | bytes 24584 | tf_op jit(solution)/shard_map/ppermute | solution.py:177
  6.6 4.0 %collective-permute-start.3 = (f32[4,512]{1,0:T(4,128)S(1)}, f32[4,512]{1,0:T(4,128)S(1)}, u32[]{:S(2)}, u32[]{:S(2)}) collective-permute-start(f32[4,512]{1,0:T(4,128)S(1)} %get-tuple-element.20), channel_id=1, source_target_pairs={{0,25},{1,24},{2,27},{3,26},{4,29},{5,28},{6,31},{7,30},{8,17},{9,... | collective-permute-start | bytes 24584 | tf_op jit(solution)/shard_map/ppermute | solution.py:177
  7.7 3.1 %collective-permute-start.4 = (f32[4,512]{1,0:T(4,128)S(1)}, f32[4,512]{1,0:T(4,128)S(1)}, u32[]{:S(2)}, u32[]{:S(2)}) collective-permute-start(f32[4,512]{1,0:T(4,128)S(1)} %get-tuple-element.20), channel_id=1, source_target_pairs={{0,9},{1,8},{2,11},{3,10},{4,13},{5,12},{6,15},{7,14},{8,1},{9,0},... | collective-permute-start | bytes 24584 | tf_op jit(solution)/shard_map/ppermute | solution.py:177
  9.1 8.1 %copy-start.2 = (f32[160,64]{0,1:T(8,128)S(1)}, f32[160,64]{0,1:T(8,128)}, u32[]{:S(2)}) copy-start(f32[160,64]{0,1:T(8,128)} %param.7) | copy-start | bytes 122884
  10.1 5.3 %collective-permute-start.1 = (f32[80,512]{1,0:T(8,128)S(1)}, f32[80,512]{1,0:T(8,128)S(1)}, u32[]{:S(2)}, u32[]{:S(2)}) collective-permute-start(f32[80,512]{1,0:T(8,128)S(1)} %densities.1.refs_0_), channel_id=1, source_target_pairs={{0,1},{1,0},{2,3},{3,2},{4,5},{5,4},{6,7},{7,6},{8,9},{9,8},{10,11... | collective-permute-start | bytes 491528 | tf_op jit(solution)/shard_map/ppermute | solution.py:167
  10.8 4.3 %collective-permute-start.5 = (f32[16,512]{1,0:T(8,128)S(1)}, f32[16,512]{1,0:T(8,128)S(1)}, u32[]{:S(2)}, u32[]{:S(2)}) collective-permute-start(f32[16,512]{1,0:T(8,128)S(1)} %pad_maximum_fusion), channel_id=1, source_target_pairs={{0,5},{1,4},{2,7},{3,6},{4,3},{5,2},{6,1},{7,0},{8,13},{9,12},{10,... | collective-permute-start | bytes 98312 | tf_op jit(solution)/shard_map/ppermute | solution.py:177
  12.3 3.8 %collective-permute-start.7 = (f32[16,512]{1,0:T(8,128)S(1)}, f32[16,512]{1,0:T(8,128)S(1)}, u32[]{:S(2)}, u32[]{:S(2)}) collective-permute-start(f32[16,512]{1,0:T(8,128)S(1)} %pad_maximum_fusion), channel_id=1, source_target_pairs={{0,7},{1,6},{2,5},{3,4},{4,1},{5,0},{6,3},{7,2},{8,15},{9,14},{10,... | collective-permute-start | bytes 98312 | tf_op jit(solution)/shard_map/ppermute | solution.py:177
  13.5 3.7 %collective-permute-start.8 = (f32[16,512]{1,0:T(8,128)S(1)}, f32[16,512]{1,0:T(8,128)S(1)}, u32[]{:S(2)}, u32[]{:S(2)}) collective-permute-start(f32[16,512]{1,0:T(8,128)S(1)} %pad_maximum_fusion), channel_id=1, source_target_pairs={{0,3},{1,2},{2,1},{3,0},{4,7},{5,6},{6,5},{7,4},{8,11},{9,10},{10,... | collective-permute-start | bytes 98312 | tf_op jit(solution)/shard_map/ppermute | solution.py:177
  15.1 2.1 %collective-permute-start.6 = (f32[16,512]{1,0:T(8,128)S(1)}, f32[16,512]{1,0:T(8,128)S(1)}, u32[]{:S(2)}, u32[]{:S(2)}) collective-permute-start(f32[16,512]{1,0:T(8,128)S(1)} %pad_maximum_fusion), channel_id=1, source_target_pairs={{0,1},{1,0},{2,3},{3,2},{4,5},{5,4},{6,7},{7,6},{8,9},{9,8},{10,11... | collective-permute-start | bytes 98312 | tf_op jit(solution)/shard_map/ppermute | solution.py:167

commit v8 on v7

--- a/solution.py
+++ b/solution.py
@@ -10,7 +10,10 @@
 SLAB_DEV = 8
 ROWS = 8
 RADIX = 4
-STEPS = ((2, 3, 1, 0), (3, 2, 0, 1), (1, 0, 3, 2))
+ROUNDS = (
+    ((2, 3, 1, 0), (3, 2, 0, 1), (1, 0, 3, 2)),
+    ((2, 0, 3, 1), (1, 3, 0, 2), (3, 2, 1, 0)),
+)
 CHUNK = 256
 MIB = 1 << 20
 
@@ -106,8 +109,8 @@
     hi_ref[...], lo_ref[...] = split(jnp.concatenate(cols, axis=0).T, 2)
 
 
-def by_digit(parts, place):
-    from_place = [[here] + [step.index(here) for step in STEPS] for here in range(RADIX)]
+def by_digit(parts, place, steps):
+    from_place = [[here] + [step.index(here) for step in steps] for here in range(RADIX)]
     out = []
     for source in range(RADIX):
         part = parts[from_place[0].index(source)]
@@ -131,7 +134,7 @@
         for j in range(len(parts)):
             if j // low % RADIX == 0:
                 held = [j + k * low for k in range(RADIX)]
-                for at, part in zip(held, by_digit([parts[at] for at in held], place)):
+                for at, part in zip(held, by_digit([parts[at] for at in held], place, ROUNDS[i % len(ROUNDS)])):
                     parts[at] = part
     held = {sum(s * (j // RADIX**i % RADIX) for i, s in enumerate(strides)): j for j in range(len(parts))}
     out_ref[...] = chi_ref[...] + jnp.concatenate([parts[held[w]] for w in range(len(parts))], axis=0)
@@ -205,13 +208,14 @@
     )(cond_orb, e_cond[None, :], pair_cond, v)
     columns = [own] + [exchange(own, n) for n in range(1, n_narrow)]
     got = [sent]
-    for stride in strides:
-        if stride == strides[0]:
-            got = [own_block] + [between_chips(sent, step, stride) for step in STEPS]
+    for i, stride in enumerate(strides):
+        steps = ROUNDS[i % len(ROUNDS)]
+        if i == 0:
+            got = [own_block] + [between_chips(sent, step, stride) for step in steps]
             *got, own = lax.optimization_barrier((*got, own))
         else:
             sent = jnp.concatenate(got, axis=0)
-            got = [between_chips(sent, step, stride) for step in STEPS]
+            got = [between_chips(sent, step, stride) for step in steps]
             sent, got[0] = lax.optimization_barrier((sent, got[0]))
             got = [exchange(sent, across)] + got
     terms = pl.pallas_call(

time: 18.2 us -> 18.3 us (level)
  transfers between devices with their start and end apart: 9 -> 9, of which waited for: 6 -> 5; matrix products, arithmetic and copies ran while one was open for 0% -> 0% of each run, Pallas kernels for 12% -> 12%
where the time goes in v8:
time: 18.3 us; the launch traced here: 18.1 us
  starting transfers between devices  10.5 us (57%)
  Pallas kernels  4.51 us (25%)
  waiting for transfers between devices  3.02 us (17%)
    ppermute x6, starting transfers between devices, between_chips(): return lax.ppermute(x, ('wide', 'narrow'), pairs_of)  9.42 us
    ppermute x6, waiting for transfers between devices, between_chips(): return lax.ppermute(x, ('wide', 'narrow'), pairs_of)  2.18 us
    pallas_call x1, Pallas kernels, shards(): pl.pallas_call(slab_kernel, in_specs=[hbm] * 4, out_specs=vmem, out_shape...  1.52 us
    ppermute x3, starting transfers between devices, exchange(): return lax.ppermute(x, 'narrow', [(i, i ^ bit) for i in range(n_narrow)])  1.04 us
    pallas_call x1, Pallas kernels, shards(): pl.pallas_call(dens_kernel, in_specs=[vmem] * 4, out_specs=vmem, out_shap...  0.96 us
    pallas_call x1, Pallas kernels, shards(): pl.pallas_call(val_kernel, in_specs=[vmem] * 3, out_specs=vmem, out_shape...  0.94 us
    pallas_call x1, Pallas kernels, shards(): pl.pallas_call(functools.partial(product_kernel, tuple(strides), row_sub)...  0.88 us
    ppermute x3, waiting for transfers between devices, exchange(): return lax.ppermute(x, 'narrow', [(i, i ^ bit) for i in range(n_narrow)])  0.84 us
  transfers between devices with their start and end apart: 9, of which 5 were waited for; matrix products, arithmetic and copies ran while one was open for 0% of the time, Pallas kernels for 12%

profile of v8, /device:TPU:0, one launch (start us, length us, event | category | flops | bytes accessed | tf_op | source)
XLA Modules:
  0.0 18.1 jit_solution(13360975157227664899)
XLA Ops:
  0.0 0.0 copy-start.5
  0.0 0.0 copy-start
  0.0 0.0 copy-start.3
  0.0 1.5 %slab_rows.1 = f32[2,4,512]{2,1,0:T(4,128)S(1)} custom-call(f32[80,4096]{1,0:T(8,128)} %val_ref.3, f32[80,4096]{1,0:T(8,128)} %cond_ref.3, s32[1,512]{1,0:T(1,128)} %pv_ref.2, s32[1,512]{1,0:T(1,128)} %pc_ref.2), custom_call_target="tpu_custom_call" | custom-call | tf_op jit(solution)/shard_map/slab_rows/pallas_call | solution.py:153
  1.5 0.0 copy-start.1
  1.5 0.0 copy-start.4
  1.6 0.0 copy-start.6
  1.6 0.5 %collective-permute-start = (f32[2,4,512]{2,1,0:T(4,128)S(1)}, f32[2,4,512]{2,1,0:T(4,128)S(1)}, u32[]{:S(2)}, u32[]{:S(2)}) collective-permute-start(f32[2,4,512]{2,1,0:T(4,128)S(1)} %slab_rows.1), channel_id=1, source_target_pairs={{0,1},{1,0},{2,3},{3,2},{4,5},{5,4},{6,7},{7,6},{8,9},{9,8},{10,11... | collective-permute-start | bytes 49160 | tf_op jit(solution)/shard_map/ppermute | solution.py:170
  2.1 0.8 %collective-permute-done = f32[2,4,512]{2,1,0:T(4,128)S(1)} collective-permute-done((f32[2,4,512]{2,1,0:T(4,128)S(1)}, f32[2,4,512]{2,1,0:T(4,128)S(1)}, u32[]{:S(2)}, u32[]{:S(2)}) %collective-permute-start) | collective-permute-done | bytes 16416 | tf_op jit(solution)/shard_map/ppermute | solution.py:170
  2.9 3.7 %collective-permute-start.2 = (f32[4,512]{1,0:T(4,128)S(1)}, f32[4,512]{1,0:T(4,128)S(1)}, u32[]{:S(2)}, u32[]{:S(2)}) collective-permute-start(f32[4,512]{1,0:T(4,128)S(1)} %get-tuple-element.20), channel_id=1, source_target_pairs={{0,17},{1,16},{2,19},{3,18},{4,21},{5,20},{6,23},{7,22},{8,25},{9,... | collective-permute-start | bytes 24584 | tf_op jit(solution)/shard_map/ppermute | solution.py:180
  6.6 1.1 %collective-permute-start.3 = (f32[4,512]{1,0:T(4,128)S(1)}, f32[4,512]{1,0:T(4,128)S(1)}, u32[]{:S(2)}, u32[]{:S(2)}) collective-permute-start(f32[4,512]{1,0:T(4,128)S(1)} %get-tuple-element.20), channel_id=1, source_target_pairs={{0,25},{1,24},{2,27},{3,26},{4,29},{5,28},{6,31},{7,30},{8,17},{9,... | collective-permute-start | bytes 24584 | tf_op jit(solution)/shard_map/ppermute | solution.py:180
  7.7 0.5 %collective-permute-start.4 = (f32[4,512]{1,0:T(4,128)S(1)}, f32[4,512]{1,0:T(4,128)S(1)}, u32[]{:S(2)}, u32[]{:S(2)}) collective-permute-start(f32[4,512]{1,0:T(4,128)S(1)} %get-tuple-element.20), channel_id=1, source_target_pairs={{0,9},{1,8},{2,11},{3,10},{4,13},{5,12},{6,15},{7,14},{8,1},{9,0},... | collective-permute-start | bytes 24584 | tf_op jit(solution)/shard_map/ppermute | solution.py:180
  8.2 0.0 copy-done.5
  8.2 0.0 copy-done
  8.2 0.0 copy-done.3
  8.2 0.9 %val_columns.1.v_ref = f32[88,512]{1,0:T(8,128)S(1)} custom-call(f32[80,4096]{1,0:T(8,128)S(1)} %copy-done, f32[1,4096]{1,0:T(1,128)S(1)} %bitcast.9, s32[1,512]{1,0:T(1,128)S(1)} %copy-done.5), custom_call_target="tpu_custom_call" | custom-call | tf_op jit(solution)/shard_map/val_columns/pallas_call | solution.py:193
  9.1 0.0 copy-start.2
  9.1 0.0 copy-done.1
  9.1 0.0 copy-done.4
  9.2 0.0 copy-done.6
  9.2 1.0 %densities.1.refs_0_ = f32[80,512]{1,0:T(8,128)S(1)} custom-call(f32[80,4096]{1,0:T(8,128)S(1)} %copy-done.1, f32[1,4096]{1,0:T(1,128)S(1)} %bitcast.10, s32[1,512]{1,0:T(1,128)S(1)} %copy-done.6, f32[88,512]{1,0:T(8,128)S(1)} %val_columns.1.v_ref), custom_call_target="tpu_custom_call" | custom-call | tf_op jit(solution)/shard_map/densities/pallas_call | solution.py:201
  10.1 0.2 %collective-permute-start.1 = (f32[80,512]{1,0:T(8,128)S(1)}, f32[80,512]{1,0:T(8,128)S(1)}, u32[]{:S(2)}, u32[]{:S(2)}) collective-permute-start(f32[80,512]{1,0:T(8,128)S(1)} %densities.1.refs_0_), channel_id=1, source_target_pairs={{0,1},{1,0},{2,3},{3,2},{4,5},{5,4},{6,7},{7,6},{8,9},{9,8},{10,11... | collective-permute-start | bytes 491528 | tf_op jit(solution)/shard_map/ppermute | solution.py:170
  10.4 0.0 collective-permute-done.2
  10.4 0.2 %collective-permute-done.3 = f32[4,512]{1,0:T(4,128)S(1)} collective-permute-done((f32[4,512]{1,0:T(4,128)S(1)}, f32[4,512]{1,0:T(4,128)S(1)}, u32[]{:S(2)}, u32[]{:S(2)}) %collective-permute-start.3) | collective-permute-done | bytes 8224 | tf_op jit(solution)/shard_map/ppermute | solution.py:180
  10.6 0.2 collective-permute-done.4
  10.8 1.5 %collective-permute-start.5 = (f32[16,512]{1,0:T(8,128)S(1)}, f32[16,512]{1,0:T(8,128)S(1)}, u32[]{:S(2)}, u32[]{:S(2)}) collective-permute-start(f32[16,512]{1,0:T(8,128)S(1)} %pad_maximum_fusion), channel_id=1, source_target_pairs={{0,5},{1,4},{2,1},{3,0},{4,7},{5,6},{6,3},{7,2},{8,13},{9,12},{10,... | collective-permute-start | bytes 98312 | tf_op jit(solution)/shard_map/ppermute | solution.py:180
  12.3 0.3 %collective-permute-start.7 = (f32[16,512]{1,0:T(8,128)S(1)}, f32[16,512]{1,0:T(8,128)S(1)}, u32[]{:S(2)}, u32[]{:S(2)}) collective-permute-start(f32[16,512]{1,0:T(8,128)S(1)} %pad_maximum_fusion), channel_id=1, source_target_pairs={{0,3},{1,2},{2,7},{3,6},{4,1},{5,0},{6,5},{7,4},{8,11},{9,10},{10,... | collective-permute-start | bytes 98312 | tf_op jit(solution)/shard_map/ppermute | solution.py:180
  12.6 2.4 %collective-permute-start.8 = (f32[16,512]{1,0:T(8,128)S(1)}, f32[16,512]{1,0:T(8,128)S(1)}, u32[]{:S(2)}, u32[]{:S(2)}) collective-permute-start(f32[16,512]{1,0:T(8,128)S(1)} %pad_maximum_fusion), channel_id=1, source_target_pairs={{0,7},{1,6},{2,5},{3,4},{4,3},{5,2},{6,1},{7,0},{8,15},{9,14},{10,... | collective-permute-start | bytes 98312 | tf_op jit(solution)/shard_map/ppermute | solution.py:180
  15.0 0.0 collective-permute-done.5.refs_1_
  15.0 0.3 %collective-permute-start.6 = (f32[16,512]{1,0:T(8,128)S(1)}, f32[16,512]{1,0:T(8,128)S(1)}, u32[]{:S(2)}, u32[]{:S(2)}) collective-permute-start(f32[16,512]{1,0:T(8,128)S(1)} %pad_maximum_fusion), channel_id=1, source_target_pairs={{0,1},{1,0},{2,3},{3,2},{4,5},{5,4},{6,7},{7,6},{8,9},{9,8},{10,11... | collective-permute-start | bytes 98312 | tf_op jit(solution)/shard_map/ppermute | solution.py:170
  15.3 0.0 collective-permute-done.1.refs_1_
  15.3 0.2 %columns.1 = (bf16[512,160]{1,0:T(8,128)(2,1)S(1)}, bf16[512,160]{1,0:T(8,128)(2,1)S(1)}) custom-call(f32[80,512]{1,0:T(8,128)S(1)} %densities.1.refs_0_, f32[80,512]{1,0:T(8,128)S(1)} %collective-permute-done.1.refs_1_), custom_call_target="tpu_custom_call" | custom-call | tf_op jit(solution)/shard_map/columns/pallas_call | solution.py:221
  15.5 0.2 collective-permute-done.7.refs_2_
  15.7 1.6 %collective-permute-done.8.refs_3_ = f32[16,512]{1,0:T(8,128)S(1)} collective-permute-done((f32[16,512]{1,0:T(8,128)S(1)}, f32[16,512]{1,0:T(8,128)S(1)}, u32[]{:S(2)}, u32[]{:S(2)}) %collective-permute-start.8) | collective-permute-done | bytes 32800 | tf_op jit(solution)/shard_map/ppermute | solution.py:180
  17.3 0.0 collective-permute-done.6.refs_0_
  17.3 0.0 copy-done.2
  17.3 0.9 %product.1 = f32[64,160]{1,0:T(8,128)} custom-call(f32[64,160]{1,0:T(8,128)S(1)} %bitcast.8, bf16[512,160]{1,0:T(8,128)(2,1)S(1)} %get-tuple-element.18.hi_ref, bf16[512,160]{1,0:T(8,128)(2,1)S(1)} %get-tuple-element.19.lo_ref, f32[16,512]{1,0:T(8,128)S(1)} %collective-permute-done.6.refs_0_, f32[16,512]{1,0:T(8,128)S(1)} %collective-permute-done.5.refs_1_, ...), custom_call_target="tpu_custom_call" | custom-call | tf_op jit(solution)/shard_map/product/pallas_call | solution.py:229
  (2 shorter events, 0.0 us)
Async XLA Ops:
  0.0 8.2 %copy-start.5 = (s32[1,512]{1,0:T(1,128)S(1)}, s32[1,512]{1,0:T(1,128)}, u32[]{:S(2)}) copy-start(s32[1,512]{1,0:T(1,128)} %pv_ref.2) | copy-start | bytes 6148
  0.0 8.2 %copy-start = (f32[80,4096]{1,0:T(8,128)S(1)}, f32[80,4096]{1,0:T(8,128)}, u32[]{:S(2)}) copy-start(f32[80,4096]{1,0:T(8,128)} %val_ref.3) | copy-start | bytes 3932164
  0.0 8.2 %copy-start.3 = (f32[4096]{0:T(1024)S(1)}, f32[4096]{0:T(1024)}, u32[]{:S(2)}) copy-start(f32[4096]{0:T(1024)} %param.10) | copy-start | bytes 49156
  1.5 7.6 %copy-start.1 = (f32[80,4096]{1,0:T(8,128)S(1)}, f32[80,4096]{1,0:T(8,128)}, u32[]{:S(2)}) copy-start(f32[80,4096]{1,0:T(8,128)} %cond_ref.3) | copy-start | bytes 3932164
  1.5 7.6 %copy-start.4 = (f32[4096]{0:T(1024)S(1)}, f32[4096]{0:T(1024)}, u32[]{:S(2)}) copy-start(f32[4096]{0:T(1024)} %param.11) | copy-start | bytes 49156
  1.6 7.6 %copy-start.6 = (s32[1,512]{1,0:T(1,128)S(1)}, s32[1,512]{1,0:T(1,128)}, u32[]{:S(2)}) copy-start(s32[1,512]{1,0:T(1,128)} %pc_ref.2) | copy-start | bytes 6148
  1.6 1.4 %collective-permute-start = (f32[2,4,512]{2,1,0:T(4,128)S(1)}, f32[2,4,512]{2,1,0:T(4,128)S(1)}, u32[]{:S(2)}, u32[]{:S(2)}) collective-permute-start(f32[2,4,512]{2,1,0:T(4,128)S(1)} %slab_rows.1), channel_id=1, source_target_pairs={{0,1},{1,0},{2,3},{3,2},{4,5},{5,4},{6,7},{7,6},{8,9},{9,8},{10,11... | collective-permute-start | bytes 49160 | tf_op jit(solution)/shard_map/ppermute | solution.py:170
  2.9 7.4 %collective-permute-start.2 = (f32[4,512]{1,0:T(4,128)S(1)}, f32[4,512]{1,0:T(4,128)S(1)}, u32[]{:S(2)}, u32[]{:S(2)}) collective-permute-start(f32[4,512]{1,0:T(4,128)S(1)} %get-tuple-element.20), channel_id=1, source_target_pairs={{0,17},{1,16},{2,19},{3,18},{4,21},{5,20},{6,23},{7,22},{8,25},{9,... | collective-permute-start | bytes 24584 | tf_op jit(solution)/shard_map/ppermute | solution.py:180
  6.6 4.0 %collective-permute-start.3 = (f32[4,512]{1,0:T(4,128)S(1)}, f32[4,512]{1,0:T(4,128)S(1)}, u32[]{:S(2)}, u32[]{:S(2)}) collective-permute-start(f32[4,512]{1,0:T(4,128)S(1)} %get-tuple-element.20), channel_id=1, source_target_pairs={{0,25},{1,24},{2,27},{3,26},{4,29},{5,28},{6,31},{7,30},{8,17},{9,... | collective-permute-start | bytes 24584 | tf_op jit(solution)/shard_map/ppermute | solution.py:180
  7.7 3.1 %collective-permute-start.4 = (f32[4,512]{1,0:T(4,128)S(1)}, f32[4,512]{1,0:T(4,128)S(1)}, u32[]{:S(2)}, u32[]{:S(2)}) collective-permute-start(f32[4,512]{1,0:T(4,128)S(1)} %get-tuple-element.20), channel_id=1, source_target_pairs={{0,9},{1,8},{2,11},{3,10},{4,13},{5,12},{6,15},{7,14},{8,1},{9,0},... | collective-permute-start | bytes 24584 | tf_op jit(solution)/shard_map/ppermute | solution.py:180
  9.1 8.1 %copy-start.2 = (f32[160,64]{0,1:T(8,128)S(1)}, f32[160,64]{0,1:T(8,128)}, u32[]{:S(2)}) copy-start(f32[160,64]{0,1:T(8,128)} %param.7) | copy-start | bytes 122884
  10.1 5.1 %collective-permute-start.1 = (f32[80,512]{1,0:T(8,128)S(1)}, f32[80,512]{1,0:T(8,128)S(1)}, u32[]{:S(2)}, u32[]{:S(2)}) collective-permute-start(f32[80,512]{1,0:T(8,128)S(1)} %densities.1.refs_0_), channel_id=1, source_target_pairs={{0,1},{1,0},{2,3},{3,2},{4,5},{5,4},{6,7},{7,6},{8,9},{9,8},{10,11... | collective-permute-start | bytes 491528 | tf_op jit(solution)/shard_map/ppermute | solution.py:170
  10.8 4.2 %collective-permute-start.5 = (f32[16,512]{1,0:T(8,128)S(1)}, f32[16,512]{1,0:T(8,128)S(1)}, u32[]{:S(2)}, u32[]{:S(2)}) collective-permute-start(f32[16,512]{1,0:T(8,128)S(1)} %pad_maximum_fusion), channel_id=1, source_target_pairs={{0,5},{1,4},{2,1},{3,0},{4,7},{5,6},{6,3},{7,2},{8,13},{9,12},{10,... | collective-permute-start | bytes 98312 | tf_op jit(solution)/shard_map/ppermute | solution.py:180
  12.3 3.3 %collective-permute-start.7 = (f32[16,512]{1,0:T(8,128)S(1)}, f32[16,512]{1,0:T(8,128)S(1)}, u32[]{:S(2)}, u32[]{:S(2)}) collective-permute-start(f32[16,512]{1,0:T(8,128)S(1)} %pad_maximum_fusion), channel_id=1, source_target_pairs={{0,3},{1,2},{2,7},{3,6},{4,1},{5,0},{6,5},{7,4},{8,11},{9,10},{10,... | collective-permute-start | bytes 98312 | tf_op jit(solution)/shard_map/ppermute | solution.py:180
  12.6 4.7 %collective-permute-start.8 = (f32[16,512]{1,0:T(8,128)S(1)}, f32[16,512]{1,0:T(8,128)S(1)}, u32[]{:S(2)}, u32[]{:S(2)}) collective-permute-start(f32[16,512]{1,0:T(8,128)S(1)} %pad_maximum_fusion), channel_id=1, source_target_pairs={{0,7},{1,6},{2,5},{3,4},{4,3},{5,2},{6,1},{7,0},{8,15},{9,14},{10,... | collective-permute-start | bytes 98312 | tf_op jit(solution)/shard_map/ppermute | solution.py:180
  15.0 2.3 %collective-permute-start.6 = (f32[16,512]{1,0:T(8,128)S(1)}, f32[16,512]{1,0:T(8,128)S(1)}, u32[]{:S(2)}, u32[]{:S(2)}) collective-permute-start(f32[16,512]{1,0:T(8,128)S(1)} %pad_maximum_fusion), channel_id=1, source_target_pairs={{0,1},{1,0},{2,3},{3,2},{4,5},{5,4},{6,7},{7,6},{8,9},{9,8},{10,11... | collective-permute-start | bytes 98312 | tf_op jit(solution)/shard_map/ppermute | solution.py:170

commit v9 on v8

--- a/solution.py
+++ b/solution.py
@@ -12,7 +12,7 @@
 RADIX = 4
 ROUNDS = (
     ((2, 3, 1, 0), (3, 2, 0, 1), (1, 0, 3, 2)),
-    ((2, 0, 3, 1), (1, 3, 0, 2), (3, 2, 1, 0)),
+    ((3, 2, 1, 0), (1, 0, 3, 2), (2, 3, 0, 1)),
 )
 CHUNK = 256
 MIB = 1 << 20

time: 18.3 us -> 18.1 us (0.989)
  starting transfers between devices: 10.5 us -> 9.56 us
  waiting for transfers between devices: 3.02 us -> 3.68 us
    ppermute x6, starting transfers between devices: 9.42 us -> 8.45 us  [between_chips(): return lax.ppermute(x, ('wide', 'narrow'), pairs_of)]
    ppermute x6, waiting for transfers between devices: 2.18 us -> 2.84 us  [between_chips(): return lax.ppermute(x, ('wide', 'narrow'), pairs_of)]
  transfers between devices with their start and end apart: 9 -> 9, of which waited for: 5 -> 6; matrix products, arithmetic and copies ran while one was open for 0% -> 0% of each run, Pallas kernels for 12% -> 12%
where the time goes in v9:
time: 18.1 us; the launch traced here: 17.9 us
  starting transfers between devices  9.56 us (53%)
  Pallas kernels  4.51 us (25%)
  waiting for transfers between devices  3.68 us (20%)
    ppermute x6, starting transfers between devices, between_chips(): return lax.ppermute(x, ('wide', 'narrow'), pairs_of)  8.45 us
    ppermute x6, waiting for transfers between devices, between_chips(): return lax.ppermute(x, ('wide', 'narrow'), pairs_of)  2.84 us
    pallas_call x1, Pallas kernels, shards(): pl.pallas_call(slab_kernel, in_specs=[hbm] * 4, out_specs=vmem, out_shape...  1.52 us
    ppermute x3, starting transfers between devices, exchange(): return lax.ppermute(x, 'narrow', [(i, i ^ bit) for i in range(n_narrow)])  1.11 us
    pallas_call x1, Pallas kernels, shards(): pl.pallas_call(dens_kernel, in_specs=[vmem] * 4, out_specs=vmem, out_shap...  0.96 us
    pallas_call x1, Pallas kernels, shards(): pl.pallas_call(val_kernel, in_specs=[vmem] * 3, out_specs=vmem, out_shape...  0.94 us
    pallas_call x1, Pallas kernels, shards(): pl.pallas_call(functools.partial(product_kernel, tuple(strides), row_sub)...  0.88 us
    ppermute x3, waiting for transfers between devices, exchange(): return lax.ppermute(x, 'narrow', [(i, i ^ bit) for i in range(n_narrow)])  0.84 us
  transfers between devices with their start and end apart: 9, of which 6 were waited for; matrix products, arithmetic and copies ran while one was open for 0% of the time, Pallas kernels for 12%

profile of v9, /device:TPU:0, one launch (start us, length us, event | category | flops | bytes accessed | tf_op | source)
XLA Modules:
  0.0 17.9 jit_solution(13498283142554727390)
XLA Ops:
  0.0 0.0 copy-start.5
  0.0 0.0 copy-start
  0.0 0.0 copy-start.3
  0.0 1.5 %slab_rows.1 = f32[2,4,512]{2,1,0:T(4,128)S(1)} custom-call(f32[80,4096]{1,0:T(8,128)} %val_ref.3, f32[80,4096]{1,0:T(8,128)} %cond_ref.3, s32[1,512]{1,0:T(1,128)} %pv_ref.2, s32[1,512]{1,0:T(1,128)} %pc_ref.2), custom_call_target="tpu_custom_call" | custom-call | tf_op jit(solution)/shard_map/slab_rows/pallas_call | solution.py:153
  1.5 0.0 copy-start.1
  1.5 0.0 copy-start.4
  1.6 0.0 copy-start.6
  1.6 0.5 %collective-permute-start = (f32[2,4,512]{2,1,0:T(4,128)S(1)}, f32[2,4,512]{2,1,0:T(4,128)S(1)}, u32[]{:S(2)}, u32[]{:S(2)}) collective-permute-start(f32[2,4,512]{2,1,0:T(4,128)S(1)} %slab_rows.1), channel_id=1, source_target_pairs={{0,1},{1,0},{2,3},{3,2},{4,5},{5,4},{6,7},{7,6},{8,9},{9,8},{10,11... | collective-permute-start | bytes 49160 | tf_op jit(solution)/shard_map/ppermute | solution.py:170
  2.1 0.8 %collective-permute-done = f32[2,4,512]{2,1,0:T(4,128)S(1)} collective-permute-done((f32[2,4,512]{2,1,0:T(4,128)S(1)}, f32[2,4,512]{2,1,0:T(4,128)S(1)}, u32[]{:S(2)}, u32[]{:S(2)}) %collective-permute-start) | collective-permute-done | bytes 16416 | tf_op jit(solution)/shard_map/ppermute | solution.py:170
  2.9 3.7 %collective-permute-start.2 = (f32[4,512]{1,0:T(4,128)S(1)}, f32[4,512]{1,0:T(4,128)S(1)}, u32[]{:S(2)}, u32[]{:S(2)}) collective-permute-start(f32[4,512]{1,0:T(4,128)S(1)} %get-tuple-element.20), channel_id=1, source_target_pairs={{0,17},{1,16},{2,19},{3,18},{4,21},{5,20},{6,23},{7,22},{8,25},{9,... | collective-permute-start | bytes 24584 | tf_op jit(solution)/shard_map/ppermute | solution.py:180
  6.6 1.1 %collective-permute-start.3 = (f32[4,512]{1,0:T(4,128)S(1)}, f32[4,512]{1,0:T(4,128)S(1)}, u32[]{:S(2)}, u32[]{:S(2)}) collective-permute-start(f32[4,512]{1,0:T(4,128)S(1)} %get-tuple-element.20), channel_id=1, source_target_pairs={{0,25},{1,24},{2,27},{3,26},{4,29},{5,28},{6,31},{7,30},{8,17},{9,... | collective-permute-start | bytes 24584 | tf_op jit(solution)/shard_map/ppermute | solution.py:180
  7.7 0.5 %collective-permute-start.4 = (f32[4,512]{1,0:T(4,128)S(1)}, f32[4,512]{1,0:T(4,128)S(1)}, u32[]{:S(2)}, u32[]{:S(2)}) collective-permute-start(f32[4,512]{1,0:T(4,128)S(1)} %get-tuple-element.20), channel_id=1, source_target_pairs={{0,9},{1,8},{2,11},{3,10},{4,13},{5,12},{6,15},{7,14},{8,1},{9,0},... | collective-permute-start | bytes 24584 | tf_op jit(solution)/shard_map/ppermute | solution.py:180
  8.2 0.0 copy-done.5
  8.2 0.0 copy-done
  8.2 0.0 copy-done.3
  8.2 0.9 %val_columns.1.v_ref = f32[88,512]{1,0:T(8,128)S(1)} custom-call(f32[80,4096]{1,0:T(8,128)S(1)} %copy-done, f32[1,4096]{1,0:T(1,128)S(1)} %bitcast.9, s32[1,512]{1,0:T(1,128)S(1)} %copy-done.5), custom_call_target="tpu_custom_call" | custom-call | tf_op jit(solution)/shard_map/val_columns/pallas_call | solution.py:193
  9.1 0.0 copy-start.2
  9.1 0.0 copy-done.1
  9.1 0.0 copy-done.4
  9.2 0.0 copy-done.6
  9.2 1.0 %densities.1.refs_0_ = f32[80,512]{1,0:T(8,128)S(1)} custom-call(f32[80,4096]{1,0:T(8,128)S(1)} %copy-done.1, f32[1,4096]{1,0:T(1,128)S(1)} %bitcast.10, s32[1,512]{1,0:T(1,128)S(1)} %copy-done.6, f32[88,512]{1,0:T(8,128)S(1)} %val_columns.1.v_ref), custom_call_target="tpu_custom_call" | custom-call | tf_op jit(solution)/shard_map/densities/pallas_call | solution.py:201
  10.1 0.2 %collective-permute-start.1 = (f32[80,512]{1,0:T(8,128)S(1)}, f32[80,512]{1,0:T(8,128)S(1)}, u32[]{:S(2)}, u32[]{:S(2)}) collective-permute-start(f32[80,512]{1,0:T(8,128)S(1)} %densities.1.refs_0_), channel_id=1, source_target_pairs={{0,1},{1,0},{2,3},{3,2},{4,5},{5,4},{6,7},{7,6},{8,9},{9,8},{10,11... | collective-permute-start | bytes 491528 | tf_op jit(solution)/shard_map/ppermute | solution.py:170
  10.4 0.0 collective-permute-done.2
  10.4 0.2 %collective-permute-done.3 = f32[4,512]{1,0:T(4,128)S(1)} collective-permute-done((f32[4,512]{1,0:T(4,128)S(1)}, f32[4,512]{1,0:T(4,128)S(1)}, u32[]{:S(2)}, u32[]{:S(2)}) %collective-permute-start.3) | collective-permute-done | bytes 8224 | tf_op jit(solution)/shard_map/ppermute | solution.py:180
  10.6 0.2 collective-permute-done.4
  10.8 2.5 %collective-permute-start.5 = (f32[16,512]{1,0:T(8,128)S(1)}, f32[16,512]{1,0:T(8,128)S(1)}, u32[]{:S(2)}, u32[]{:S(2)}) collective-permute-start(f32[16,512]{1,0:T(8,128)S(1)} %pad_maximum_fusion), channel_id=1, source_target_pairs={{0,7},{1,6},{2,5},{3,4},{4,3},{5,2},{6,1},{7,0},{8,15},{9,14},{10,... | collective-permute-start | bytes 98312 | tf_op jit(solution)/shard_map/ppermute | solution.py:180
  13.3 0.4 %collective-permute-start.7 = (f32[16,512]{1,0:T(8,128)S(1)}, f32[16,512]{1,0:T(8,128)S(1)}, u32[]{:S(2)}, u32[]{:S(2)}) collective-permute-start(f32[16,512]{1,0:T(8,128)S(1)} %pad_maximum_fusion), channel_id=1, source_target_pairs={{0,3},{1,2},{2,1},{3,0},{4,7},{5,6},{6,5},{7,4},{8,11},{9,10},{10,... | collective-permute-start | bytes 98312 | tf_op jit(solution)/shard_map/ppermute | solution.py:180
  13.7 0.3 %collective-permute-start.8 = (f32[16,512]{1,0:T(8,128)S(1)}, f32[16,512]{1,0:T(8,128)S(1)}, u32[]{:S(2)}, u32[]{:S(2)}) collective-permute-start(f32[16,512]{1,0:T(8,128)S(1)} %pad_maximum_fusion), channel_id=1, source_target_pairs={{0,5},{1,4},{2,7},{3,6},{4,1},{5,0},{6,3},{7,2},{8,13},{9,12},{10,... | collective-permute-start | bytes 98312 | tf_op jit(solution)/shard_map/ppermute | solution.py:180
  14.0 1.1 %collective-permute-done.5.refs_1_ = f32[16,512]{1,0:T(8,128)S(1)} collective-permute-done((f32[16,512]{1,0:T(8,128)S(1)}, f32[16,512]{1,0:T(8,128)S(1)}, u32[]{:S(2)}, u32[]{:S(2)}) %collective-permute-start.5) | collective-permute-done | bytes 32800 | tf_op jit(solution)/shard_map/ppermute | solution.py:180
  15.1 0.3 %collective-permute-start.6 = (f32[16,512]{1,0:T(8,128)S(1)}, f32[16,512]{1,0:T(8,128)S(1)}, u32[]{:S(2)}, u32[]{:S(2)}) collective-permute-start(f32[16,512]{1,0:T(8,128)S(1)} %pad_maximum_fusion), channel_id=1, source_target_pairs={{0,1},{1,0},{2,3},{3,2},{4,5},{5,4},{6,7},{7,6},{8,9},{9,8},{10,11... | collective-permute-start | bytes 98312 | tf_op jit(solution)/shard_map/ppermute | solution.py:170
  15.5 0.0 collective-permute-done.1.refs_1_
  15.5 0.2 %columns.1 = (bf16[512,160]{1,0:T(8,128)(2,1)S(1)}, bf16[512,160]{1,0:T(8,128)(2,1)S(1)}) custom-call(f32[80,512]{1,0:T(8,128)S(1)} %densities.1.refs_0_, f32[80,512]{1,0:T(8,128)S(1)} %collective-permute-done.1.refs_1_), custom_call_target="tpu_custom_call" | custom-call | tf_op jit(solution)/shard_map/columns/pallas_call | solution.py:221
  15.7 0.9 %collective-permute-done.7.refs_2_ = f32[16,512]{1,0:T(8,128)S(1)} collective-permute-done((f32[16,512]{1,0:T(8,128)S(1)}, f32[16,512]{1,0:T(8,128)S(1)}, u32[]{:S(2)}, u32[]{:S(2)}) %collective-permute-start.7) | collective-permute-done | bytes 32800 | tf_op jit(solution)/shard_map/ppermute | solution.py:180
  16.6 0.4 %collective-permute-done.8.refs_3_ = f32[16,512]{1,0:T(8,128)S(1)} collective-permute-done((f32[16,512]{1,0:T(8,128)S(1)}, f32[16,512]{1,0:T(8,128)S(1)}, u32[]{:S(2)}, u32[]{:S(2)}) %collective-permute-start.8) | collective-permute-done | bytes 32800 | tf_op jit(solution)/shard_map/ppermute | solution.py:180
  17.0 0.0 collective-permute-done.6.refs_0_
  17.0 0.0 copy-done.2
  17.0 0.9 %product.1 = f32[64,160]{1,0:T(8,128)} custom-call(f32[64,160]{1,0:T(8,128)S(1)} %bitcast.8, bf16[512,160]{1,0:T(8,128)(2,1)S(1)} %get-tuple-element.18.hi_ref, bf16[512,160]{1,0:T(8,128)(2,1)S(1)} %get-tuple-element.19.lo_ref, f32[16,512]{1,0:T(8,128)S(1)} %collective-permute-done.6.refs_0_, f32[16,512]{1,0:T(8,128)S(1)} %collective-permute-done.5.refs_1_, ...), custom_call_target="tpu_custom_call" | custom-call | tf_op jit(solution)/shard_map/product/pallas_call | solution.py:229
  (2 shorter events, 0.0 us)
Async XLA Ops:
  0.0 8.2 %copy-start.5 = (s32[1,512]{1,0:T(1,128)S(1)}, s32[1,512]{1,0:T(1,128)}, u32[]{:S(2)}) copy-start(s32[1,512]{1,0:T(1,128)} %pv_ref.2) | copy-start | bytes 6148
  0.0 8.2 %copy-start = (f32[80,4096]{1,0:T(8,128)S(1)}, f32[80,4096]{1,0:T(8,128)}, u32[]{:S(2)}) copy-start(f32[80,4096]{1,0:T(8,128)} %val_ref.3) | copy-start | bytes 3932164
  0.0 8.2 %copy-start.3 = (f32[4096]{0:T(1024)S(1)}, f32[4096]{0:T(1024)}, u32[]{:S(2)}) copy-start(f32[4096]{0:T(1024)} %param.10) | copy-start | bytes 49156
  1.5 7.6 %copy-start.1 = (f32[80,4096]{1,0:T(8,128)S(1)}, f32[80,4096]{1,0:T(8,128)}, u32[]{:S(2)}) copy-start(f32[80,4096]{1,0:T(8,128)} %cond_ref.3) | copy-start | bytes 3932164
  1.5 7.6 %copy-start.4 = (f32[4096]{0:T(1024)S(1)}, f32[4096]{0:T(1024)}, u32[]{:S(2)}) copy-start(f32[4096]{0:T(1024)} %param.11) | copy-start | bytes 49156
  1.6 7.6 %copy-start.6 = (s32[1,512]{1,0:T(1,128)S(1)}, s32[1,512]{1,0:T(1,128)}, u32[]{:S(2)}) copy-start(s32[1,512]{1,0:T(1,128)} %pc_ref.2) | copy-start | bytes 6148
  1.6 1.4 %collective-permute-start = (f32[2,4,512]{2,1,0:T(4,128)S(1)}, f32[2,4,512]{2,1,0:T(4,128)S(1)}, u32[]{:S(2)}, u32[]{:S(2)}) collective-permute-start(f32[2,4,512]{2,1,0:T(4,128)S(1)} %slab_rows.1), channel_id=1, source_target_pairs={{0,1},{1,0},{2,3},{3,2},{4,5},{5,4},{6,7},{7,6},{8,9},{9,8},{10,11... | collective-permute-start | bytes 49160 | tf_op jit(solution)/shard_map/ppermute | solution.py:170
  2.9 7.4 %collective-permute-start.2 = (f32[4,512]{1,0:T(4,128)S(1)}, f32[4,512]{1,0:T(4,128)S(1)}, u32[]{:S(2)}, u32[]{:S(2)}) collective-permute-start(f32[4,512]{1,0:T(4,128)S(1)} %get-tuple-element.20), channel_id=1, source_target_pairs={{0,17},{1,16},{2,19},{3,18},{4,21},{5,20},{6,23},{7,22},{8,25},{9,... | collective-permute-start | bytes 24584 | tf_op jit(solution)/shard_map/ppermute | solution.py:180
  6.6 4.0 %collective-permute-start.3 = (f32[4,512]{1,0:T(4,128)S(1)}, f32[4,512]{1,0:T(4,128)S(1)}, u32[]{:S(2)}, u32[]{:S(2)}) collective-permute-start(f32[4,512]{1,0:T(4,128)S(1)} %get-tuple-element.20), channel_id=1, source_target_pairs={{0,25},{1,24},{2,27},{3,26},{4,29},{5,28},{6,31},{7,30},{8,17},{9,... | collective-permute-start | bytes 24584 | tf_op jit(solution)/shard_map/ppermute | solution.py:180
  7.7 3.1 %collective-permute-start.4 = (f32[4,512]{1,0:T(4,128)S(1)}, f32[4,512]{1,0:T(4,128)S(1)}, u32[]{:S(2)}, u32[]{:S(2)}) collective-permute-start(f32[4,512]{1,0:T(4,128)S(1)} %get-tuple-element.20), channel_id=1, source_target_pairs={{0,9},{1,8},{2,11},{3,10},{4,13},{5,12},{6,15},{7,14},{8,1},{9,0},... | collective-permute-start | bytes 24584 | tf_op jit(solution)/shard_map/ppermute | solution.py:180
  9.1 7.9 %copy-start.2 = (f32[160,64]{0,1:T(8,128)S(1)}, f32[160,64]{0,1:T(8,128)}, u32[]{:S(2)}) copy-start(f32[160,64]{0,1:T(8,128)} %param.7) | copy-start | bytes 122884
  10.1 5.3 %collective-permute-start.1 = (f32[80,512]{1,0:T(8,128)S(1)}, f32[80,512]{1,0:T(8,128)S(1)}, u32[]{:S(2)}, u32[]{:S(2)}) collective-permute-start(f32[80,512]{1,0:T(8,128)S(1)} %densities.1.refs_0_), channel_id=1, source_target_pairs={{0,1},{1,0},{2,3},{3,2},{4,5},{5,4},{6,7},{7,6},{8,9},{9,8},{10,11... | collective-permute-start | bytes 491528 | tf_op jit(solution)/shard_map/ppermute | solution.py:170
  10.8 4.3 %collective-permute-start.5 = (f32[16,512]{1,0:T(8,128)S(1)}, f32[16,512]{1,0:T(8,128)S(1)}, u32[]{:S(2)}, u32[]{:S(2)}) collective-permute-start(f32[16,512]{1,0:T(8,128)S(1)} %pad_maximum_fusion), channel_id=1, source_target_pairs={{0,7},{1,6},{2,5},{3,4},{4,3},{5,2},{6,1},{7,0},{8,15},{9,14},{10,... | collective-permute-start | bytes 98312 | tf_op jit(solution)/shard_map/ppermute | solution.py:180
  13.3 3.3 %collective-permute-start.7 = (f32[16,512]{1,0:T(8,128)S(1)}, f32[16,512]{1,0:T(8,128)S(1)}, u32[]{:S(2)}, u32[]{:S(2)}) collective-permute-start(f32[16,512]{1,0:T(8,128)S(1)} %pad_maximum_fusion), channel_id=1, source_target_pairs={{0,3},{1,2},{2,1},{3,0},{4,7},{5,6},{6,5},{7,4},{8,11},{9,10},{10,... | collective-permute-start | bytes 98312 | tf_op jit(solution)/shard_map/ppermute | solution.py:180
  13.7 3.3 %collective-permute-start.8 = (f32[16,512]{1,0:T(8,128)S(1)}, f32[16,512]{1,0:T(8,128)S(1)}, u32[]{:S(2)}, u32[]{:S(2)}) collective-permute-start(f32[16,512]{1,0:T(8,128)S(1)} %pad_maximum_fusion), channel_id=1, source_target_pairs={{0,5},{1,4},{2,7},{3,6},{4,1},{5,0},{6,3},{7,2},{8,13},{9,12},{10,... | collective-permute-start | bytes 98312 | tf_op jit(solution)/shard_map/ppermute | solution.py:180
  15.1 1.9 %collective-permute-start.6 = (f32[16,512]{1,0:T(8,128)S(1)}, f32[16,512]{1,0:T(8,128)S(1)}, u32[]{:S(2)}, u32[]{:S(2)}) collective-permute-start(f32[16,512]{1,0:T(8,128)S(1)} %pad_maximum_fusion), channel_id=1, source_target_pairs={{0,1},{1,0},{2,3},{3,2},{4,5},{5,4},{6,7},{7,6},{8,9},{9,8},{10,11... | collective-permute-start | bytes 98312 | tf_op jit(solution)/shard_map/ppermute | solution.py:170

commit v10 on v9

--- a/solution.py
+++ b/solution.py
@@ -48,10 +48,10 @@
 
 
 def pick_few(rows, hot, idx):
-    terms = split(by_chunk(rows, CHUNK), 2)
+    terms = split(by_chunk(rows, 2 * CHUNK), 2)
     m = terms[0].shape[0]
     every = jnp.dot(jnp.concatenate(terms, axis=0), hot, preferred_element_type=jnp.float32)
-    return own_chunk(every[:m] + every[m:], idx, CHUNK, rows.shape[0])
+    return own_chunk(every[:m] + every[m:], idx, 2 * CHUNK, rows.shape[0])
 
 
 def pick_many(rows, idx):
@@ -67,9 +67,9 @@
     for copy in copies:
         copy.start(priority=1)
     copies[0].wait()
-    hot_v = one_hot(pv[...], CHUNK)
+    hot_v = one_hot(pv[...], 2 * CHUNK)
     copies[1].wait()
-    hot_c = one_hot(pc[...], CHUNK)
+    hot_c = one_hot(pc[...], 2 * CHUNK)
     copies[2].wait()
     dens = pick_few(val[...], hot_v, pv[...])
     copies[3].wait()
@@ -120,24 +120,17 @@
     return out
 
 
-def product_kernel(strides, sub, chi_ref, hi_ref, lo_ref, *refs):
+def product_kernel(stride, steps, sub, chi_ref, hi_ref, lo_ref, *refs):
     *rows_refs, out_ref = refs
     s_hi, s_lo = split(jnp.concatenate([ref[...] for ref in rows_refs], axis=0), 2)
     m = s_hi.shape[0]
     by_hi = jnp.dot(jnp.concatenate([s_hi, s_lo], axis=0), hi_ref[...], preferred_element_type=jnp.float32)
     by_lo = jnp.dot(s_hi, lo_ref[...], preferred_element_type=jnp.float32)
     total = by_hi[:m] + (by_hi[m:] + by_lo)
-    wide = lax.axis_index("wide")
-    parts = [total[at : at + sub] for at in range(0, m, sub)]
-    for i, stride in enumerate(strides):
-        place, low = lax.rem(lax.div(wide, stride), RADIX), RADIX**i
-        for j in range(len(parts)):
-            if j // low % RADIX == 0:
-                held = [j + k * low for k in range(RADIX)]
-                for at, part in zip(held, by_digit([parts[at] for at in held], place, ROUNDS[i % len(ROUNDS)])):
-                    parts[at] = part
-    held = {sum(s * (j // RADIX**i % RADIX) for i, s in enumerate(strides)): j for j in range(len(parts))}
-    out_ref[...] = chi_ref[...] + jnp.concatenate([parts[held[w]] for w in range(len(parts))], axis=0)
+    place, each = lax.rem(lax.div(lax.axis_index("wide"), stride), RADIX), m // len(rows_refs)
+    parts = by_digit([total[at : at + each] for at in range(0, m, each)], place, steps)
+    rows = [part[at : at + sub] for at in range(0, each, sub) for part in parts]
+    out_ref[...] = chi_ref[...] + jnp.concatenate(rows, axis=0)
 
 
 def in_hbm(x):
@@ -178,6 +171,14 @@
             to = w + (step[place] - place) * stride
             pairs_of += [(w * n_narrow + n, to * n_narrow + (n ^ across)) for n in range(n_narrow)]
         return lax.ppermute(x, ("wide", "narrow"), pairs_of)
+
+    def in_order(blocks, stride, steps):
+        blocks = by_digit(blocks, lax.rem(lax.div(lax.axis_index("wide"), stride), RADIX), steps)
+        groups = blocks[0].shape[0] // row_sub
+        if groups == 1:
+            return jnp.concatenate(blocks, axis=0)
+        joined = jnp.stack([block.reshape(groups, row_sub, pairs) for block in blocks], axis=1)
+        return joined.reshape(-1, pairs)
 
     strides = []
     while RADIX ** (len(strides) + 1) <= n_wide:
@@ -214,7 +215,7 @@
             got = [own_block] + [between_chips(sent, step, stride) for step in steps]
             *got, own = lax.optimization_barrier((*got, own))
         else:
-            sent = jnp.concatenate(got, axis=0)
+            sent = in_order(got, strides[i - 1], ROUNDS[(i - 1) % len(ROUNDS)])
             got = [between_chips(sent, step, stride) for step in steps]
             sent, got[0] = lax.optimization_barrier((sent, got[0]))
             got = [exchange(sent, across)] + got
@@ -227,7 +228,7 @@
         name="columns",
     )(*columns)
     out = pl.pallas_call(
-        functools.partial(product_kernel, tuple(strides), row_sub),
+        functools.partial(product_kernel, strides[-1], ROUNDS[(len(strides) - 1) % len(ROUNDS)], row_sub),
         in_specs=[vmem] * (3 + len(got)),
         out_specs=vmem,
         out_shape=jax.ShapeDtypeStruct(chi_in.shape[::-1], jnp.float32),

time: 18.1 us -> 18.1 us (level)
  no operation moved by 1% of the time
where the time goes in v10:
time: 18.1 us; the launch traced here: 18 us
  starting transfers between devices  9.56 us (53%)
  Pallas kernels  4.55 us (25%)
  waiting for transfers between devices  3.69 us (20%)
    ppermute x6, starting transfers between devices, between_chips(): return lax.ppermute(x, ('wide', 'narrow'), pairs_of)  8.45 us
    ppermute x6, waiting for transfers between devices, between_chips(): return lax.ppermute(x, ('wide', 'narrow'), pairs_of)  2.84 us
    pallas_call x1, Pallas kernels, shards(): pl.pallas_call(slab_kernel, in_specs=[hbm] * 4, out_specs=vmem, out_shape...  1.57 us
    ppermute x3, starting transfers between devices, exchange(): return lax.ppermute(x, 'narrow', [(i, i ^ bit) for i in range(n_narrow)])  1.1 us
    pallas_call x1, Pallas kernels, shards(): pl.pallas_call(dens_kernel, in_specs=[vmem] * 4, out_specs=vmem, out_shap...  0.96 us
    pallas_call x1, Pallas kernels, shards(): pl.pallas_call(val_kernel, in_specs=[vmem] * 3, out_specs=vmem, out_shape...  0.94 us
    pallas_call x1, Pallas kernels, shards(): pl.pallas_call(functools.partial(product_kernel, strides[-1], ROUNDS[(len...  0.86 us
    ppermute x3, waiting for transfers between devices, exchange(): return lax.ppermute(x, 'narrow', [(i, i ^ bit) for i in range(n_narrow)])  0.84 us
  transfers between devices with their start and end apart: 9, of which 6 were waited for; matrix products, arithmetic and copies ran while one was open for 0% of the time, Pallas kernels for 12%

profile of v10, /device:TPU:0, one launch (start us, length us, event | category | flops | bytes accessed | tf_op | source)
XLA Modules:
  0.0 18.0 jit_solution(6310230783007192488)
XLA Ops:
  0.0 0.0 copy-start.5
  0.0 0.0 copy-start
  0.0 0.0 copy-start.3
  0.0 1.6 %slab_rows.1 = f32[2,4,512]{2,1,0:T(4,128)S(1)} custom-call(f32[80,4096]{1,0:T(8,128)} %val_ref.3, f32[80,4096]{1,0:T(8,128)} %cond_ref.3, s32[1,512]{1,0:T(1,128)} %pv_ref.2, s32[1,512]{1,0:T(1,128)} %pc_ref.2), custom_call_target="tpu_custom_call" | custom-call | tf_op jit(solution)/shard_map/slab_rows/pallas_call | solution.py:146
  1.6 0.0 copy-start.1
  1.6 0.0 copy-start.4
  1.6 0.0 copy-start.6
  1.6 0.5 %collective-permute-start = (f32[2,4,512]{2,1,0:T(4,128)S(1)}, f32[2,4,512]{2,1,0:T(4,128)S(1)}, u32[]{:S(2)}, u32[]{:S(2)}) collective-permute-start(f32[2,4,512]{2,1,0:T(4,128)S(1)} %slab_rows.1), channel_id=1, source_target_pairs={{0,1},{1,0},{2,3},{3,2},{4,5},{5,4},{6,7},{7,6},{8,9},{9,8},{10,11... | collective-permute-start | bytes 49160 | tf_op jit(solution)/shard_map/ppermute | solution.py:163
  2.2 0.8 %collective-permute-done = f32[2,4,512]{2,1,0:T(4,128)S(1)} collective-permute-done((f32[2,4,512]{2,1,0:T(4,128)S(1)}, f32[2,4,512]{2,1,0:T(4,128)S(1)}, u32[]{:S(2)}, u32[]{:S(2)}) %collective-permute-start) | collective-permute-done | bytes 16416 | tf_op jit(solution)/shard_map/ppermute | solution.py:163
  3.0 3.7 %collective-permute-start.2 = (f32[4,512]{1,0:T(4,128)S(1)}, f32[4,512]{1,0:T(4,128)S(1)}, u32[]{:S(2)}, u32[]{:S(2)}) collective-permute-start(f32[4,512]{1,0:T(4,128)S(1)} %get-tuple-element.20), channel_id=1, source_target_pairs={{0,17},{1,16},{2,19},{3,18},{4,21},{5,20},{6,23},{7,22},{8,25},{9,... | collective-permute-start | bytes 24584 | tf_op jit(solution)/shard_map/ppermute | solution.py:173
  6.7 1.1 %collective-permute-start.3 = (f32[4,512]{1,0:T(4,128)S(1)}, f32[4,512]{1,0:T(4,128)S(1)}, u32[]{:S(2)}, u32[]{:S(2)}) collective-permute-start(f32[4,512]{1,0:T(4,128)S(1)} %get-tuple-element.20), channel_id=1, source_target_pairs={{0,25},{1,24},{2,27},{3,26},{4,29},{5,28},{6,31},{7,30},{8,17},{9,... | collective-permute-start | bytes 24584 | tf_op jit(solution)/shard_map/ppermute | solution.py:173
  7.8 0.5 %collective-permute-start.4 = (f32[4,512]{1,0:T(4,128)S(1)}, f32[4,512]{1,0:T(4,128)S(1)}, u32[]{:S(2)}, u32[]{:S(2)}) collective-permute-start(f32[4,512]{1,0:T(4,128)S(1)} %get-tuple-element.20), channel_id=1, source_target_pairs={{0,9},{1,8},{2,11},{3,10},{4,13},{5,12},{6,15},{7,14},{8,1},{9,0},... | collective-permute-start | bytes 24584 | tf_op jit(solution)/shard_map/ppermute | solution.py:173
  8.2 0.0 copy-done.5
  8.2 0.0 copy-done
  8.2 0.0 copy-done.3
  8.2 0.9 %val_columns.1.v_ref = f32[88,512]{1,0:T(8,128)S(1)} custom-call(f32[80,4096]{1,0:T(8,128)S(1)} %copy-done, f32[1,4096]{1,0:T(1,128)S(1)} %bitcast.9, s32[1,512]{1,0:T(1,128)S(1)} %copy-done.5), custom_call_target="tpu_custom_call" | custom-call | tf_op jit(solution)/shard_map/val_columns/pallas_call | solution.py:194
  9.2 0.0 copy-start.2
  9.2 0.0 copy-done.1
  9.2 0.0 copy-done.4
  9.2 0.0 copy-done.6
  9.2 1.0 %densities.1.refs_0_ = f32[80,512]{1,0:T(8,128)S(1)} custom-call(f32[80,4096]{1,0:T(8,128)S(1)} %copy-done.1, f32[1,4096]{1,0:T(1,128)S(1)} %bitcast.10, s32[1,512]{1,0:T(1,128)S(1)} %copy-done.6, f32[88,512]{1,0:T(8,128)S(1)} %val_columns.1.v_ref), custom_call_target="tpu_custom_call" | custom-call | tf_op jit(solution)/shard_map/densities/pallas_call | solution.py:202
  10.2 0.2 %collective-permute-start.1 = (f32[80,512]{1,0:T(8,128)S(1)}, f32[80,512]{1,0:T(8,128)S(1)}, u32[]{:S(2)}, u32[]{:S(2)}) collective-permute-start(f32[80,512]{1,0:T(8,128)S(1)} %densities.1.refs_0_), channel_id=1, source_target_pairs={{0,1},{1,0},{2,3},{3,2},{4,5},{5,4},{6,7},{7,6},{8,9},{9,8},{10,11... | collective-permute-start | bytes 491528 | tf_op jit(solution)/shard_map/ppermute | solution.py:163
  10.4 0.0 collective-permute-done.2
  10.4 0.2 %collective-permute-done.3 = f32[4,512]{1,0:T(4,128)S(1)} collective-permute-done((f32[4,512]{1,0:T(4,128)S(1)}, f32[4,512]{1,0:T(4,128)S(1)}, u32[]{:S(2)}, u32[]{:S(2)}) %collective-permute-start.3) | collective-permute-done | bytes 8224 | tf_op jit(solution)/shard_map/ppermute | solution.py:173
  10.7 0.2 collective-permute-done.4
  10.9 2.5 %collective-permute-start.5 = (f32[16,512]{1,0:T(8,128)S(1)}, f32[16,512]{1,0:T(8,128)S(1)}, u32[]{:S(2)}, u32[]{:S(2)}) collective-permute-start(f32[16,512]{1,0:T(8,128)S(1)} %pad_maximum_fusion), channel_id=1, source_target_pairs={{0,7},{1,6},{2,5},{3,4},{4,3},{5,2},{6,1},{7,0},{8,15},{9,14},{10,... | collective-permute-start | bytes 98312 | tf_op jit(solution)/shard_map/ppermute | solution.py:173
  13.3 0.4 %collective-permute-start.7 = (f32[16,512]{1,0:T(8,128)S(1)}, f32[16,512]{1,0:T(8,128)S(1)}, u32[]{:S(2)}, u32[]{:S(2)}) collective-permute-start(f32[16,512]{1,0:T(8,128)S(1)} %pad_maximum_fusion), channel_id=1, source_target_pairs={{0,3},{1,2},{2,1},{3,0},{4,7},{5,6},{6,5},{7,4},{8,11},{9,10},{10,... | collective-permute-start | bytes 98312 | tf_op jit(solution)/shard_map/ppermute | solution.py:173
  13.8 0.3 %collective-permute-start.8 = (f32[16,512]{1,0:T(8,128)S(1)}, f32[16,512]{1,0:T(8,128)S(1)}, u32[]{:S(2)}, u32[]{:S(2)}) collective-permute-start(f32[16,512]{1,0:T(8,128)S(1)} %pad_maximum_fusion), channel_id=1, source_target_pairs={{0,5},{1,4},{2,7},{3,6},{4,1},{5,0},{6,3},{7,2},{8,13},{9,12},{10,... | collective-permute-start | bytes 98312 | tf_op jit(solution)/shard_map/ppermute | solution.py:173
  14.1 1.1 %collective-permute-done.5.refs_1_ = f32[16,512]{1,0:T(8,128)S(1)} collective-permute-done((f32[16,512]{1,0:T(8,128)S(1)}, f32[16,512]{1,0:T(8,128)S(1)}, u32[]{:S(2)}, u32[]{:S(2)}) %collective-permute-start.5) | collective-permute-done | bytes 32800 | tf_op jit(solution)/shard_map/ppermute | solution.py:173
  15.2 0.3 %collective-permute-start.6 = (f32[16,512]{1,0:T(8,128)S(1)}, f32[16,512]{1,0:T(8,128)S(1)}, u32[]{:S(2)}, u32[]{:S(2)}) collective-permute-start(f32[16,512]{1,0:T(8,128)S(1)} %pad_maximum_fusion), channel_id=1, source_target_pairs={{0,1},{1,0},{2,3},{3,2},{4,5},{5,4},{6,7},{7,6},{8,9},{9,8},{10,11... | collective-permute-start | bytes 98312 | tf_op jit(solution)/shard_map/ppermute | solution.py:163
  15.5 0.0 collective-permute-done.1.refs_1_
  15.5 0.2 %columns.1 = (bf16[512,160]{1,0:T(8,128)(2,1)S(1)}, bf16[512,160]{1,0:T(8,128)(2,1)S(1)}) custom-call(f32[80,512]{1,0:T(8,128)S(1)} %densities.1.refs_0_, f32[80,512]{1,0:T(8,128)S(1)} %collective-permute-done.1.refs_1_), custom_call_target="tpu_custom_call" | custom-call | tf_op jit(solution)/shard_map/columns/pallas_call | solution.py:222
  15.8 0.9 %collective-permute-done.7.refs_2_ = f32[16,512]{1,0:T(8,128)S(1)} collective-permute-done((f32[16,512]{1,0:T(8,128)S(1)}, f32[16,512]{1,0:T(8,128)S(1)}, u32[]{:S(2)}, u32[]{:S(2)}) %collective-permute-start.7) | collective-permute-done | bytes 32800 | tf_op jit(solution)/shard_map/ppermute | solution.py:173
  16.7 0.4 %collective-permute-done.8.refs_3_ = f32[16,512]{1,0:T(8,128)S(1)} collective-permute-done((f32[16,512]{1,0:T(8,128)S(1)}, f32[16,512]{1,0:T(8,128)S(1)}, u32[]{:S(2)}, u32[]{:S(2)}) %collective-permute-start.8) | collective-permute-done | bytes 32800 | tf_op jit(solution)/shard_map/ppermute | solution.py:173
  17.1 0.0 collective-permute-done.6.refs_0_
  17.1 0.0 copy-done.2
  17.1 0.9 %product.1 = f32[64,160]{1,0:T(8,128)} custom-call(f32[64,160]{1,0:T(8,128)S(1)} %bitcast.8, bf16[512,160]{1,0:T(8,128)(2,1)S(1)} %get-tuple-element.18.hi_ref, bf16[512,160]{1,0:T(8,128)(2,1)S(1)} %get-tuple-element.19.lo_ref, f32[16,512]{1,0:T(8,128)S(1)} %collective-permute-done.6.refs_0_, f32[16,512]{1,0:T(8,128)S(1)} %collective-permute-done.5.refs_1_, ...), custom_call_target="tpu_custom_call" | custom-call | tf_op jit(solution)/shard_map/product/pallas_call | solution.py:230
  (3 shorter events, 0.0 us)
Async XLA Ops:
  0.0 8.2 %copy-start.5 = (s32[1,512]{1,0:T(1,128)S(1)}, s32[1,512]{1,0:T(1,128)}, u32[]{:S(2)}) copy-start(s32[1,512]{1,0:T(1,128)} %pv_ref.2) | copy-start | bytes 6148
  0.0 8.2 %copy-start = (f32[80,4096]{1,0:T(8,128)S(1)}, f32[80,4096]{1,0:T(8,128)}, u32[]{:S(2)}) copy-start(f32[80,4096]{1,0:T(8,128)} %val_ref.3) | copy-start | bytes 3932164
  0.0 8.2 %copy-start.3 = (f32[4096]{0:T(1024)S(1)}, f32[4096]{0:T(1024)}, u32[]{:S(2)}) copy-start(f32[4096]{0:T(1024)} %param.10) | copy-start | bytes 49156
  1.6 7.6 %copy-start.1 = (f32[80,4096]{1,0:T(8,128)S(1)}, f32[80,4096]{1,0:T(8,128)}, u32[]{:S(2)}) copy-start(f32[80,4096]{1,0:T(8,128)} %cond_ref.3) | copy-start | bytes 3932164
  1.6 7.6 %copy-start.4 = (f32[4096]{0:T(1024)S(1)}, f32[4096]{0:T(1024)}, u32[]{:S(2)}) copy-start(f32[4096]{0:T(1024)} %param.11) | copy-start | bytes 49156
  1.6 7.6 %copy-start.6 = (s32[1,512]{1,0:T(1,128)S(1)}, s32[1,512]{1,0:T(1,128)}, u32[]{:S(2)}) copy-start(s32[1,512]{1,0:T(1,128)} %pc_ref.2) | copy-start | bytes 6148
  1.6 1.4 %collective-permute-start = (f32[2,4,512]{2,1,0:T(4,128)S(1)}, f32[2,4,512]{2,1,0:T(4,128)S(1)}, u32[]{:S(2)}, u32[]{:S(2)}) collective-permute-start(f32[2,4,512]{2,1,0:T(4,128)S(1)} %slab_rows.1), channel_id=1, source_target_pairs={{0,1},{1,0},{2,3},{3,2},{4,5},{5,4},{6,7},{7,6},{8,9},{9,8},{10,11... | collective-permute-start | bytes 49160 | tf_op jit(solution)/shard_map/ppermute | solution.py:163
  3.0 7.4 %collective-permute-start.2 = (f32[4,512]{1,0:T(4,128)S(1)}, f32[4,512]{1,0:T(4,128)S(1)}, u32[]{:S(2)}, u32[]{:S(2)}) collective-permute-start(f32[4,512]{1,0:T(4,128)S(1)} %get-tuple-element.20), channel_id=1, source_target_pairs={{0,17},{1,16},{2,19},{3,18},{4,21},{5,20},{6,23},{7,22},{8,25},{9,... | collective-permute-start | bytes 24584 | tf_op jit(solution)/shard_map/ppermute | solution.py:173
  6.7 4.0 %collective-permute-start.3 = (f32[4,512]{1,0:T(4,128)S(1)}, f32[4,512]{1,0:T(4,128)S(1)}, u32[]{:S(2)}, u32[]{:S(2)}) collective-permute-start(f32[4,512]{1,0:T(4,128)S(1)} %get-tuple-element.20), channel_id=1, source_target_pairs={{0,25},{1,24},{2,27},{3,26},{4,29},{5,28},{6,31},{7,30},{8,17},{9,... | collective-permute-start | bytes 24584 | tf_op jit(solution)/shard_map/ppermute | solution.py:173
  7.8 3.1 %collective-permute-start.4 = (f32[4,512]{1,0:T(4,128)S(1)}, f32[4,512]{1,0:T(4,128)S(1)}, u32[]{:S(2)}, u32[]{:S(2)}) collective-permute-start(f32[4,512]{1,0:T(4,128)S(1)} %get-tuple-element.20), channel_id=1, source_target_pairs={{0,9},{1,8},{2,11},{3,10},{4,13},{5,12},{6,15},{7,14},{8,1},{9,0},... | collective-permute-start | bytes 24584 | tf_op jit(solution)/shard_map/ppermute | solution.py:173
  9.2 7.9 %copy-start.2 = (f32[160,64]{0,1:T(8,128)S(1)}, f32[160,64]{0,1:T(8,128)}, u32[]{:S(2)}) copy-start(f32[160,64]{0,1:T(8,128)} %param.7) | copy-start | bytes 122884
  10.2 5.3 %collective-permute-start.1 = (f32[80,512]{1,0:T(8,128)S(1)}, f32[80,512]{1,0:T(8,128)S(1)}, u32[]{:S(2)}, u32[]{:S(2)}) collective-permute-start(f32[80,512]{1,0:T(8,128)S(1)} %densities.1.refs_0_), channel_id=1, source_target_pairs={{0,1},{1,0},{2,3},{3,2},{4,5},{5,4},{6,7},{7,6},{8,9},{9,8},{10,11... | collective-permute-start | bytes 491528 | tf_op jit(solution)/shard_map/ppermute | solution.py:163
  10.9 4.3 %collective-permute-start.5 = (f32[16,512]{1,0:T(8,128)S(1)}, f32[16,512]{1,0:T(8,128)S(1)}, u32[]{:S(2)}, u32[]{:S(2)}) collective-permute-start(f32[16,512]{1,0:T(8,128)S(1)} %pad_maximum_fusion), channel_id=1, source_target_pairs={{0,7},{1,6},{2,5},{3,4},{4,3},{5,2},{6,1},{7,0},{8,15},{9,14},{10,... | collective-permute-start | bytes 98312 | tf_op jit(solution)/shard_map/ppermute | solution.py:173
  13.3 3.3 %collective-permute-start.7 = (f32[16,512]{1,0:T(8,128)S(1)}, f32[16,512]{1,0:T(8,128)S(1)}, u32[]{:S(2)}, u32[]{:S(2)}) collective-permute-start(f32[16,512]{1,0:T(8,128)S(1)} %pad_maximum_fusion), channel_id=1, source_target_pairs={{0,3},{1,2},{2,1},{3,0},{4,7},{5,6},{6,5},{7,4},{8,11},{9,10},{10,... | collective-permute-start | bytes 98312 | tf_op jit(solution)/shard_map/ppermute | solution.py:173
  13.8 3.3 %collective-permute-start.8 = (f32[16,512]{1,0:T(8,128)S(1)}, f32[16,512]{1,0:T(8,128)S(1)}, u32[]{:S(2)}, u32[]{:S(2)}) collective-permute-start(f32[16,512]{1,0:T(8,128)S(1)} %pad_maximum_fusion), channel_id=1, source_target_pairs={{0,5},{1,4},{2,7},{3,6},{4,1},{5,0},{6,3},{7,2},{8,13},{9,12},{10,... | collective-permute-start | bytes 98312 | tf_op jit(solution)/shard_map/ppermute | solution.py:173
  15.2 1.9 %collective-permute-start.6 = (f32[16,512]{1,0:T(8,128)S(1)}, f32[16,512]{1,0:T(8,128)S(1)}, u32[]{:S(2)}, u32[]{:S(2)}) collective-permute-start(f32[16,512]{1,0:T(8,128)S(1)} %pad_maximum_fusion), channel_id=1, source_target_pairs={{0,1},{1,0},{2,3},{3,2},{4,5},{5,4},{6,7},{7,6},{8,9},{9,8},{10,11... | collective-permute-start | bytes 98312 | tf_op jit(solution)/shard_map/ppermute | solution.py:163

commit v11 on v10

--- a/solution.py
+++ b/solution.py
@@ -48,10 +48,10 @@
 
 
 def pick_few(rows, hot, idx):
-    terms = split(by_chunk(rows, 2 * CHUNK), 2)
+    terms = split(by_chunk(rows, CHUNK), 2)
     m = terms[0].shape[0]
     every = jnp.dot(jnp.concatenate(terms, axis=0), hot, preferred_element_type=jnp.float32)
-    return own_chunk(every[:m] + every[m:], idx, 2 * CHUNK, rows.shape[0])
+    return own_chunk(every[:m] + every[m:], idx, CHUNK, rows.shape[0])
 
 
 def pick_many(rows, idx):
@@ -67,9 +67,9 @@
     for copy in copies:
         copy.start(priority=1)
     copies[0].wait()
-    hot_v = one_hot(pv[...], 2 * CHUNK)
+    hot_v = one_hot(pv[...], CHUNK)
     copies[1].wait()
-    hot_c = one_hot(pc[...], 2 * CHUNK)
+    hot_c = one_hot(pc[...], CHUNK)
     copies[2].wait()
     dens = pick_few(val[...], hot_v, pv[...])
     copies[3].wait()

time: 18.1 us -> 18.1 us (level)
  no operation moved by 1% of the time
where the time goes in v11:
time: 18.1 us; the launch traced here: 17.9 us
  starting transfers between devices  9.56 us (53%)
  Pallas kernels  4.49 us (25%)
  waiting for transfers between devices  3.68 us (20%)
    ppermute x6, starting transfers between devices, between_chips(): return lax.ppermute(x, ('wide', 'narrow'), pairs_of)  8.45 us
    ppermute x6, waiting for transfers between devices, between_chips(): return lax.ppermute(x, ('wide', 'narrow'), pairs_of)  2.84 us
    pallas_call x1, Pallas kernels, shards(): pl.pallas_call(slab_kernel, in_specs=[hbm] * 4, out_specs=vmem, out_shape...  1.52 us
    ppermute x3, starting transfers between devices, exchange(): return lax.ppermute(x, 'narrow', [(i, i ^ bit) for i in range(n_narrow)])  1.11 us
    pallas_call x1, Pallas kernels, shards(): pl.pallas_call(dens_kernel, in_specs=[vmem] * 4, out_specs=vmem, out_shap...  0.96 us
    pallas_call x1, Pallas kernels, shards(): pl.pallas_call(val_kernel, in_specs=[vmem] * 3, out_specs=vmem, out_shape...  0.94 us
    pallas_call x1, Pallas kernels, shards(): pl.pallas_call(functools.partial(product_kernel, strides[-1], ROUNDS[(len...  0.86 us
    ppermute x3, waiting for transfers between devices, exchange(): return lax.ppermute(x, 'narrow', [(i, i ^ bit) for i in range(n_narrow)])  0.84 us
  transfers between devices with their start and end apart: 9, of which 6 were waited for; matrix products, arithmetic and copies ran while one was open for 0% of the time, Pallas kernels for 12%

profile of v11, /device:TPU:0, one launch (start us, length us, event | category | flops | bytes accessed | tf_op | source)
XLA Modules:
  0.0 17.9 jit_solution(2872561603315601013)
XLA Ops:
  0.0 0.0 copy-start.5
  0.0 0.0 copy-start
  0.0 0.0 copy-start.3
  0.0 1.5 %slab_rows.1 = f32[2,4,512]{2,1,0:T(4,128)S(1)} custom-call(f32[80,4096]{1,0:T(8,128)} %val_ref.3, f32[80,4096]{1,0:T(8,128)} %cond_ref.3, s32[1,512]{1,0:T(1,128)} %pv_ref.2, s32[1,512]{1,0:T(1,128)} %pc_ref.2), custom_call_target="tpu_custom_call" | custom-call | tf_op jit(solution)/shard_map/slab_rows/pallas_call | solution.py:146
  1.5 0.0 copy-start.1
  1.5 0.0 copy-start.4
  1.6 0.0 copy-start.6
  1.6 0.5 %collective-permute-start = (f32[2,4,512]{2,1,0:T(4,128)S(1)}, f32[2,4,512]{2,1,0:T(4,128)S(1)}, u32[]{:S(2)}, u32[]{:S(2)}) collective-permute-start(f32[2,4,512]{2,1,0:T(4,128)S(1)} %slab_rows.1), channel_id=1, source_target_pairs={{0,1},{1,0},{2,3},{3,2},{4,5},{5,4},{6,7},{7,6},{8,9},{9,8},{10,11... | collective-permute-start | bytes 49160 | tf_op jit(solution)/shard_map/ppermute | solution.py:163
  2.1 0.8 %collective-permute-done = f32[2,4,512]{2,1,0:T(4,128)S(1)} collective-permute-done((f32[2,4,512]{2,1,0:T(4,128)S(1)}, f32[2,4,512]{2,1,0:T(4,128)S(1)}, u32[]{:S(2)}, u32[]{:S(2)}) %collective-permute-start) | collective-permute-done | bytes 16416 | tf_op jit(solution)/shard_map/ppermute | solution.py:163
  2.9 3.7 %collective-permute-start.2 = (f32[4,512]{1,0:T(4,128)S(1)}, f32[4,512]{1,0:T(4,128)S(1)}, u32[]{:S(2)}, u32[]{:S(2)}) collective-permute-start(f32[4,512]{1,0:T(4,128)S(1)} %get-tuple-element.20), channel_id=1, source_target_pairs={{0,17},{1,16},{2,19},{3,18},{4,21},{5,20},{6,23},{7,22},{8,25},{9,... | collective-permute-start | bytes 24584 | tf_op jit(solution)/shard_map/ppermute | solution.py:173
  6.6 1.1 %collective-permute-start.3 = (f32[4,512]{1,0:T(4,128)S(1)}, f32[4,512]{1,0:T(4,128)S(1)}, u32[]{:S(2)}, u32[]{:S(2)}) collective-permute-start(f32[4,512]{1,0:T(4,128)S(1)} %get-tuple-element.20), channel_id=1, source_target_pairs={{0,25},{1,24},{2,27},{3,26},{4,29},{5,28},{6,31},{7,30},{8,17},{9,... | collective-permute-start | bytes 24584 | tf_op jit(solution)/shard_map/ppermute | solution.py:173
  7.7 0.5 %collective-permute-start.4 = (f32[4,512]{1,0:T(4,128)S(1)}, f32[4,512]{1,0:T(4,128)S(1)}, u32[]{:S(2)}, u32[]{:S(2)}) collective-permute-start(f32[4,512]{1,0:T(4,128)S(1)} %get-tuple-element.20), channel_id=1, source_target_pairs={{0,9},{1,8},{2,11},{3,10},{4,13},{5,12},{6,15},{7,14},{8,1},{9,0},... | collective-permute-start | bytes 24584 | tf_op jit(solution)/shard_map/ppermute | solution.py:173
  8.2 0.0 copy-done.5
  8.2 0.0 copy-done
  8.2 0.0 copy-done.3
  8.2 0.9 %val_columns.1.v_ref = f32[88,512]{1,0:T(8,128)S(1)} custom-call(f32[80,4096]{1,0:T(8,128)S(1)} %copy-done, f32[1,4096]{1,0:T(1,128)S(1)} %bitcast.9, s32[1,512]{1,0:T(1,128)S(1)} %copy-done.5), custom_call_target="tpu_custom_call" | custom-call | tf_op jit(solution)/shard_map/val_columns/pallas_call | solution.py:194
  9.1 0.0 copy-start.2
  9.1 0.0 copy-done.1
  9.1 0.0 copy-done.4
  9.2 0.0 copy-done.6
  9.2 1.0 %densities.1.refs_0_ = f32[80,512]{1,0:T(8,128)S(1)} custom-call(f32[80,4096]{1,0:T(8,128)S(1)} %copy-done.1, f32[1,4096]{1,0:T(1,128)S(1)} %bitcast.10, s32[1,512]{1,0:T(1,128)S(1)} %copy-done.6, f32[88,512]{1,0:T(8,128)S(1)} %val_columns.1.v_ref), custom_call_target="tpu_custom_call" | custom-call | tf_op jit(solution)/shard_map/densities/pallas_call | solution.py:202
  10.1 0.2 %collective-permute-start.1 = (f32[80,512]{1,0:T(8,128)S(1)}, f32[80,512]{1,0:T(8,128)S(1)}, u32[]{:S(2)}, u32[]{:S(2)}) collective-permute-start(f32[80,512]{1,0:T(8,128)S(1)} %densities.1.refs_0_), channel_id=1, source_target_pairs={{0,1},{1,0},{2,3},{3,2},{4,5},{5,4},{6,7},{7,6},{8,9},{9,8},{10,11... | collective-permute-start | bytes 491528 | tf_op jit(solution)/shard_map/ppermute | solution.py:163
  10.4 0.0 collective-permute-done.2
  10.4 0.2 %collective-permute-done.3 = f32[4,512]{1,0:T(4,128)S(1)} collective-permute-done((f32[4,512]{1,0:T(4,128)S(1)}, f32[4,512]{1,0:T(4,128)S(1)}, u32[]{:S(2)}, u32[]{:S(2)}) %collective-permute-start.3) | collective-permute-done | bytes 8224 | tf_op jit(solution)/shard_map/ppermute | solution.py:173
  10.6 0.2 collective-permute-done.4
  10.8 2.5 %collective-permute-start.5 = (f32[16,512]{1,0:T(8,128)S(1)}, f32[16,512]{1,0:T(8,128)S(1)}, u32[]{:S(2)}, u32[]{:S(2)}) collective-permute-start(f32[16,512]{1,0:T(8,128)S(1)} %pad_maximum_fusion), channel_id=1, source_target_pairs={{0,7},{1,6},{2,5},{3,4},{4,3},{5,2},{6,1},{7,0},{8,15},{9,14},{10,... | collective-permute-start | bytes 98312 | tf_op jit(solution)/shard_map/ppermute | solution.py:173
  13.3 0.4 %collective-permute-start.7 = (f32[16,512]{1,0:T(8,128)S(1)}, f32[16,512]{1,0:T(8,128)S(1)}, u32[]{:S(2)}, u32[]{:S(2)}) collective-permute-start(f32[16,512]{1,0:T(8,128)S(1)} %pad_maximum_fusion), channel_id=1, source_target_pairs={{0,3},{1,2},{2,1},{3,0},{4,7},{5,6},{6,5},{7,4},{8,11},{9,10},{10,... | collective-permute-start | bytes 98312 | tf_op jit(solution)/shard_map/ppermute | solution.py:173
  13.7 0.3 %collective-permute-start.8 = (f32[16,512]{1,0:T(8,128)S(1)}, f32[16,512]{1,0:T(8,128)S(1)}, u32[]{:S(2)}, u32[]{:S(2)}) collective-permute-start(f32[16,512]{1,0:T(8,128)S(1)} %pad_maximum_fusion), channel_id=1, source_target_pairs={{0,5},{1,4},{2,7},{3,6},{4,1},{5,0},{6,3},{7,2},{8,13},{9,12},{10,... | collective-permute-start | bytes 98312 | tf_op jit(solution)/shard_map/ppermute | solution.py:173
  14.1 1.1 %collective-permute-done.5.refs_1_ = f32[16,512]{1,0:T(8,128)S(1)} collective-permute-done((f32[16,512]{1,0:T(8,128)S(1)}, f32[16,512]{1,0:T(8,128)S(1)}, u32[]{:S(2)}, u32[]{:S(2)}) %collective-permute-start.5) | collective-permute-done | bytes 32800 | tf_op jit(solution)/shard_map/ppermute | solution.py:173
  15.1 0.3 %collective-permute-start.6 = (f32[16,512]{1,0:T(8,128)S(1)}, f32[16,512]{1,0:T(8,128)S(1)}, u32[]{:S(2)}, u32[]{:S(2)}) collective-permute-start(f32[16,512]{1,0:T(8,128)S(1)} %pad_maximum_fusion), channel_id=1, source_target_pairs={{0,1},{1,0},{2,3},{3,2},{4,5},{5,4},{6,7},{7,6},{8,9},{9,8},{10,11... | collective-permute-start | bytes 98312 | tf_op jit(solution)/shard_map/ppermute | solution.py:163
  15.5 0.0 collective-permute-done.1.refs_1_
  15.5 0.2 %columns.1 = (bf16[512,160]{1,0:T(8,128)(2,1)S(1)}, bf16[512,160]{1,0:T(8,128)(2,1)S(1)}) custom-call(f32[80,512]{1,0:T(8,128)S(1)} %densities.1.refs_0_, f32[80,512]{1,0:T(8,128)S(1)} %collective-permute-done.1.refs_1_), custom_call_target="tpu_custom_call" | custom-call | tf_op jit(solution)/shard_map/columns/pallas_call | solution.py:222
  15.7 0.9 %collective-permute-done.7.refs_2_ = f32[16,512]{1,0:T(8,128)S(1)} collective-permute-done((f32[16,512]{1,0:T(8,128)S(1)}, f32[16,512]{1,0:T(8,128)S(1)}, u32[]{:S(2)}, u32[]{:S(2)}) %collective-permute-start.7) | collective-permute-done | bytes 32800 | tf_op jit(solution)/shard_map/ppermute | solution.py:173
  16.6 0.4 %collective-permute-done.8.refs_3_ = f32[16,512]{1,0:T(8,128)S(1)} collective-permute-done((f32[16,512]{1,0:T(8,128)S(1)}, f32[16,512]{1,0:T(8,128)S(1)}, u32[]{:S(2)}, u32[]{:S(2)}) %collective-permute-start.8) | collective-permute-done | bytes 32800 | tf_op jit(solution)/shard_map/ppermute | solution.py:173
  17.0 0.0 collective-permute-done.6.refs_0_
  17.0 0.0 copy-done.2
  17.0 0.9 %product.1 = f32[64,160]{1,0:T(8,128)} custom-call(f32[64,160]{1,0:T(8,128)S(1)} %bitcast.8, bf16[512,160]{1,0:T(8,128)(2,1)S(1)} %get-tuple-element.18.hi_ref, bf16[512,160]{1,0:T(8,128)(2,1)S(1)} %get-tuple-element.19.lo_ref, f32[16,512]{1,0:T(8,128)S(1)} %collective-permute-done.6.refs_0_, f32[16,512]{1,0:T(8,128)S(1)} %collective-permute-done.5.refs_1_, ...), custom_call_target="tpu_custom_call" | custom-call | tf_op jit(solution)/shard_map/product/pallas_call | solution.py:230
  (3 shorter events, 0.0 us)
Async XLA Ops:
  0.0 8.2 %copy-start.5 = (s32[1,512]{1,0:T(1,128)S(1)}, s32[1,512]{1,0:T(1,128)}, u32[]{:S(2)}) copy-start(s32[1,512]{1,0:T(1,128)} %pv_ref.2) | copy-start | bytes 6148
  0.0 8.2 %copy-start = (f32[80,4096]{1,0:T(8,128)S(1)}, f32[80,4096]{1,0:T(8,128)}, u32[]{:S(2)}) copy-start(f32[80,4096]{1,0:T(8,128)} %val_ref.3) | copy-start | bytes 3932164
  0.0 8.2 %copy-start.3 = (f32[4096]{0:T(1024)S(1)}, f32[4096]{0:T(1024)}, u32[]{:S(2)}) copy-start(f32[4096]{0:T(1024)} %param.10) | copy-start | bytes 49156
  1.5 7.6 %copy-start.1 = (f32[80,4096]{1,0:T(8,128)S(1)}, f32[80,4096]{1,0:T(8,128)}, u32[]{:S(2)}) copy-start(f32[80,4096]{1,0:T(8,128)} %cond_ref.3) | copy-start | bytes 3932164
  1.5 7.6 %copy-start.4 = (f32[4096]{0:T(1024)S(1)}, f32[4096]{0:T(1024)}, u32[]{:S(2)}) copy-start(f32[4096]{0:T(1024)} %param.11) | copy-start | bytes 49156
  1.6 7.6 %copy-start.6 = (s32[1,512]{1,0:T(1,128)S(1)}, s32[1,512]{1,0:T(1,128)}, u32[]{:S(2)}) copy-start(s32[1,512]{1,0:T(1,128)} %pc_ref.2) | copy-start | bytes 6148
  1.6 1.4 %collective-permute-start = (f32[2,4,512]{2,1,0:T(4,128)S(1)}, f32[2,4,512]{2,1,0:T(4,128)S(1)}, u32[]{:S(2)}, u32[]{:S(2)}) collective-permute-start(f32[2,4,512]{2,1,0:T(4,128)S(1)} %slab_rows.1), channel_id=1, source_target_pairs={{0,1},{1,0},{2,3},{3,2},{4,5},{5,4},{6,7},{7,6},{8,9},{9,8},{10,11... | collective-permute-start | bytes 49160 | tf_op jit(solution)/shard_map/ppermute | solution.py:163
  2.9 7.4 %collective-permute-start.2 = (f32[4,512]{1,0:T(4,128)S(1)}, f32[4,512]{1,0:T(4,128)S(1)}, u32[]{:S(2)}, u32[]{:S(2)}) collective-permute-start(f32[4,512]{1,0:T(4,128)S(1)} %get-tuple-element.20), channel_id=1, source_target_pairs={{0,17},{1,16},{2,19},{3,18},{4,21},{5,20},{6,23},{7,22},{8,25},{9,... | collective-permute-start | bytes 24584 | tf_op jit(solution)/shard_map/ppermute | solution.py:173
  6.6 4.0 %collective-permute-start.3 = (f32[4,512]{1,0:T(4,128)S(1)}, f32[4,512]{1,0:T(4,128)S(1)}, u32[]{:S(2)}, u32[]{:S(2)}) collective-permute-start(f32[4,512]{1,0:T(4,128)S(1)} %get-tuple-element.20), channel_id=1, source_target_pairs={{0,25},{1,24},{2,27},{3,26},{4,29},{5,28},{6,31},{7,30},{8,17},{9,... | collective-permute-start | bytes 24584 | tf_op jit(solution)/shard_map/ppermute | solution.py:173
  7.7 3.1 %collective-permute-start.4 = (f32[4,512]{1,0:T(4,128)S(1)}, f32[4,512]{1,0:T(4,128)S(1)}, u32[]{:S(2)}, u32[]{:S(2)}) collective-permute-start(f32[4,512]{1,0:T(4,128)S(1)} %get-tuple-element.20), channel_id=1, source_target_pairs={{0,9},{1,8},{2,11},{3,10},{4,13},{5,12},{6,15},{7,14},{8,1},{9,0},... | collective-permute-start | bytes 24584 | tf_op jit(solution)/shard_map/ppermute | solution.py:173
  9.1 7.9 %copy-start.2 = (f32[160,64]{0,1:T(8,128)S(1)}, f32[160,64]{0,1:T(8,128)}, u32[]{:S(2)}) copy-start(f32[160,64]{0,1:T(8,128)} %param.7) | copy-start | bytes 122884
  10.1 5.3 %collective-permute-start.1 = (f32[80,512]{1,0:T(8,128)S(1)}, f32[80,512]{1,0:T(8,128)S(1)}, u32[]{:S(2)}, u32[]{:S(2)}) collective-permute-start(f32[80,512]{1,0:T(8,128)S(1)} %densities.1.refs_0_), channel_id=1, source_target_pairs={{0,1},{1,0},{2,3},{3,2},{4,5},{5,4},{6,7},{7,6},{8,9},{9,8},{10,11... | collective-permute-start | bytes 491528 | tf_op jit(solution)/shard_map/ppermute | solution.py:163
  10.8 4.3 %collective-permute-start.5 = (f32[16,512]{1,0:T(8,128)S(1)}, f32[16,512]{1,0:T(8,128)S(1)}, u32[]{:S(2)}, u32[]{:S(2)}) collective-permute-start(f32[16,512]{1,0:T(8,128)S(1)} %pad_maximum_fusion), channel_id=1, source_target_pairs={{0,7},{1,6},{2,5},{3,4},{4,3},{5,2},{6,1},{7,0},{8,15},{9,14},{10,... | collective-permute-start | bytes 98312 | tf_op jit(solution)/shard_map/ppermute | solution.py:173
  13.3 3.3 %collective-permute-start.7 = (f32[16,512]{1,0:T(8,128)S(1)}, f32[16,512]{1,0:T(8,128)S(1)}, u32[]{:S(2)}, u32[]{:S(2)}) collective-permute-start(f32[16,512]{1,0:T(8,128)S(1)} %pad_maximum_fusion), channel_id=1, source_target_pairs={{0,3},{1,2},{2,1},{3,0},{4,7},{5,6},{6,5},{7,4},{8,11},{9,10},{10,... | collective-permute-start | bytes 98312 | tf_op jit(solution)/shard_map/ppermute | solution.py:173
  13.7 3.3 %collective-permute-start.8 = (f32[16,512]{1,0:T(8,128)S(1)}, f32[16,512]{1,0:T(8,128)S(1)}, u32[]{:S(2)}, u32[]{:S(2)}) collective-permute-start(f32[16,512]{1,0:T(8,128)S(1)} %pad_maximum_fusion), channel_id=1, source_target_pairs={{0,5},{1,4},{2,7},{3,6},{4,1},{5,0},{6,3},{7,2},{8,13},{9,12},{10,... | collective-permute-start | bytes 98312 | tf_op jit(solution)/shard_map/ppermute | solution.py:173
  15.1 1.9 %collective-permute-start.6 = (f32[16,512]{1,0:T(8,128)S(1)}, f32[16,512]{1,0:T(8,128)S(1)}, u32[]{:S(2)}, u32[]{:S(2)}) collective-permute-start(f32[16,512]{1,0:T(8,128)S(1)} %pad_maximum_fusion), channel_id=1, source_target_pairs={{0,1},{1,0},{2,3},{3,2},{4,5},{5,4},{6,7},{7,6},{8,9},{9,8},{10,11... | collective-permute-start | bytes 98312 | tf_op jit(solution)/shard_map/ppermute | solution.py:163

commit v12 on v11

--- a/solution.py
+++ b/solution.py
@@ -15,6 +15,7 @@
     ((3, 2, 1, 0), (1, 0, 3, 2), (2, 3, 0, 1)),
 )
 CHUNK = 256
+PIECES = 4
 MIB = 1 << 20
 
 
@@ -62,7 +63,10 @@
 
 
 def slab_kernel(val_ref, cond_ref, pv_ref, pc_ref, out_ref, val, cond, pv, pc, sems):
-    moves = ((pv_ref, pv), (pc_ref, pc), (val_ref.at[pl.ds(0, ROWS)], val), (cond_ref.at[pl.ds(0, ROWS)], cond))
+    cuts = [pl.ds(at, val.shape[1] // PIECES) for at in range(0, val.shape[1], val.shape[1] // PIECES)]
+    moves = [(pv_ref, pv), (pc_ref, pc)]
+    for src, dst in ((val_ref, val), (cond_ref, cond)):
+        moves += [(src.at[pl.ds(0, ROWS), cut], dst.at[:, cut]) for cut in cuts]
     copies = [pltpu.make_async_copy(src, dst, sems.at[i]) for i, (src, dst) in enumerate(moves)]
     for copy in copies:
         copy.start(priority=1)
@@ -70,9 +74,11 @@
     hot_v = one_hot(pv[...], CHUNK)
     copies[1].wait()
     hot_c = one_hot(pc[...], CHUNK)
-    copies[2].wait()
+    for copy in copies[2 : 2 + PIECES]:
+        copy.wait()
     dens = pick_few(val[...], hot_v, pv[...])
-    copies[3].wait()
+    for copy in copies[2 + PIECES :]:
+        copy.wait()
     dens = dens * pick_few(cond[...], hot_c, pc[...])
     sub = out_ref.shape[1]
     for n in range(out_ref.shape[0]):
@@ -153,7 +159,7 @@
             pltpu.VMEM((ROWS, bands), jnp.float32),
             pltpu.VMEM((1, pairs), jnp.int32),
             pltpu.VMEM((1, pairs), jnp.int32),
-            pltpu.SemaphoreType.DMA((4,)),
+            pltpu.SemaphoreType.DMA((2 + 2 * PIECES,)),
         ],
         compiler_params=params(16),
         name="slab_rows",

time: 18.1 us -> 18 us (level)
  no operation moved by 1% of the time
where the time goes in v12:
time: 18 us; the launch traced here: 17.9 us
  starting transfers between devices  9.56 us (53%)
  Pallas kernels  4.47 us (25%)
  waiting for transfers between devices  3.68 us (20%)
    ppermute x6, starting transfers between devices, between_chips(): return lax.ppermute(x, ('wide', 'narrow'), pairs_of)  8.45 us
    ppermute x6, waiting for transfers between devices, between_chips(): return lax.ppermute(x, ('wide', 'narrow'), pairs_of)  2.84 us
    pallas_call x1, Pallas kernels, shards(): pl.pallas_call(slab_kernel, in_specs=[hbm] * 4, out_specs=vmem, out_shape...  1.5 us
    ppermute x3, starting transfers between devices, exchange(): return lax.ppermute(x, 'narrow', [(i, i ^ bit) for i in range(n_narrow)])  1.11 us
    pallas_call x1, Pallas kernels, shards(): pl.pallas_call(dens_kernel, in_specs=[vmem] * 4, out_specs=vmem, out_shap...  0.96 us
    pallas_call x1, Pallas kernels, shards(): pl.pallas_call(val_kernel, in_specs=[vmem] * 3, out_specs=vmem, out_shape...  0.94 us
    pallas_call x1, Pallas kernels, shards(): pl.pallas_call(functools.partial(product_kernel, strides[-1], ROUNDS[(len...  0.86 us
    ppermute x3, waiting for transfers between devices, exchange(): return lax.ppermute(x, 'narrow', [(i, i ^ bit) for i in range(n_narrow)])  0.84 us
  transfers between devices with their start and end apart: 9, of which 6 were waited for; matrix products, arithmetic and copies ran while one was open for 0% of the time, Pallas kernels for 12%

profile of v12, /device:TPU:0, one launch (start us, length us, event | category | flops | bytes accessed | tf_op | source)
XLA Modules:
  0.0 17.9 jit_solution(2517693747890565220)
XLA Ops:
  0.0 0.0 copy-start.5
  0.0 0.0 copy-start
  0.0 0.0 copy-start.3
  0.0 1.5 %slab_rows.1 = f32[2,4,512]{2,1,0:T(4,128)S(1)} custom-call(f32[80,4096]{1,0:T(8,128)} %val_ref.3, f32[80,4096]{1,0:T(8,128)} %cond_ref.3, s32[1,512]{1,0:T(1,128)} %pv_ref.2, s32[1,512]{1,0:T(1,128)} %pc_ref.2), custom_call_target="tpu_custom_call" | custom-call | tf_op jit(solution)/shard_map/slab_rows/pallas_call | solution.py:152
  1.5 0.0 copy-start.1
  1.5 0.0 copy-start.4
  1.5 0.0 copy-start.6
  1.5 0.5 %collective-permute-start = (f32[2,4,512]{2,1,0:T(4,128)S(1)}, f32[2,4,512]{2,1,0:T(4,128)S(1)}, u32[]{:S(2)}, u32[]{:S(2)}) collective-permute-start(f32[2,4,512]{2,1,0:T(4,128)S(1)} %slab_rows.1), channel_id=1, source_target_pairs={{0,1},{1,0},{2,3},{3,2},{4,5},{5,4},{6,7},{7,6},{8,9},{9,8},{10,11... | collective-permute-start | bytes 49160 | tf_op jit(solution)/shard_map/ppermute | solution.py:169
  2.1 0.8 %collective-permute-done = f32[2,4,512]{2,1,0:T(4,128)S(1)} collective-permute-done((f32[2,4,512]{2,1,0:T(4,128)S(1)}, f32[2,4,512]{2,1,0:T(4,128)S(1)}, u32[]{:S(2)}, u32[]{:S(2)}) %collective-permute-start) | collective-permute-done | bytes 16416 | tf_op jit(solution)/shard_map/ppermute | solution.py:169
  2.9 3.7 %collective-permute-start.2 = (f32[4,512]{1,0:T(4,128)S(1)}, f32[4,512]{1,0:T(4,128)S(1)}, u32[]{:S(2)}, u32[]{:S(2)}) collective-permute-start(f32[4,512]{1,0:T(4,128)S(1)} %get-tuple-element.20), channel_id=1, source_target_pairs={{0,17},{1,16},{2,19},{3,18},{4,21},{5,20},{6,23},{7,22},{8,25},{9,... | collective-permute-start | bytes 24584 | tf_op jit(solution)/shard_map/ppermute | solution.py:179
  6.6 1.1 %collective-permute-start.3 = (f32[4,512]{1,0:T(4,128)S(1)}, f32[4,512]{1,0:T(4,128)S(1)}, u32[]{:S(2)}, u32[]{:S(2)}) collective-permute-start(f32[4,512]{1,0:T(4,128)S(1)} %get-tuple-element.20), channel_id=1, source_target_pairs={{0,25},{1,24},{2,27},{3,26},{4,29},{5,28},{6,31},{7,30},{8,17},{9,... | collective-permute-start | bytes 24584 | tf_op jit(solution)/shard_map/ppermute | solution.py:179
  7.7 0.5 %collective-permute-start.4 = (f32[4,512]{1,0:T(4,128)S(1)}, f32[4,512]{1,0:T(4,128)S(1)}, u32[]{:S(2)}, u32[]{:S(2)}) collective-permute-start(f32[4,512]{1,0:T(4,128)S(1)} %get-tuple-element.20), channel_id=1, source_target_pairs={{0,9},{1,8},{2,11},{3,10},{4,13},{5,12},{6,15},{7,14},{8,1},{9,0},... | collective-permute-start | bytes 24584 | tf_op jit(solution)/shard_map/ppermute | solution.py:179
  8.1 0.0 copy-done.5
  8.1 0.0 copy-done
  8.2 0.0 copy-done.3
  8.2 0.9 %val_columns.1.v_ref = f32[88,512]{1,0:T(8,128)S(1)} custom-call(f32[80,4096]{1,0:T(8,128)S(1)} %copy-done, f32[1,4096]{1,0:T(1,128)S(1)} %bitcast.9, s32[1,512]{1,0:T(1,128)S(1)} %copy-done.5), custom_call_target="tpu_custom_call" | custom-call | tf_op jit(solution)/shard_map/val_columns/pallas_call | solution.py:200
  9.1 0.0 copy-start.2
  9.1 0.0 copy-done.1
  9.1 0.0 copy-done.4
  9.1 0.0 copy-done.6
  9.1 1.0 %densities.1.refs_0_ = f32[80,512]{1,0:T(8,128)S(1)} custom-call(f32[80,4096]{1,0:T(8,128)S(1)} %copy-done.1, f32[1,4096]{1,0:T(1,128)S(1)} %bitcast.10, s32[1,512]{1,0:T(1,128)S(1)} %copy-done.6, f32[88,512]{1,0:T(8,128)S(1)} %val_columns.1.v_ref), custom_call_target="tpu_custom_call" | custom-call | tf_op jit(solution)/shard_map/densities/pallas_call | solution.py:208
  10.1 0.2 %collective-permute-start.1 = (f32[80,512]{1,0:T(8,128)S(1)}, f32[80,512]{1,0:T(8,128)S(1)}, u32[]{:S(2)}, u32[]{:S(2)}) collective-permute-start(f32[80,512]{1,0:T(8,128)S(1)} %densities.1.refs_0_), channel_id=1, source_target_pairs={{0,1},{1,0},{2,3},{3,2},{4,5},{5,4},{6,7},{7,6},{8,9},{9,8},{10,11... | collective-permute-start | bytes 491528 | tf_op jit(solution)/shard_map/ppermute | solution.py:169
  10.3 0.0 collective-permute-done.2
  10.3 0.2 %collective-permute-done.3 = f32[4,512]{1,0:T(4,128)S(1)} collective-permute-done((f32[4,512]{1,0:T(4,128)S(1)}, f32[4,512]{1,0:T(4,128)S(1)}, u32[]{:S(2)}, u32[]{:S(2)}) %collective-permute-start.3) | collective-permute-done | bytes 8224 | tf_op jit(solution)/shard_map/ppermute | solution.py:179
  10.6 0.2 collective-permute-done.4
  10.8 2.5 %collective-permute-start.5 = (f32[16,512]{1,0:T(8,128)S(1)}, f32[16,512]{1,0:T(8,128)S(1)}, u32[]{:S(2)}, u32[]{:S(2)}) collective-permute-start(f32[16,512]{1,0:T(8,128)S(1)} %pad_maximum_fusion), channel_id=1, source_target_pairs={{0,7},{1,6},{2,5},{3,4},{4,3},{5,2},{6,1},{7,0},{8,15},{9,14},{10,... | collective-permute-start | bytes 98312 | tf_op jit(solution)/shard_map/ppermute | solution.py:179
  13.3 0.4 %collective-permute-start.7 = (f32[16,512]{1,0:T(8,128)S(1)}, f32[16,512]{1,0:T(8,128)S(1)}, u32[]{:S(2)}, u32[]{:S(2)}) collective-permute-start(f32[16,512]{1,0:T(8,128)S(1)} %pad_maximum_fusion), channel_id=1, source_target_pairs={{0,3},{1,2},{2,1},{3,0},{4,7},{5,6},{6,5},{7,4},{8,11},{9,10},{10,... | collective-permute-start | bytes 98312 | tf_op jit(solution)/shard_map/ppermute | solution.py:179
  13.7 0.3 %collective-permute-start.8 = (f32[16,512]{1,0:T(8,128)S(1)}, f32[16,512]{1,0:T(8,128)S(1)}, u32[]{:S(2)}, u32[]{:S(2)}) collective-permute-start(f32[16,512]{1,0:T(8,128)S(1)} %pad_maximum_fusion), channel_id=1, source_target_pairs={{0,5},{1,4},{2,7},{3,6},{4,1},{5,0},{6,3},{7,2},{8,13},{9,12},{10,... | collective-permute-start | bytes 98312 | tf_op jit(solution)/shard_map/ppermute | solution.py:179
  14.0 1.1 %collective-permute-done.5.refs_1_ = f32[16,512]{1,0:T(8,128)S(1)} collective-permute-done((f32[16,512]{1,0:T(8,128)S(1)}, f32[16,512]{1,0:T(8,128)S(1)}, u32[]{:S(2)}, u32[]{:S(2)}) %collective-permute-start.5) | collective-permute-done | bytes 32800 | tf_op jit(solution)/shard_map/ppermute | solution.py:179
  15.1 0.3 %collective-permute-start.6 = (f32[16,512]{1,0:T(8,128)S(1)}, f32[16,512]{1,0:T(8,128)S(1)}, u32[]{:S(2)}, u32[]{:S(2)}) collective-permute-start(f32[16,512]{1,0:T(8,128)S(1)} %pad_maximum_fusion), channel_id=1, source_target_pairs={{0,1},{1,0},{2,3},{3,2},{4,5},{5,4},{6,7},{7,6},{8,9},{9,8},{10,11... | collective-permute-start | bytes 98312 | tf_op jit(solution)/shard_map/ppermute | solution.py:169
  15.5 0.0 collective-permute-done.1.refs_1_
  15.5 0.2 %columns.1 = (bf16[512,160]{1,0:T(8,128)(2,1)S(1)}, bf16[512,160]{1,0:T(8,128)(2,1)S(1)}) custom-call(f32[80,512]{1,0:T(8,128)S(1)} %densities.1.refs_0_, f32[80,512]{1,0:T(8,128)S(1)} %collective-permute-done.1.refs_1_), custom_call_target="tpu_custom_call" | custom-call | tf_op jit(solution)/shard_map/columns/pallas_call | solution.py:228
  15.7 0.9 %collective-permute-done.7.refs_2_ = f32[16,512]{1,0:T(8,128)S(1)} collective-permute-done((f32[16,512]{1,0:T(8,128)S(1)}, f32[16,512]{1,0:T(8,128)S(1)}, u32[]{:S(2)}, u32[]{:S(2)}) %collective-permute-start.7) | collective-permute-done | bytes 32800 | tf_op jit(solution)/shard_map/ppermute | solution.py:179
  16.6 0.4 %collective-permute-done.8.refs_3_ = f32[16,512]{1,0:T(8,128)S(1)} collective-permute-done((f32[16,512]{1,0:T(8,128)S(1)}, f32[16,512]{1,0:T(8,128)S(1)}, u32[]{:S(2)}, u32[]{:S(2)}) %collective-permute-start.8) | collective-permute-done | bytes 32800 | tf_op jit(solution)/shard_map/ppermute | solution.py:179
  17.0 0.0 collective-permute-done.6.refs_0_
  17.0 0.0 copy-done.2
  17.0 0.9 %product.1 = f32[64,160]{1,0:T(8,128)} custom-call(f32[64,160]{1,0:T(8,128)S(1)} %bitcast.8, bf16[512,160]{1,0:T(8,128)(2,1)S(1)} %get-tuple-element.18.hi_ref, bf16[512,160]{1,0:T(8,128)(2,1)S(1)} %get-tuple-element.19.lo_ref, f32[16,512]{1,0:T(8,128)S(1)} %collective-permute-done.6.refs_0_, f32[16,512]{1,0:T(8,128)S(1)} %collective-permute-done.5.refs_1_, ...), custom_call_target="tpu_custom_call" | custom-call | tf_op jit(solution)/shard_map/product/pallas_call | solution.py:236
  (3 shorter events, 0.0 us)
Async XLA Ops:
  0.0 8.1 %copy-start.5 = (s32[1,512]{1,0:T(1,128)S(1)}, s32[1,512]{1,0:T(1,128)}, u32[]{:S(2)}) copy-start(s32[1,512]{1,0:T(1,128)} %pv_ref.2) | copy-start | bytes 6148
  0.0 8.1 %copy-start = (f32[80,4096]{1,0:T(8,128)S(1)}, f32[80,4096]{1,0:T(8,128)}, u32[]{:S(2)}) copy-start(f32[80,4096]{1,0:T(8,128)} %val_ref.3) | copy-start | bytes 3932164
  0.0 8.1 %copy-start.3 = (f32[4096]{0:T(1024)S(1)}, f32[4096]{0:T(1024)}, u32[]{:S(2)}) copy-start(f32[4096]{0:T(1024)} %param.10) | copy-start | bytes 49156
  1.5 7.6 %copy-start.1 = (f32[80,4096]{1,0:T(8,128)S(1)}, f32[80,4096]{1,0:T(8,128)}, u32[]{:S(2)}) copy-start(f32[80,4096]{1,0:T(8,128)} %cond_ref.3) | copy-start | bytes 3932164
  1.5 7.6 %copy-start.4 = (f32[4096]{0:T(1024)S(1)}, f32[4096]{0:T(1024)}, u32[]{:S(2)}) copy-start(f32[4096]{0:T(1024)} %param.11) | copy-start | bytes 49156
  1.5 7.6 %copy-start.6 = (s32[1,512]{1,0:T(1,128)S(1)}, s32[1,512]{1,0:T(1,128)}, u32[]{:S(2)}) copy-start(s32[1,512]{1,0:T(1,128)} %pc_ref.2) | copy-start | bytes 6148
  1.5 1.4 %collective-permute-start = (f32[2,4,512]{2,1,0:T(4,128)S(1)}, f32[2,4,512]{2,1,0:T(4,128)S(1)}, u32[]{:S(2)}, u32[]{:S(2)}) collective-permute-start(f32[2,4,512]{2,1,0:T(4,128)S(1)} %slab_rows.1), channel_id=1, source_target_pairs={{0,1},{1,0},{2,3},{3,2},{4,5},{5,4},{6,7},{7,6},{8,9},{9,8},{10,11... | collective-permute-start | bytes 49160 | tf_op jit(solution)/shard_map/ppermute | solution.py:169
  2.9 7.4 %collective-permute-start.2 = (f32[4,512]{1,0:T(4,128)S(1)}, f32[4,512]{1,0:T(4,128)S(1)}, u32[]{:S(2)}, u32[]{:S(2)}) collective-permute-start(f32[4,512]{1,0:T(4,128)S(1)} %get-tuple-element.20), channel_id=1, source_target_pairs={{0,17},{1,16},{2,19},{3,18},{4,21},{5,20},{6,23},{7,22},{8,25},{9,... | collective-permute-start | bytes 24584 | tf_op jit(solution)/shard_map/ppermute | solution.py:179
  6.6 4.0 %collective-permute-start.3 = (f32[4,512]{1,0:T(4,128)S(1)}, f32[4,512]{1,0:T(4,128)S(1)}, u32[]{:S(2)}, u32[]{:S(2)}) collective-permute-start(f32[4,512]{1,0:T(4,128)S(1)} %get-tuple-element.20), channel_id=1, source_target_pairs={{0,25},{1,24},{2,27},{3,26},{4,29},{5,28},{6,31},{7,30},{8,17},{9,... | collective-permute-start | bytes 24584 | tf_op jit(solution)/shard_map/ppermute | solution.py:179
  7.7 3.1 %collective-permute-start.4 = (f32[4,512]{1,0:T(4,128)S(1)}, f32[4,512]{1,0:T(4,128)S(1)}, u32[]{:S(2)}, u32[]{:S(2)}) collective-permute-start(f32[4,512]{1,0:T(4,128)S(1)} %get-tuple-element.20), channel_id=1, source_target_pairs={{0,9},{1,8},{2,11},{3,10},{4,13},{5,12},{6,15},{7,14},{8,1},{9,0},... | collective-permute-start | bytes 24584 | tf_op jit(solution)/shard_map/ppermute | solution.py:179
  9.1 7.9 %copy-start.2 = (f32[160,64]{0,1:T(8,128)S(1)}, f32[160,64]{0,1:T(8,128)}, u32[]{:S(2)}) copy-start(f32[160,64]{0,1:T(8,128)} %param.7) | copy-start | bytes 122884
  10.1 5.3 %collective-permute-start.1 = (f32[80,512]{1,0:T(8,128)S(1)}, f32[80,512]{1,0:T(8,128)S(1)}, u32[]{:S(2)}, u32[]{:S(2)}) collective-permute-start(f32[80,512]{1,0:T(8,128)S(1)} %densities.1.refs_0_), channel_id=1, source_target_pairs={{0,1},{1,0},{2,3},{3,2},{4,5},{5,4},{6,7},{7,6},{8,9},{9,8},{10,11... | collective-permute-start | bytes 491528 | tf_op jit(solution)/shard_map/ppermute | solution.py:169
  10.8 4.3 %collective-permute-start.5 = (f32[16,512]{1,0:T(8,128)S(1)}, f32[16,512]{1,0:T(8,128)S(1)}, u32[]{:S(2)}, u32[]{:S(2)}) collective-permute-start(f32[16,512]{1,0:T(8,128)S(1)} %pad_maximum_fusion), channel_id=1, source_target_pairs={{0,7},{1,6},{2,5},{3,4},{4,3},{5,2},{6,1},{7,0},{8,15},{9,14},{10,... | collective-permute-start | bytes 98312 | tf_op jit(solution)/shard_map/ppermute | solution.py:179
  13.3 3.3 %collective-permute-start.7 = (f32[16,512]{1,0:T(8,128)S(1)}, f32[16,512]{1,0:T(8,128)S(1)}, u32[]{:S(2)}, u32[]{:S(2)}) collective-permute-start(f32[16,512]{1,0:T(8,128)S(1)} %pad_maximum_fusion), channel_id=1, source_target_pairs={{0,3},{1,2},{2,1},{3,0},{4,7},{5,6},{6,5},{7,4},{8,11},{9,10},{10,... | collective-permute-start | bytes 98312 | tf_op jit(solution)/shard_map/ppermute | solution.py:179
  13.7 3.3 %collective-permute-start.8 = (f32[16,512]{1,0:T(8,128)S(1)}, f32[16,512]{1,0:T(8,128)S(1)}, u32[]{:S(2)}, u32[]{:S(2)}) collective-permute-start(f32[16,512]{1,0:T(8,128)S(1)} %pad_maximum_fusion), channel_id=1, source_target_pairs={{0,5},{1,4},{2,7},{3,6},{4,1},{5,0},{6,3},{7,2},{8,13},{9,12},{10,... | collective-permute-start | bytes 98312 | tf_op jit(solution)/shard_map/ppermute | solution.py:179
  15.1 1.9 %collective-permute-start.6 = (f32[16,512]{1,0:T(8,128)S(1)}, f32[16,512]{1,0:T(8,128)S(1)}, u32[]{:S(2)}, u32[]{:S(2)}) collective-permute-start(f32[16,512]{1,0:T(8,128)S(1)} %pad_maximum_fusion), channel_id=1, source_target_pairs={{0,1},{1,0},{2,3},{3,2},{4,5},{5,4},{6,7},{7,6},{8,9},{9,8},{10,11... | collective-permute-start | bytes 98312 | tf_op jit(solution)/shard_map/ppermute | solution.py:169

commit v13 on v12

--- a/solution.py
+++ b/solution.py
@@ -191,12 +191,7 @@
         strides.append(n_wide // RADIX ** (len(strides) + 1))
     start = across if len(strides) % 2 else 0
     narrow = lax.axis_index("narrow")
-    sent, own_block = mine[start], mine[start ^ across]
-    for n in range(1, n_narrow):
-        got = exchange(mine, n)
-        sent = jnp.where(narrow == n, got[n ^ start], sent)
-        own_block = jnp.where(narrow == n, got[n ^ start ^ across], own_block)
-    pair_val, pair_cond, sent = lax.optimization_barrier((pair_val, pair_cond, sent))
+    pair_val, mine = lax.optimization_barrier((pair_val, mine))
     v = pl.pallas_call(
         val_kernel,
         in_specs=[vmem] * 3,
@@ -205,6 +200,12 @@
         compiler_params=params(24),
         name="val_columns",
     )(val_orb, e_val[None, :], pair_val)
+    sent, own_block = mine[start], mine[start ^ across]
+    for n in range(1, n_narrow):
+        got, v = lax.optimization_barrier((exchange(mine, n), v))
+        sent = jnp.where(narrow == n, got[n ^ start], sent)
+        own_block = jnp.where(narrow == n, got[n ^ start ^ across], own_block)
+    pair_cond, sent = lax.optimization_barrier((pair_cond, sent))
     own = pl.pallas_call(
         dens_kernel,
         in_specs=[vmem] * 4,

time: 18 us -> 18.1 us (level)
  waiting for transfers between devices: 3.68 us -> 4.11 us
  starting transfers between devices: 9.56 us -> 9.23 us
    ppermute x6, waiting for transfers between devices: 2.84 us -> 4.1 us  [between_chips(): return lax.ppermute(x, ('wide', 'narrow'), pairs_of)]
    ppermute x3, waiting for transfers between devices: 0.84 us -> 0.01 us  [exchange(): return lax.ppermute(x, 'narrow', [(i, i ^ bit) for i in range(n_narrow)])]
    ppermute x6, starting transfers between devices: 8.45 us -> 8.13 us  [between_chips(): return lax.ppermute(x, ('wide', 'narrow'), pairs_of)]
  transfers between devices with their start and end apart: 9 -> 9, of which waited for: 6 -> 5; matrix products, arithmetic and copies ran while one was open for 0% -> 0% of each run, Pallas kernels for 12% -> 12%
where the time goes in v13:
time: 18.1 us; the launch traced here: 18 us
  starting transfers between devices  9.23 us (51%)
  Pallas kernels  4.47 us (25%)
  waiting for transfers between devices  4.11 us (23%)
    ppermute x6, starting transfers between devices, between_chips(): return lax.ppermute(x, ('wide', 'narrow'), pairs_of)  8.13 us
    ppermute x6, waiting for transfers between devices, between_chips(): return lax.ppermute(x, ('wide', 'narrow'), pairs_of)  4.1 us
    pallas_call x1, Pallas kernels, shards(): pl.pallas_call(slab_kernel, in_specs=[hbm] * 4, out_specs=vmem, out_shape...  1.5 us
    ppermute x3, starting transfers between devices, exchange(): return lax.ppermute(x, 'narrow', [(i, i ^ bit) for i in range(n_narrow)])  1.1 us
    pallas_call x1, Pallas kernels, shards(): pl.pallas_call(dens_kernel, in_specs=[vmem] * 4, out_specs=vmem, out_shap...  0.96 us
    pallas_call x1, Pallas kernels, shards(): pl.pallas_call(val_kernel, in_specs=[vmem] * 3, out_specs=vmem, out_shape...  0.94 us
    pallas_call x1, Pallas kernels, shards(): pl.pallas_call(functools.partial(product_kernel, strides[-1], ROUNDS[(len...  0.86 us
  transfers between devices with their start and end apart: 9, of which 5 were waited for; matrix products, arithmetic and copies ran while one was open for 0% of the time, Pallas kernels for 12%

profile of v13, /device:TPU:0, one launch (start us, length us, event | category | flops | bytes accessed | tf_op | source)
XLA Modules:
  0.0 18.0 jit_solution(15323401520925901317)
XLA Ops:
  0.0 0.0 copy-start.5
  0.0 0.0 copy-start
  0.0 0.0 copy-start.3
  0.0 1.5 %slab_rows.1 = f32[2,4,512]{2,1,0:T(4,128)S(1)} custom-call(f32[80,4096]{1,0:T(8,128)} %val_ref.3, f32[80,4096]{1,0:T(8,128)} %cond_ref.3, s32[1,512]{1,0:T(1,128)} %pv_ref.2, s32[1,512]{1,0:T(1,128)} %pc_ref.2), custom_call_target="tpu_custom_call" | custom-call | tf_op jit(solution)/shard_map/slab_rows/pallas_call | solution.py:152
  1.5 0.0 copy-start.1
  1.5 0.0 copy-start.4
  1.5 0.0 copy-start.6
  1.5 0.5 %collective-permute-start = (f32[2,4,512]{2,1,0:T(4,128)S(1)}, f32[2,4,512]{2,1,0:T(4,128)S(1)}, u32[]{:S(2)}, u32[]{:S(2)}) collective-permute-start(f32[2,4,512]{2,1,0:T(4,128)S(1)} %slab_rows.1), channel_id=1, source_target_pairs={{0,1},{1,0},{2,3},{3,2},{4,5},{5,4},{6,7},{7,6},{8,9},{9,8},{10,11... | collective-permute-start | bytes 49160 | tf_op jit(solution)/shard_map/ppermute | solution.py:169
  2.1 0.0 copy-done.5
  2.1 0.0 copy-done
  2.1 0.0 copy-done.3
  2.1 0.9 %val_columns.1.v_ref = f32[88,512]{1,0:T(8,128)S(1)} custom-call(f32[80,4096]{1,0:T(8,128)S(1)} %copy-done, f32[1,4096]{1,0:T(1,128)S(1)} %bitcast.9, s32[1,512]{1,0:T(1,128)S(1)} %copy-done.5), custom_call_target="tpu_custom_call" | custom-call | tf_op jit(solution)/shard_map/val_columns/pallas_call | solution.py:195
  3.0 0.0 copy-start.2
  3.0 0.0 collective-permute-done
  3.1 3.7 %collective-permute-start.2 = (f32[4,512]{1,0:T(4,128)S(1)}, f32[4,512]{1,0:T(4,128)S(1)}, u32[]{:S(2)}, u32[]{:S(2)}) collective-permute-start(f32[4,512]{1,0:T(4,128)S(1)} %get-tuple-element.26), channel_id=1, source_target_pairs={{0,17},{1,16},{2,19},{3,18},{4,21},{5,20},{6,23},{7,22},{8,25},{9,... | collective-permute-start | bytes 24584 | tf_op jit(solution)/shard_map/ppermute | solution.py:179
  6.8 1.1 %collective-permute-start.3 = (f32[4,512]{1,0:T(4,128)S(1)}, f32[4,512]{1,0:T(4,128)S(1)}, u32[]{:S(2)}, u32[]{:S(2)}) collective-permute-start(f32[4,512]{1,0:T(4,128)S(1)} %get-tuple-element.26), channel_id=1, source_target_pairs={{0,25},{1,24},{2,27},{3,26},{4,29},{5,28},{6,31},{7,30},{8,17},{9,... | collective-permute-start | bytes 24584 | tf_op jit(solution)/shard_map/ppermute | solution.py:179
  7.9 0.3 %collective-permute-start.4 = (f32[4,512]{1,0:T(4,128)S(1)}, f32[4,512]{1,0:T(4,128)S(1)}, u32[]{:S(2)}, u32[]{:S(2)}) collective-permute-start(f32[4,512]{1,0:T(4,128)S(1)} %get-tuple-element.26), channel_id=1, source_target_pairs={{0,9},{1,8},{2,11},{3,10},{4,13},{5,12},{6,15},{7,14},{8,1},{9,0},... | collective-permute-start | bytes 24584 | tf_op jit(solution)/shard_map/ppermute | solution.py:179
  8.2 0.0 copy-done.1
  8.2 0.0 copy-done.4
  8.2 0.0 copy-done.6
  8.2 1.0 %densities.1.refs_0_ = f32[80,512]{1,0:T(8,128)S(1)} custom-call(f32[80,4096]{1,0:T(8,128)S(1)} %copy-done.1, f32[1,4096]{1,0:T(1,128)S(1)} %bitcast.10, s32[1,512]{1,0:T(1,128)S(1)} %copy-done.6, f32[88,512]{1,0:T(8,128)S(1)} %val_columns.1.v_ref), custom_call_target="tpu_custom_call" | custom-call | tf_op jit(solution)/shard_map/densities/pallas_call | solution.py:209
  9.1 0.4 %collective-permute-start.1 = (f32[80,512]{1,0:T(8,128)S(1)}, f32[80,512]{1,0:T(8,128)S(1)}, u32[]{:S(2)}, u32[]{:S(2)}) collective-permute-start(f32[80,512]{1,0:T(8,128)S(1)} %densities.1.refs_0_), channel_id=1, source_target_pairs={{0,1},{1,0},{2,3},{3,2},{4,5},{5,4},{6,7},{7,6},{8,9},{9,8},{10,11... | collective-permute-start | bytes 491528 | tf_op jit(solution)/shard_map/ppermute | solution.py:169
  9.6 0.0 collective-permute-done.2
  9.6 1.2 %collective-permute-done.3 = f32[4,512]{1,0:T(4,128)S(1)} collective-permute-done((f32[4,512]{1,0:T(4,128)S(1)}, f32[4,512]{1,0:T(4,128)S(1)}, u32[]{:S(2)}, u32[]{:S(2)}) %collective-permute-start.3) | collective-permute-done | bytes 8224 | tf_op jit(solution)/shard_map/ppermute | solution.py:179
  10.8 0.2 %collective-permute-done.4 = f32[4,512]{1,0:T(4,128)S(1)} collective-permute-done((f32[4,512]{1,0:T(4,128)S(1)}, f32[4,512]{1,0:T(4,128)S(1)}, u32[]{:S(2)}, u32[]{:S(2)}) %collective-permute-start.4) | collective-permute-done | bytes 8224 | tf_op jit(solution)/shard_map/ppermute | solution.py:179
  11.0 2.4 %collective-permute-start.5 = (f32[16,512]{1,0:T(8,128)S(1)}, f32[16,512]{1,0:T(8,128)S(1)}, u32[]{:S(2)}, u32[]{:S(2)}) collective-permute-start(f32[16,512]{1,0:T(8,128)S(1)} %pad_maximum_fusion), channel_id=1, source_target_pairs={{0,7},{1,6},{2,5},{3,4},{4,3},{5,2},{6,1},{7,0},{8,15},{9,14},{10,... | collective-permute-start | bytes 98312 | tf_op jit(solution)/shard_map/ppermute | solution.py:179
  13.4 0.4 %collective-permute-start.7 = (f32[16,512]{1,0:T(8,128)S(1)}, f32[16,512]{1,0:T(8,128)S(1)}, u32[]{:S(2)}, u32[]{:S(2)}) collective-permute-start(f32[16,512]{1,0:T(8,128)S(1)} %pad_maximum_fusion), channel_id=1, source_target_pairs={{0,3},{1,2},{2,1},{3,0},{4,7},{5,6},{6,5},{7,4},{8,11},{9,10},{10,... | collective-permute-start | bytes 98312 | tf_op jit(solution)/shard_map/ppermute | solution.py:179
  13.8 0.3 %collective-permute-start.8 = (f32[16,512]{1,0:T(8,128)S(1)}, f32[16,512]{1,0:T(8,128)S(1)}, u32[]{:S(2)}, u32[]{:S(2)}) collective-permute-start(f32[16,512]{1,0:T(8,128)S(1)} %pad_maximum_fusion), channel_id=1, source_target_pairs={{0,5},{1,4},{2,7},{3,6},{4,1},{5,0},{6,3},{7,2},{8,13},{9,12},{10,... | collective-permute-start | bytes 98312 | tf_op jit(solution)/shard_map/ppermute | solution.py:179
  14.1 1.3 %collective-permute-done.5.refs_1_ = f32[16,512]{1,0:T(8,128)S(1)} collective-permute-done((f32[16,512]{1,0:T(8,128)S(1)}, f32[16,512]{1,0:T(8,128)S(1)}, u32[]{:S(2)}, u32[]{:S(2)}) %collective-permute-start.5) | collective-permute-done | bytes 32800 | tf_op jit(solution)/shard_map/ppermute | solution.py:179
  15.3 0.2 collective-permute-start.6
  15.5 0.0 collective-permute-done.1.refs_1_
  15.5 0.2 %columns.1 = (bf16[512,160]{1,0:T(8,128)(2,1)S(1)}, bf16[512,160]{1,0:T(8,128)(2,1)S(1)}) custom-call(f32[80,512]{1,0:T(8,128)S(1)} %densities.1.refs_0_, f32[80,512]{1,0:T(8,128)S(1)} %collective-permute-done.1.refs_1_), custom_call_target="tpu_custom_call" | custom-call | tf_op jit(solution)/shard_map/columns/pallas_call | solution.py:229
  15.7 1.0 %collective-permute-done.7.refs_2_ = f32[16,512]{1,0:T(8,128)S(1)} collective-permute-done((f32[16,512]{1,0:T(8,128)S(1)}, f32[16,512]{1,0:T(8,128)S(1)}, u32[]{:S(2)}, u32[]{:S(2)}) %collective-permute-start.7) | collective-permute-done | bytes 32800 | tf_op jit(solution)/shard_map/ppermute | solution.py:179
  16.7 0.4 %collective-permute-done.8.refs_3_ = f32[16,512]{1,0:T(8,128)S(1)} collective-permute-done((f32[16,512]{1,0:T(8,128)S(1)}, f32[16,512]{1,0:T(8,128)S(1)}, u32[]{:S(2)}, u32[]{:S(2)}) %collective-permute-start.8) | collective-permute-done | bytes 32800 | tf_op jit(solution)/shard_map/ppermute | solution.py:179
  17.1 0.0 collective-permute-done.6.refs_0_
  17.1 0.0 copy-done.2
  17.1 0.9 %product.1 = f32[64,160]{1,0:T(8,128)} custom-call(f32[64,160]{1,0:T(8,128)S(1)} %bitcast.8, bf16[512,160]{1,0:T(8,128)(2,1)S(1)} %get-tuple-element.24.hi_ref, bf16[512,160]{1,0:T(8,128)(2,1)S(1)} %get-tuple-element.25.lo_ref, f32[16,512]{1,0:T(8,128)S(1)} %collective-permute-done.6.refs_0_, f32[16,512]{1,0:T(8,128)S(1)} %collective-permute-done.5.refs_1_, ...), custom_call_target="tpu_custom_call" | custom-call | tf_op jit(solution)/shard_map/product/pallas_call | solution.py:237
  (3 shorter events, 0.0 us)
Async XLA Ops:
  0.0 2.1 %copy-start.5 = (s32[1,512]{1,0:T(1,128)S(1)}, s32[1,512]{1,0:T(1,128)}, u32[]{:S(2)}) copy-start(s32[1,512]{1,0:T(1,128)} %pv_ref.2) | copy-start | bytes 6148
  0.0 2.1 %copy-start = (f32[80,4096]{1,0:T(8,128)S(1)}, f32[80,4096]{1,0:T(8,128)}, u32[]{:S(2)}) copy-start(f32[80,4096]{1,0:T(8,128)} %val_ref.3) | copy-start | bytes 3932164
  0.0 2.1 %copy-start.3 = (f32[4096]{0:T(1024)S(1)}, f32[4096]{0:T(1024)}, u32[]{:S(2)}) copy-start(f32[4096]{0:T(1024)} %param.10) | copy-start | bytes 49156
  1.5 6.7 %copy-start.1 = (f32[80,4096]{1,0:T(8,128)S(1)}, f32[80,4096]{1,0:T(8,128)}, u32[]{:S(2)}) copy-start(f32[80,4096]{1,0:T(8,128)} %cond_ref.3) | copy-start | bytes 3932164
  1.5 6.6 %copy-start.4 = (f32[4096]{0:T(1024)S(1)}, f32[4096]{0:T(1024)}, u32[]{:S(2)}) copy-start(f32[4096]{0:T(1024)} %param.11) | copy-start | bytes 49156
  1.5 6.6 %copy-start.6 = (s32[1,512]{1,0:T(1,128)S(1)}, s32[1,512]{1,0:T(1,128)}, u32[]{:S(2)}) copy-start(s32[1,512]{1,0:T(1,128)} %pc_ref.2) | copy-start | bytes 6148
  1.5 1.5 %collective-permute-start = (f32[2,4,512]{2,1,0:T(4,128)S(1)}, f32[2,4,512]{2,1,0:T(4,128)S(1)}, u32[]{:S(2)}, u32[]{:S(2)}) collective-permute-start(f32[2,4,512]{2,1,0:T(4,128)S(1)} %slab_rows.1), channel_id=1, source_target_pairs={{0,1},{1,0},{2,3},{3,2},{4,5},{5,4},{6,7},{7,6},{8,9},{9,8},{10,11... | collective-permute-start | bytes 49160 | tf_op jit(solution)/shard_map/ppermute | solution.py:169
  3.0 14.1 %copy-start.2 = (f32[160,64]{0,1:T(8,128)S(1)}, f32[160,64]{0,1:T(8,128)}, u32[]{:S(2)}) copy-start(f32[160,64]{0,1:T(8,128)} %param.7) | copy-start | bytes 122884
  3.1 6.5 %collective-permute-start.2 = (f32[4,512]{1,0:T(4,128)S(1)}, f32[4,512]{1,0:T(4,128)S(1)}, u32[]{:S(2)}, u32[]{:S(2)}) collective-permute-start(f32[4,512]{1,0:T(4,128)S(1)} %get-tuple-element.26), channel_id=1, source_target_pairs={{0,17},{1,16},{2,19},{3,18},{4,21},{5,20},{6,23},{7,22},{8,25},{9,... | collective-permute-start | bytes 24584 | tf_op jit(solution)/shard_map/ppermute | solution.py:179
  6.8 4.0 %collective-permute-start.3 = (f32[4,512]{1,0:T(4,128)S(1)}, f32[4,512]{1,0:T(4,128)S(1)}, u32[]{:S(2)}, u32[]{:S(2)}) collective-permute-start(f32[4,512]{1,0:T(4,128)S(1)} %get-tuple-element.26), channel_id=1, source_target_pairs={{0,25},{1,24},{2,27},{3,26},{4,29},{5,28},{6,31},{7,30},{8,17},{9,... | collective-permute-start | bytes 24584 | tf_op jit(solution)/shard_map/ppermute | solution.py:179
  7.9 3.1 %collective-permute-start.4 = (f32[4,512]{1,0:T(4,128)S(1)}, f32[4,512]{1,0:T(4,128)S(1)}, u32[]{:S(2)}, u32[]{:S(2)}) collective-permute-start(f32[4,512]{1,0:T(4,128)S(1)} %get-tuple-element.26), channel_id=1, source_target_pairs={{0,9},{1,8},{2,11},{3,10},{4,13},{5,12},{6,15},{7,14},{8,1},{9,0},... | collective-permute-start | bytes 24584 | tf_op jit(solution)/shard_map/ppermute | solution.py:179
  9.1 6.4 %collective-permute-start.1 = (f32[80,512]{1,0:T(8,128)S(1)}, f32[80,512]{1,0:T(8,128)S(1)}, u32[]{:S(2)}, u32[]{:S(2)}) collective-permute-start(f32[80,512]{1,0:T(8,128)S(1)} %densities.1.refs_0_), channel_id=1, source_target_pairs={{0,1},{1,0},{2,3},{3,2},{4,5},{5,4},{6,7},{7,6},{8,9},{9,8},{10,11... | collective-permute-start | bytes 491528 | tf_op jit(solution)/shard_map/ppermute | solution.py:169
  11.0 4.3 %collective-permute-start.5 = (f32[16,512]{1,0:T(8,128)S(1)}, f32[16,512]{1,0:T(8,128)S(1)}, u32[]{:S(2)}, u32[]{:S(2)}) collective-permute-start(f32[16,512]{1,0:T(8,128)S(1)} %pad_maximum_fusion), channel_id=1, source_target_pairs={{0,7},{1,6},{2,5},{3,4},{4,3},{5,2},{6,1},{7,0},{8,15},{9,14},{10,... | collective-permute-start | bytes 98312 | tf_op jit(solution)/shard_map/ppermute | solution.py:179
  13.4 3.3 %collective-permute-start.7 = (f32[16,512]{1,0:T(8,128)S(1)}, f32[16,512]{1,0:T(8,128)S(1)}, u32[]{:S(2)}, u32[]{:S(2)}) collective-permute-start(f32[16,512]{1,0:T(8,128)S(1)} %pad_maximum_fusion), channel_id=1, source_target_pairs={{0,3},{1,2},{2,1},{3,0},{4,7},{5,6},{6,5},{7,4},{8,11},{9,10},{10,... | collective-permute-start | bytes 98312 | tf_op jit(solution)/shard_map/ppermute | solution.py:179
  13.8 3.3 %collective-permute-start.8 = (f32[16,512]{1,0:T(8,128)S(1)}, f32[16,512]{1,0:T(8,128)S(1)}, u32[]{:S(2)}, u32[]{:S(2)}) collective-permute-start(f32[16,512]{1,0:T(8,128)S(1)} %pad_maximum_fusion), channel_id=1, source_target_pairs={{0,5},{1,4},{2,7},{3,6},{4,1},{5,0},{6,3},{7,2},{8,13},{9,12},{10,... | collective-permute-start | bytes 98312 | tf_op jit(solution)/shard_map/ppermute | solution.py:179
  15.3 1.8 %collective-permute-start.6 = (f32[16,512]{1,0:T(8,128)S(1)}, f32[16,512]{1,0:T(8,128)S(1)}, u32[]{:S(2)}, u32[]{:S(2)}) collective-permute-start(f32[16,512]{1,0:T(8,128)S(1)} %pad_maximum_fusion), channel_id=1, source_target_pairs={{0,1},{1,0},{2,3},{3,2},{4,5},{5,4},{6,7},{7,6},{8,9},{9,8},{10,11... | collective-permute-start | bytes 98312 | tf_op jit(solution)/shard_map/ppermute | solution.py:169

commit v14 on v12

--- a/solution.py
+++ b/solution.py
@@ -12,7 +12,7 @@
 RADIX = 4
 ROUNDS = (
     ((2, 3, 1, 0), (3, 2, 0, 1), (1, 0, 3, 2)),
-    ((3, 2, 1, 0), (1, 0, 3, 2), (2, 3, 0, 1)),
+    ((3, 2, 1, 0), (2, 3, 0, 1), (1, 0, 3, 2)),
 )
 CHUNK = 256
 PIECES = 4

time: 18 us -> 18 us (level)
  no operation moved by 1% of the time
where the time goes in v14:
time: 18 us; the launch traced here: 17.9 us
  starting transfers between devices  9.56 us (53%)
  Pallas kernels  4.47 us (25%)
  waiting for transfers between devices  3.65 us (20%)
    ppermute x6, starting transfers between devices, between_chips(): return lax.ppermute(x, ('wide', 'narrow'), pairs_of)  8.45 us
    ppermute x6, waiting for transfers between devices, between_chips(): return lax.ppermute(x, ('wide', 'narrow'), pairs_of)  2.81 us
    pallas_call x1, Pallas kernels, shards(): pl.pallas_call(slab_kernel, in_specs=[hbm] * 4, out_specs=vmem, out_shape...  1.5 us
    ppermute x3, starting transfers between devices, exchange(): return lax.ppermute(x, 'narrow', [(i, i ^ bit) for i in range(n_narrow)])  1.11 us
    pallas_call x1, Pallas kernels, shards(): pl.pallas_call(dens_kernel, in_specs=[vmem] * 4, out_specs=vmem, out_shap...  0.96 us
    pallas_call x1, Pallas kernels, shards(): pl.pallas_call(val_kernel, in_specs=[vmem] * 3, out_specs=vmem, out_shape...  0.94 us
    pallas_call x1, Pallas kernels, shards(): pl.pallas_call(functools.partial(product_kernel, strides[-1], ROUNDS[(len...  0.86 us
    ppermute x3, waiting for transfers between devices, exchange(): return lax.ppermute(x, 'narrow', [(i, i ^ bit) for i in range(n_narrow)])  0.84 us
  transfers between devices with their start and end apart: 9, of which 6 were waited for; matrix products, arithmetic and copies ran while one was open for 0% of the time, Pallas kernels for 12%

profile of v14, /device:TPU:0, one launch (start us, length us, event | category | flops | bytes accessed | tf_op | source)
XLA Modules:
  0.0 17.9 jit_solution(2198621149780298973)
XLA Ops:
  0.0 0.0 copy-start.5
  0.0 0.0 copy-start
  0.0 0.0 copy-start.3
  0.0 1.5 %slab_rows.1 = f32[2,4,512]{2,1,0:T(4,128)S(1)} custom-call(f32[80,4096]{1,0:T(8,128)} %val_ref.3, f32[80,4096]{1,0:T(8,128)} %cond_ref.3, s32[1,512]{1,0:T(1,128)} %pv_ref.2, s32[1,512]{1,0:T(1,128)} %pc_ref.2), custom_call_target="tpu_custom_call" | custom-call | tf_op jit(solution)/shard_map/slab_rows/pallas_call | solution.py:152
  1.5 0.0 copy-start.1
  1.5 0.0 copy-start.4
  1.5 0.0 copy-start.6
  1.5 0.5 %collective-permute-start = (f32[2,4,512]{2,1,0:T(4,128)S(1)}, f32[2,4,512]{2,1,0:T(4,128)S(1)}, u32[]{:S(2)}, u32[]{:S(2)}) collective-permute-start(f32[2,4,512]{2,1,0:T(4,128)S(1)} %slab_rows.1), channel_id=1, source_target_pairs={{0,1},{1,0},{2,3},{3,2},{4,5},{5,4},{6,7},{7,6},{8,9},{9,8},{10,11... | collective-permute-start | bytes 49160 | tf_op jit(solution)/shard_map/ppermute | solution.py:169
  2.1 0.8 %collective-permute-done = f32[2,4,512]{2,1,0:T(4,128)S(1)} collective-permute-done((f32[2,4,512]{2,1,0:T(4,128)S(1)}, f32[2,4,512]{2,1,0:T(4,128)S(1)}, u32[]{:S(2)}, u32[]{:S(2)}) %collective-permute-start) | collective-permute-done | bytes 16416 | tf_op jit(solution)/shard_map/ppermute | solution.py:169
  2.9 3.7 %collective-permute-start.2 = (f32[4,512]{1,0:T(4,128)S(1)}, f32[4,512]{1,0:T(4,128)S(1)}, u32[]{:S(2)}, u32[]{:S(2)}) collective-permute-start(f32[4,512]{1,0:T(4,128)S(1)} %get-tuple-element.20), channel_id=1, source_target_pairs={{0,17},{1,16},{2,19},{3,18},{4,21},{5,20},{6,23},{7,22},{8,25},{9,... | collective-permute-start | bytes 24584 | tf_op jit(solution)/shard_map/ppermute | solution.py:179
  6.6 1.1 %collective-permute-start.3 = (f32[4,512]{1,0:T(4,128)S(1)}, f32[4,512]{1,0:T(4,128)S(1)}, u32[]{:S(2)}, u32[]{:S(2)}) collective-permute-start(f32[4,512]{1,0:T(4,128)S(1)} %get-tuple-element.20), channel_id=1, source_target_pairs={{0,25},{1,24},{2,27},{3,26},{4,29},{5,28},{6,31},{7,30},{8,17},{9,... | collective-permute-start | bytes 24584 | tf_op jit(solution)/shard_map/ppermute | solution.py:179
  7.7 0.5 %collective-permute-start.4 = (f32[4,512]{1,0:T(4,128)S(1)}, f32[4,512]{1,0:T(4,128)S(1)}, u32[]{:S(2)}, u32[]{:S(2)}) collective-permute-start(f32[4,512]{1,0:T(4,128)S(1)} %get-tuple-element.20), channel_id=1, source_target_pairs={{0,9},{1,8},{2,11},{3,10},{4,13},{5,12},{6,15},{7,14},{8,1},{9,0},... | collective-permute-start | bytes 24584 | tf_op jit(solution)/shard_map/ppermute | solution.py:179
  8.1 0.0 copy-done.5
  8.1 0.0 copy-done
  8.2 0.0 copy-done.3
  8.2 0.9 %val_columns.1.v_ref = f32[88,512]{1,0:T(8,128)S(1)} custom-call(f32[80,4096]{1,0:T(8,128)S(1)} %copy-done, f32[1,4096]{1,0:T(1,128)S(1)} %bitcast.9, s32[1,512]{1,0:T(1,128)S(1)} %copy-done.5), custom_call_target="tpu_custom_call" | custom-call | tf_op jit(solution)/shard_map/val_columns/pallas_call | solution.py:200
  9.1 0.0 copy-start.2
  9.1 0.0 copy-done.1
  9.1 0.0 copy-done.4
  9.1 0.0 copy-done.6
  9.1 1.0 %densities.1.refs_0_ = f32[80,512]{1,0:T(8,128)S(1)} custom-call(f32[80,4096]{1,0:T(8,128)S(1)} %copy-done.1, f32[1,4096]{1,0:T(1,128)S(1)} %bitcast.10, s32[1,512]{1,0:T(1,128)S(1)} %copy-done.6, f32[88,512]{1,0:T(8,128)S(1)} %val_columns.1.v_ref), custom_call_target="tpu_custom_call" | custom-call | tf_op jit(solution)/shard_map/densities/pallas_call | solution.py:208
  10.1 0.2 %collective-permute-start.1 = (f32[80,512]{1,0:T(8,128)S(1)}, f32[80,512]{1,0:T(8,128)S(1)}, u32[]{:S(2)}, u32[]{:S(2)}) collective-permute-start(f32[80,512]{1,0:T(8,128)S(1)} %densities.1.refs_0_), channel_id=1, source_target_pairs={{0,1},{1,0},{2,3},{3,2},{4,5},{5,4},{6,7},{7,6},{8,9},{9,8},{10,11... | collective-permute-start | bytes 491528 | tf_op jit(solution)/shard_map/ppermute | solution.py:169
  10.3 0.0 collective-permute-done.2
  10.3 0.2 %collective-permute-done.3 = f32[4,512]{1,0:T(4,128)S(1)} collective-permute-done((f32[4,512]{1,0:T(4,128)S(1)}, f32[4,512]{1,0:T(4,128)S(1)}, u32[]{:S(2)}, u32[]{:S(2)}) %collective-permute-start.3) | collective-permute-done | bytes 8224 | tf_op jit(solution)/shard_map/ppermute | solution.py:179
  10.6 0.2 collective-permute-done.4
  10.8 2.5 %collective-permute-start.5 = (f32[16,512]{1,0:T(8,128)S(1)}, f32[16,512]{1,0:T(8,128)S(1)}, u32[]{:S(2)}, u32[]{:S(2)}) collective-permute-start(f32[16,512]{1,0:T(8,128)S(1)} %pad_maximum_fusion), channel_id=1, source_target_pairs={{0,7},{1,6},{2,5},{3,4},{4,3},{5,2},{6,1},{7,0},{8,15},{9,14},{10,... | collective-permute-start | bytes 98312 | tf_op jit(solution)/shard_map/ppermute | solution.py:179
  13.3 0.4 %collective-permute-start.7 = (f32[16,512]{1,0:T(8,128)S(1)}, f32[16,512]{1,0:T(8,128)S(1)}, u32[]{:S(2)}, u32[]{:S(2)}) collective-permute-start(f32[16,512]{1,0:T(8,128)S(1)} %pad_maximum_fusion), channel_id=1, source_target_pairs={{0,5},{1,4},{2,7},{3,6},{4,1},{5,0},{6,3},{7,2},{8,13},{9,12},{10,... | collective-permute-start | bytes 98312 | tf_op jit(solution)/shard_map/ppermute | solution.py:179
  13.7 0.4 %collective-permute-start.8 = (f32[16,512]{1,0:T(8,128)S(1)}, f32[16,512]{1,0:T(8,128)S(1)}, u32[]{:S(2)}, u32[]{:S(2)}) collective-permute-start(f32[16,512]{1,0:T(8,128)S(1)} %pad_maximum_fusion), channel_id=1, source_target_pairs={{0,3},{1,2},{2,1},{3,0},{4,7},{5,6},{6,5},{7,4},{8,11},{9,10},{10,... | collective-permute-start | bytes 98312 | tf_op jit(solution)/shard_map/ppermute | solution.py:179
  14.0 1.1 %collective-permute-done.5.refs_1_ = f32[16,512]{1,0:T(8,128)S(1)} collective-permute-done((f32[16,512]{1,0:T(8,128)S(1)}, f32[16,512]{1,0:T(8,128)S(1)}, u32[]{:S(2)}, u32[]{:S(2)}) %collective-permute-start.5) | collective-permute-done | bytes 32800 | tf_op jit(solution)/shard_map/ppermute | solution.py:179
  15.1 0.3 %collective-permute-start.6 = (f32[16,512]{1,0:T(8,128)S(1)}, f32[16,512]{1,0:T(8,128)S(1)}, u32[]{:S(2)}, u32[]{:S(2)}) collective-permute-start(f32[16,512]{1,0:T(8,128)S(1)} %pad_maximum_fusion), channel_id=1, source_target_pairs={{0,1},{1,0},{2,3},{3,2},{4,5},{5,4},{6,7},{7,6},{8,9},{9,8},{10,11... | collective-permute-start | bytes 98312 | tf_op jit(solution)/shard_map/ppermute | solution.py:169
  15.5 0.0 collective-permute-done.1.refs_1_
  15.5 0.2 %columns.1 = (bf16[512,160]{1,0:T(8,128)(2,1)S(1)}, bf16[512,160]{1,0:T(8,128)(2,1)S(1)}) custom-call(f32[80,512]{1,0:T(8,128)S(1)} %densities.1.refs_0_, f32[80,512]{1,0:T(8,128)S(1)} %collective-permute-done.1.refs_1_), custom_call_target="tpu_custom_call" | custom-call | tf_op jit(solution)/shard_map/columns/pallas_call | solution.py:228
  15.7 0.9 %collective-permute-done.7.refs_2_ = f32[16,512]{1,0:T(8,128)S(1)} collective-permute-done((f32[16,512]{1,0:T(8,128)S(1)}, f32[16,512]{1,0:T(8,128)S(1)}, u32[]{:S(2)}, u32[]{:S(2)}) %collective-permute-start.7) | collective-permute-done | bytes 32800 | tf_op jit(solution)/shard_map/ppermute | solution.py:179
  16.6 0.4 %collective-permute-done.8.refs_3_ = f32[16,512]{1,0:T(8,128)S(1)} collective-permute-done((f32[16,512]{1,0:T(8,128)S(1)}, f32[16,512]{1,0:T(8,128)S(1)}, u32[]{:S(2)}, u32[]{:S(2)}) %collective-permute-start.8) | collective-permute-done | bytes 32800 | tf_op jit(solution)/shard_map/ppermute | solution.py:179
  17.0 0.0 collective-permute-done.6.refs_0_
  17.0 0.0 copy-done.2
  17.0 0.9 %product.1 = f32[64,160]{1,0:T(8,128)} custom-call(f32[64,160]{1,0:T(8,128)S(1)} %bitcast.8, bf16[512,160]{1,0:T(8,128)(2,1)S(1)} %get-tuple-element.18.hi_ref, bf16[512,160]{1,0:T(8,128)(2,1)S(1)} %get-tuple-element.19.lo_ref, f32[16,512]{1,0:T(8,128)S(1)} %collective-permute-done.6.refs_0_, f32[16,512]{1,0:T(8,128)S(1)} %collective-permute-done.5.refs_1_, ...), custom_call_target="tpu_custom_call" | custom-call | tf_op jit(solution)/shard_map/product/pallas_call | solution.py:236
  (3 shorter events, 0.0 us)
Async XLA Ops:
  0.0 8.1 %copy-start.5 = (s32[1,512]{1,0:T(1,128)S(1)}, s32[1,512]{1,0:T(1,128)}, u32[]{:S(2)}) copy-start(s32[1,512]{1,0:T(1,128)} %pv_ref.2) | copy-start | bytes 6148
  0.0 8.1 %copy-start = (f32[80,4096]{1,0:T(8,128)S(1)}, f32[80,4096]{1,0:T(8,128)}, u32[]{:S(2)}) copy-start(f32[80,4096]{1,0:T(8,128)} %val_ref.3) | copy-start | bytes 3932164
  0.0 8.1 %copy-start.3 = (f32[4096]{0:T(1024)S(1)}, f32[4096]{0:T(1024)}, u32[]{:S(2)}) copy-start(f32[4096]{0:T(1024)} %param.10) | copy-start | bytes 49156
  1.5 7.6 %copy-start.1 = (f32[80,4096]{1,0:T(8,128)S(1)}, f32[80,4096]{1,0:T(8,128)}, u32[]{:S(2)}) copy-start(f32[80,4096]{1,0:T(8,128)} %cond_ref.3) | copy-start | bytes 3932164
  1.5 7.6 %copy-start.4 = (f32[4096]{0:T(1024)S(1)}, f32[4096]{0:T(1024)}, u32[]{:S(2)}) copy-start(f32[4096]{0:T(1024)} %param.11) | copy-start | bytes 49156
  1.5 7.6 %copy-start.6 = (s32[1,512]{1,0:T(1,128)S(1)}, s32[1,512]{1,0:T(1,128)}, u32[]{:S(2)}) copy-start(s32[1,512]{1,0:T(1,128)} %pc_ref.2) | copy-start | bytes 6148
  1.5 1.4 %collective-permute-start = (f32[2,4,512]{2,1,0:T(4,128)S(1)}, f32[2,4,512]{2,1,0:T(4,128)S(1)}, u32[]{:S(2)}, u32[]{:S(2)}) collective-permute-start(f32[2,4,512]{2,1,0:T(4,128)S(1)} %slab_rows.1), channel_id=1, source_target_pairs={{0,1},{1,0},{2,3},{3,2},{4,5},{5,4},{6,7},{7,6},{8,9},{9,8},{10,11... | collective-permute-start | bytes 49160 | tf_op jit(solution)/shard_map/ppermute | solution.py:169
  2.9 7.4 %collective-permute-start.2 = (f32[4,512]{1,0:T(4,128)S(1)}, f32[4,512]{1,0:T(4,128)S(1)}, u32[]{:S(2)}, u32[]{:S(2)}) collective-permute-start(f32[4,512]{1,0:T(4,128)S(1)} %get-tuple-element.20), channel_id=1, source_target_pairs={{0,17},{1,16},{2,19},{3,18},{4,21},{5,20},{6,23},{7,22},{8,25},{9,... | collective-permute-start | bytes 24584 | tf_op jit(solution)/shard_map/ppermute | solution.py:179
  6.6 4.0 %collective-permute-start.3 = (f32[4,512]{1,0:T(4,128)S(1)}, f32[4,512]{1,0:T(4,128)S(1)}, u32[]{:S(2)}, u32[]{:S(2)}) collective-permute-start(f32[4,512]{1,0:T(4,128)S(1)} %get-tuple-element.20), channel_id=1, source_target_pairs={{0,25},{1,24},{2,27},{3,26},{4,29},{5,28},{6,31},{7,30},{8,17},{9,... | collective-permute-start | bytes 24584 | tf_op jit(solution)/shard_map/ppermute | solution.py:179
  7.7 3.1 %collective-permute-start.4 = (f32[4,512]{1,0:T(4,128)S(1)}, f32[4,512]{1,0:T(4,128)S(1)}, u32[]{:S(2)}, u32[]{:S(2)}) collective-permute-start(f32[4,512]{1,0:T(4,128)S(1)} %get-tuple-element.20), channel_id=1, source_target_pairs={{0,9},{1,8},{2,11},{3,10},{4,13},{5,12},{6,15},{7,14},{8,1},{9,0},... | collective-permute-start | bytes 24584 | tf_op jit(solution)/shard_map/ppermute | solution.py:179
  9.1 7.9 %copy-start.2 = (f32[160,64]{0,1:T(8,128)S(1)}, f32[160,64]{0,1:T(8,128)}, u32[]{:S(2)}) copy-start(f32[160,64]{0,1:T(8,128)} %param.7) | copy-start | bytes 122884
  10.1 5.3 %collective-permute-start.1 = (f32[80,512]{1,0:T(8,128)S(1)}, f32[80,512]{1,0:T(8,128)S(1)}, u32[]{:S(2)}, u32[]{:S(2)}) collective-permute-start(f32[80,512]{1,0:T(8,128)S(1)} %densities.1.refs_0_), channel_id=1, source_target_pairs={{0,1},{1,0},{2,3},{3,2},{4,5},{5,4},{6,7},{7,6},{8,9},{9,8},{10,11... | collective-permute-start | bytes 491528 | tf_op jit(solution)/shard_map/ppermute | solution.py:169
  10.8 4.3 %collective-permute-start.5 = (f32[16,512]{1,0:T(8,128)S(1)}, f32[16,512]{1,0:T(8,128)S(1)}, u32[]{:S(2)}, u32[]{:S(2)}) collective-permute-start(f32[16,512]{1,0:T(8,128)S(1)} %pad_maximum_fusion), channel_id=1, source_target_pairs={{0,7},{1,6},{2,5},{3,4},{4,3},{5,2},{6,1},{7,0},{8,15},{9,14},{10,... | collective-permute-start | bytes 98312 | tf_op jit(solution)/shard_map/ppermute | solution.py:179
  13.3 3.3 %collective-permute-start.7 = (f32[16,512]{1,0:T(8,128)S(1)}, f32[16,512]{1,0:T(8,128)S(1)}, u32[]{:S(2)}, u32[]{:S(2)}) collective-permute-start(f32[16,512]{1,0:T(8,128)S(1)} %pad_maximum_fusion), channel_id=1, source_target_pairs={{0,5},{1,4},{2,7},{3,6},{4,1},{5,0},{6,3},{7,2},{8,13},{9,12},{10,... | collective-permute-start | bytes 98312 | tf_op jit(solution)/shard_map/ppermute | solution.py:179
  13.7 3.3 %collective-permute-start.8 = (f32[16,512]{1,0:T(8,128)S(1)}, f32[16,512]{1,0:T(8,128)S(1)}, u32[]{:S(2)}, u32[]{:S(2)}) collective-permute-start(f32[16,512]{1,0:T(8,128)S(1)} %pad_maximum_fusion), channel_id=1, source_target_pairs={{0,3},{1,2},{2,1},{3,0},{4,7},{5,6},{6,5},{7,4},{8,11},{9,10},{10,... | collective-permute-start | bytes 98312 | tf_op jit(solution)/shard_map/ppermute | solution.py:179
  15.1 1.9 %collective-permute-start.6 = (f32[16,512]{1,0:T(8,128)S(1)}, f32[16,512]{1,0:T(8,128)S(1)}, u32[]{:S(2)}, u32[]{:S(2)}) collective-permute-start(f32[16,512]{1,0:T(8,128)S(1)} %pad_maximum_fusion), channel_id=1, source_target_pairs={{0,1},{1,0},{2,3},{3,2},{4,5},{5,4},{6,7},{7,6},{8,9},{9,8},{10,11... | collective-permute-start | bytes 98312 | tf_op jit(solution)/shard_map/ppermute | solution.py:169
